TPU v7x, 128 devices: a whole 4x4x4 slice. The times are simulated.
128 devices in a mesh: rep: 16 (over y_lo, z, core), shard: 8 (over x, y_hi).
Axes of the slice: x: 4, y: 4 (y_hi: 2, y_lo: 2; y = y_hi * 2 + y_lo), z: 4, core: 2. Of those that a mesh axis runs over, the one named last changes fastest.
Arguments:
- grads: bfloat16 [16, 8, 256, 22016], P('rep', 'shard'), may hold values from -6 to 6
- momentum: float32 [16, 256, 22016], P('rep', None, 'shard'), may hold values from -12 to 12
Outputs:
- new_momentum: float32 [16, 256, 22016], P('rep', None, 'shard')
- update: float32 [256, 22016], P(None, 'shard')
All inputs are finite; a program needn't handle non-finite values.
Results may differ from a plain program's by a relative error of at most 0.0003.
Values sent between devices are 32-bit elements; how exact they have to be, the bound alone decides.
No kernel may reach another device: no remote copies, remote signals or barrier semaphores. Data moves between devices by JAX's collectives and lax.ppermute only.
A program may use at most 192 MiB of HBM per device.

v0:
```python
import jax
import jax.numpy as jnp
from jax import lax
from jax.sharding import PartitionSpec as P

BETA = 0.9
SHARP = 4.0


def cosine_table():
    freqs = jnp.arange(16, dtype=jnp.float32)[:, None]
    points = jnp.arange(64, dtype=jnp.float32)[None, :]
    norming = jnp.where(
        freqs == 0.0, jnp.sqrt(jnp.float32(1.0 / 64.0)), jnp.sqrt(jnp.float32(2.0 / 64.0))
    )
    return norming * jnp.cos(jnp.pi * (2.0 * points + 1.0) * freqs / 128.0)


def transform(values, basis):
    row_blocks = values.shape[0] // 64
    blocks = values.reshape(row_blocks, 64, -1)
    rowwise = jnp.einsum("kn,anf->akf", basis, blocks, precision=lax.Precision.HIGHEST)
    rowwise = rowwise.reshape(row_blocks, 16, -1, 64)
    return jnp.einsum("akbm,lm->akbl", rowwise, basis, precision=lax.Precision.HIGHEST)


def restore(coeffs, basis):
    row_blocks = coeffs.shape[0]
    rowwise = jnp.einsum("akbl,lm->akbm", coeffs, basis, precision=lax.Precision.HIGHEST)
    rowwise = rowwise.reshape(row_blocks, 16, -1)
    output = jnp.einsum("kn,akf->anf", basis, rowwise, precision=lax.Precision.HIGHEST)
    return output.reshape(row_blocks * 64, -1)


def local(grads, momentum):
    basis = cosine_table()
    replicas = lax.axis_size("rep")
    partials = grads[0, 0]
    previous = momentum[0]
    summed = lax.psum_scatter(
        partials.astype(jnp.float32), "shard", scatter_dimension=1, tiled=True
    )
    merged = BETA * previous + summed
    coeffs = transform(merged, basis)
    component = restore(coeffs, basis)
    summed_coeffs = lax.psum(coeffs, "rep")
    decoded = restore(summed_coeffs / replicas, basis)
    new_rows = merged - component
    update = jnp.tanh(SHARP * decoded)
    return (new_rows[None], update)


def solution(mesh):
    placed = (P("rep", "shard", None, None), P("rep", None, "shard"))
    return jax.shard_map(
        local,
        mesh=mesh,
        in_specs=placed,
        out_specs=(P("rep", None, "shard"), P(None, "shard")),
        check_vma=False,
    )
```

profile of v0, /device:TPU:1, one launch (start us, length us, event | category | flops | bytes accessed | tf_op | source)
XLA Modules:
  0.0 446.3 jit_solution(2332903805449008770)
XLA Ops:
  7.2 0.0 reduce-scatter.4.cloned.1.call-start
  7.2 12.7 %bitcast_convert_fusion = f32[256,22016]{1,0:T(8,128)} fusion(bf16[1,1,256,22016]{3,2,1,0:T(8,128)(2,1)} %param.2), kind=kLoop, calls=%fused_computation | loop fusion | flops 5636096 | bytes 33816576 | tf_op jit(solution)/shard_map/convert_element_type | solution.py:41
  19.9 22.8 %copy.15 = f32[256,22016]{0,1:T(8,128)} copy(f32[256,22016]{1,0:T(8,128)} %bitcast_convert_fusion) | data formatting | bytes 45088768
  42.7 0.0 copy-start.1
  42.7 0.0 reduce-scatter.4.cloned.1.call-update
  42.7 1.8 copy-done.1
  44.5 2.3 copy.11
  46.8 238.6 %reduce-scatter.4.cloned.1.call-done = f32[2752,256]{1,0:T(8,128)} async-done(((f32[22016,256]{1,0:T(8,128)}), f32[2752,256]{1,0:T(8,128)}) %reduce-scatter.4.cloned.1.call-update) | async-done | bytes 2818064
  285.4 3.4 copy.16
  288.8 3.0 bitcast_add_fusion
  291.8 2.5 convolution_bitcast_fusion
  294.3 2.7 reshape.44
  297.0 6.0 %fusion.7 = f32[4,16,43,16]{2,3,1,0:T(8,128)S(1)} fusion(f32[4,16,43,64]{3,2,1,0:T(8,128)} %reshape.44, f32[64]{0:T(128)S(1)} %add_multiply_fusion, f32[16]{0:T(128)S(1)} %compare_select_fusion), kind=kOutput, calls=%fused_computation.12 | convolution fusion | flops 33819648 | bytes 880960 | tf_op jit(solution)/shard_map/akbm,lm->akbl/dot_general | solution.py:24
  303.0 0.0 copy-start
  303.0 3.8 fusion.5
  306.8 0.0 all-reduce.2.cloned.1.call-start
  306.8 2.7 reshape.45
  309.4 0.0 copy-done
  309.4 0.0 all-reduce.2.cloned.1.call-update
  309.5 3.6 fusion.10
  313.1 1.9 bitcast_subtract_fusion
  315.0 3.4 copy.12
  318.3 110.2 %all-reduce.2.cloned.1.call-done = f32[4,16,43,16]{2,3,1,0:T(8,128)} async-done(((f32[4,16,43,16]{2,3,1,0:T(8,128)}), f32[4,16,43,16]{2,3,1,0:T(8,128)}) %all-reduce.2.cloned.1.call-update) | async-done | bytes 176144 | tf_op jit(solution)/shard_map/psum | solution.py:46
  428.6 3.7 fusion.1
  432.3 1.3 reshape.47
  433.5 3.7 fusion
  437.2 2.2 copy.13
  (2 shorter events, 0.0 us)
Async XLA Ops:
  7.2 278.2 %reduce-scatter.4.cloned.1.call-start = ((), (), s32[]{:S(2)}) async-start(), calls=%async_computation.2 | async-start | bytes 25362432
  42.7 1.8 copy-start.1
  303.0 6.5 %copy-start = (f32[4,16,43,16]{2,3,1,0:T(8,128)}, f32[4,16,43,16]{2,3,1,0:T(8,128)S(1)}, u32[]{:S(2)}) copy-start(f32[4,16,43,16]{2,3,1,0:T(8,128)S(1)} %fusion.7) | copy-start | bytes 528388
  306.8 121.8 %all-reduce.2.cloned.1.call-start = ((), (), s32[]{:S(2)}) async-start(), calls=%async_computation.1 | async-start | bytes 1048576 | tf_op jit(solution)/shard_map/psum | solution.py:46
Sparse Core Ops, SparseCore 0:
  42.8 242.4 reduce-scatter.3
  310.1 118.4 all-reduce.1
where the time goes:
time: 447 us; the launch traced here: 446 us
  waiting for transfers between devices  349 us (78%)
  local copies, waits for them, and re-layouts  42.3 us (9%)
  matrix products  23.3 us (5%)
  other arithmetic  17.7 us (4%)
  between operations  14.1 us (3%)
    unnamed x3, waiting for transfers between devices  239 us
    psum x1, waiting for transfers between devices, local(): summed_coeffs = lax.psum(coeffs, 'rep')  110 us
    unnamed x9, local copies, waits for them, and re-layouts  35.7 us
    convert_element_type x1, other arithmetic, local(): partials.astype(jnp.float32)  12.7 us
  transfers between devices with their start and end apart: 2, of which 2 were waited for; matrix products, arithmetic and copies ran while one was open for 2% of the time, Pallas kernels for 0%

commit v1 on v0

v1 whole, which is shorter than its diff:
```python
import functools

import jax
import jax.numpy as jnp
import numpy as np
from jax import lax
from jax.experimental import pallas as pl
from jax.experimental.pallas import tpu as pltpu
from jax.sharding import PartitionSpec as P

BETA = 0.9
SHARP = 4.0
ROWS = 256
LANES = 128
SUPER = 43
MID = 21
OWN = 22
NB = 9
NBP = 5
STEP_ROWS = 64

F32 = jnp.float32


def x_ring(step):
    return [(s, ((s // 2 + step) % 4) * 2 + s % 2) for s in range(8)]


Y_FLIP = [(s, s ^ 1) for s in range(8)]
CORE_FLIP = [(r, r ^ 1) for r in range(16)]
YLO_FLIP = [(r, r ^ 8) for r in range(16)]


def z_ring(step):
    return [(r, (r // 8) * 8 + ((r // 2 % 4 + step) % 4) * 2 + r % 2) for r in range(16)]


def up(value):
    return lax.ppermute(value, "shard", x_ring(1))


def down(value):
    return lax.ppermute(value, "shard", x_ring(-1))


def across(value):
    return lax.ppermute(value, "shard", Y_FLIP)


def grads_spec(slot, tiles):
    def where(row, starts):
        return row * STEP_ROWS, pl.multiple_of(starts[slot] * LANES, LANES)

    return pl.BlockSpec((pl.Element(STEP_ROWS), pl.Element(tiles * LANES)), where)


def rows_spec(tiles):
    return pl.BlockSpec((STEP_ROWS, tiles * LANES), lambda row, starts: (row, 0))


def rows_call(kernel, starts, ins, in_specs, out_tiles, bytes_moved):
    outs = [jax.ShapeDtypeStruct((ROWS, t * LANES), F32) for t in out_tiles]
    return pl.pallas_call(
        kernel,
        grid_spec=pltpu.PrefetchScalarGridSpec(
            num_scalar_prefetch=1,
            grid=(ROWS // STEP_ROWS,),
            in_specs=in_specs,
            out_specs=[rows_spec(t) for t in out_tiles],
        ),
        out_shape=outs,
        cost_estimate=pl.CostEstimate(
            flops=bytes_moved // 4, bytes_accessed=bytes_moved, transcendentals=0
        ),
    )(jnp.stack(starts).astype(jnp.int32), *ins)


def widen_kernel(counts, starts, *refs):
    n = sum(len(c) for c in counts)
    ins, outs = refs[:n], refs[n:]
    at = 0
    for out, group in zip(outs, counts):
        col = 0
        for tiles in group:
            out[:, col : col + tiles * LANES] = ins[at][...].astype(F32)
            col += tiles * LANES
            at += 1


def widen(grads, groups):
    counts = [[t for _, t in g] for g in groups]
    flat = [piece for g in groups for piece in g]
    total = sum(t for _, t in flat)
    return rows_call(
        functools.partial(widen_kernel, counts),
        [s for s, _ in flat],
        [grads] * len(flat),
        [grads_spec(k, t) for k, (_, t) in enumerate(flat)],
        [sum(c) for c in counts],
        total * LANES * ROWS * 6,
    )


def add_kernel(tiles, offsets, starts, g, *refs):
    out = refs[-1]
    total = g[...].astype(F32)
    for ref, off in zip(refs[:-1], offsets):
        total = total + ref[:, off * LANES : (off + tiles) * LANES]
    out[...] = total


def add(grads, start, tiles, parts):
    return rows_call(
        functools.partial(add_kernel, tiles, [o for _, o in parts]),
        [start],
        [grads] + [a for a, _ in parts],
        [grads_spec(0, tiles)] + [rows_spec(a.shape[1] // LANES) for a, _ in parts],
        [tiles],
        tiles * LANES * ROWS * (6 + 4 * len(parts)),
    )[0]


def cross_first_kernel(starts, g, plus, minus, out):
    @pl.when(starts[1] == 0)
    def _():
        out[...] = minus[...] + g[...].astype(F32)

    @pl.when(starts[1] == 1)
    def _():
        w = 6 * LANES
        out[:, :w] = plus[...] + g[:, :w].astype(F32)
        out[:, w:] = minus[:, :LANES] + g[:, w:].astype(F32)


def cross_second_kernel(starts, g, plus, minus, out):
    @pl.when(starts[1] == 0)
    def _():
        out[...] = minus[...] + g[...].astype(F32)

    @pl.when(starts[1] == 1)
    def _():
        out[...] = plus[...] + g[...].astype(F32)


def cross_call(kernel, grads, start, yh, tiles, plus, minus):
    return rows_call(
        kernel,
        [start, yh],
        [grads, plus, minus],
        [
            grads_spec(0, tiles),
            rows_spec(plus.shape[1] // LANES),
            rows_spec(minus.shape[1] // LANES),
        ],
        [tiles],
        tiles * LANES * ROWS * 14,
    )[0]


def half_roll(tile):
    return pltpu.roll(tile, 64, axis=1)


def base_kernel(starts, g, momentum, out):
    low = lax.broadcasted_iota(jnp.int32, (STEP_ROWS, LANES), 1) < 64

    @pl.when(starts[1] == 0)
    def _():
        for t in range(OWN):
            at = slice(t * LANES, (t + 1) * LANES)
            if t < OWN - 1:
                m = momentum[:, at]
            else:
                m = jnp.concatenate(
                    [momentum[:, t * LANES : t * LANES + 64], jnp.zeros((STEP_ROWS, 64), F32)], 1
                )
            total = BETA * m + g[:, at].astype(F32)
            if t == OWN - 1:
                total = jnp.where(low, total, 0.0)
            out[:, at] = total

    @pl.when(starts[1] == 1)
    def _():
        before = jnp.zeros((STEP_ROWS, LANES), F32)
        for t in range(OWN):
            at = slice(t * LANES, (t + 1) * LANES)
            if t < OWN - 1:
                m = half_roll(momentum[:, at])
            else:
                m = jnp.concatenate(
                    [jnp.zeros((STEP_ROWS, 64), F32), momentum[:, t * LANES : t * LANES + 64]], 1
                )
            total = BETA * jnp.where(low, before, m) + g[:, at].astype(F32)
            if t == 0:
                total = jnp.where(low, 0.0, total)
            out[:, at] = total
            before = m


def base_call(grads, momentum, start, yh):
    return rows_call(
        base_kernel,
        [start, yh],
        [grads, momentum],
        [
            grads_spec(0, OWN),
            pl.BlockSpec((STEP_ROWS, momentum.shape[1]), lambda row, starts: (row, 0)),
        ],
        [OWN],
        OWN * LANES * ROWS * 10,
    )[0]


def whole(*shape):
    return pl.BlockSpec(shape, lambda *_: (0,) * len(shape))


def dot(a, b):
    return lax.dot_general(
        a, b, (((1,), (0,)), ((), ())), precision=lax.Precision.HIGHEST, preferred_element_type=F32
    )


def mix_kernel(starts, base, pa, ma, ca, pb, mb, cb, bp, bm, rowmat, colmat, merged, coeffs):
    def put(tile, tiles, *sources):
        at = slice(tile * LANES, (tile + tiles) * LANES)
        total = base[:, at]
        for ref, off in sources:
            total = total + ref[:, off * LANES : (off + tiles) * LANES]
        merged[:, at] = total

    @pl.when(starts[0] == 0)
    def _():
        put(0, NBP, (bp, 0))
        put(NBP, NB - NBP, (bm, 0))
        put(9, 6, (pb, 0), (cb, 0))
        put(15, 6, (pa, 0), (ca, 0))
        put(21, 1, (ma, 0), (ca, 6))
        t = merged[:, 21 * LANES :]
        low = lax.broadcasted_iota(jnp.int32, t.shape, 1) < 64
        merged[:, 21 * LANES :] = jnp.where(low, t, 0.0)

    @pl.when(starts[0] == 1)
    def _():
        put(0, 7, (ma, 0), (ca, 0))
        put(7, 6, (mb, 0), (cb, 0))
        put(13, NBP, (bp, 0))
        put(13 + NBP, NB - NBP, (bm, 0))
        t = merged[:, :LANES]
        low = lax.broadcasted_iota(jnp.int32, t.shape, 1) < 64
        merged[:, :LANES] = jnp.where(low, 0.0, t)

    for t in range(0, OWN, 2):
        rowwise = dot(rowmat[...], merged[:, t * LANES : (t + 2) * LANES])
        coeffs[:, t * 32 : (t + 2) * 32] = dot(rowwise, colmat[...])


def expand(coeffs, rowmat_t, colmat_t):
    return dot(rowmat_t, dot(coeffs, colmat_t))


def pair_out(index, yh_is_one, tiles_of, out):
    width = out.shape[1]
    if not yh_is_one:
        for t in range(OWN):
            v = tiles_of(t)
            if t < OWN - 1:
                out[:, t * LANES : (t + 1) * LANES] = v
            else:
                out[:, t * LANES : width] = v[:, : width - t * LANES]
        return
    low = lax.broadcasted_iota(jnp.int32, (ROWS, LANES), 1) < 64
    ahead = half_roll(tiles_of(0))
    for t in range(OWN):
        if t < OWN - 1:
            following = half_roll(tiles_of(t + 1))
            out[:, t * LANES : (t + 1) * LANES] = jnp.where(low, ahead, following)
            ahead = following
        else:
            out[:, t * LANES : width] = ahead[:, : width - t * LANES]


def finish_kernel(starts, merged, coeffs, rowmat_t, colmat_t, out, full):
    for t in range(0, OWN, 2):
        at = slice(t * LANES, (t + 2) * LANES)
        full[:, at] = merged[:, at] - expand(
            coeffs[:, t * 32 : (t + 2) * 32], rowmat_t[...], colmat_t[...]
        )
    for yh in range(2):

        @pl.when(starts[0] == yh)
        def _():
            pair_out(None, yh == 1, lambda t: full[:, t * LANES : (t + 1) * LANES], out)


def update_kernel(starts, total, rowmat_t, colmat_t, out, full):
    for t in range(0, OWN, 2):
        at = slice(t * LANES, (t + 2) * LANES)
        decoded = expand(total[:, t * 32 : (t + 2) * 32], rowmat_t[...], colmat_t[...])
        full[:, at] = jnp.tanh(SHARP * decoded)
    for yh in range(2):

        @pl.when(starts[0] == yh)
        def _():
            pair_out(None, yh == 1, lambda t: full[:, t * LANES : (t + 1) * LANES], out)


def whole_call(kernel, starts, ins, outs, scratch, flops, moved):
    return pl.pallas_call(
        kernel,
        grid_spec=pltpu.PrefetchScalarGridSpec(
            num_scalar_prefetch=1,
            grid=(1,),
            in_specs=[whole(*a.shape) for a in ins],
            out_specs=[whole(*o) for o in outs],
            scratch_shapes=scratch,
        ),
        out_shape=[jax.ShapeDtypeStruct(o, F32) for o in outs],
        compiler_params=pltpu.CompilerParams(vmem_limit_bytes=48 << 20),
        cost_estimate=pl.CostEstimate(flops=flops, bytes_accessed=moved, transcendentals=0),
    )(jnp.stack(starts).astype(jnp.int32), *ins)


def cosine_table():
    freqs = np.arange(16, dtype=np.float64)[:, None]
    points = np.arange(64, dtype=np.float64)[None, :]
    norming = np.where(freqs == 0.0, np.sqrt(1.0 / 64.0), np.sqrt(2.0 / 64.0))
    return norming * np.cos(np.pi * (2.0 * points + 1.0) * freqs / 128.0)


def after(value, *others):
    return lax.optimization_barrier((value, *others))[0]


def local(grads, momentum):
    grads = grads[0, 0]
    momentum = momentum[0]
    shard = lax.axis_index("shard")
    x, yh = shard // 2, shard % 2
    other = 1 - yh

    def tile(dx, t):
        return ((x + dx) % 4) * SUPER + t

    b_own, b_other = 34 * yh, 34 * other

    def b_piece(k):
        return [(tile(-1 - k, b_other), NBP), (tile(1 + k, b_other + NBP), NB - NBP)]

    y0, pa, ma = widen(
        grads, [b_piece(0), [(tile(-1, 15), 6)], [(tile(1, 21), 7)]]
    )
    y0, pa, ma = across(y0), up(pa), down(ma)
    pb, mb, y1 = widen(grads, [[(tile(-1, 9), 6)], [(tile(1, 28), 6)], b_piece(1)])
    pb, mb, y1 = up(pb), down(mb), across(y1)
    y2, y3 = widen(grads, [b_piece(2), b_piece(3)])
    y2, y3 = across(y2), across(y3)
    ys = [y0, y1, y2, y3]

    base = base_call(grads, momentum, tile(0, MID * yh), yh)

    bp = bm = None
    for k in range(2):
        pa = up(add(grads, tile(-2 - k, 15), 6, [(pa, 0)]))
        ma = down(add(grads, tile(2 + k, 21), 7, [(ma, 0)]))
        pb = up(add(grads, tile(-2 - k, 9), 6, [(pb, 0)]))
        mb = down(add(grads, tile(2 + k, 28), 6, [(mb, 0)]))
    for k in range(3):
        bp = up(add(grads, tile(-1 - k, b_own), NBP, [(ys[k], 0)] + ([(bp, 0)] if k else [])))
        bm = down(
            add(grads, tile(1 + k, b_own + NBP), NB - NBP, [(ys[k], NBP)] + ([(bm, 0)] if k else []))
        )
    ca = across(cross_call(cross_first_kernel, grads, tile(0, 15 + 6 * other), yh, 7, pa, ma))
    cb = across(cross_call(cross_second_kernel, grads, tile(0, 9 + 19 * other), yh, 6, pb, mb))
    bp = add_plain(bp, ys[3], 0, NBP)
    bm = add_plain(bm, ys[3], NBP, NB - NBP)

    table = cosine_table()
    rowmat = jnp.asarray(np.kron(np.eye(4), table), F32)
    colmat = jnp.asarray(np.kron(np.eye(4), table.T), F32)
    rowmat_t = jnp.asarray(np.kron(np.eye(4), table.T), F32)
    colmat_t = jnp.asarray(np.kron(np.eye(4), table), F32)

    width = OWN * LANES
    merged, coeffs = whole_call(
        mix_kernel,
        [yh],
        [base, pa, ma, ca, pb, mb, cb, bp, bm, rowmat, colmat],
        [(ROWS, width), (64, width // 4)],
        [],
        2 * 64 * 256 * width * 6,
        ROWS * width * 16,
    )
    total = coeffs + lax.ppermute(coeffs, "rep", CORE_FLIP)
    total = (
        total
        + lax.ppermute(total, "rep", z_ring(1))
        + lax.ppermute(total, "rep", z_ring(-1))
        + lax.ppermute(total, "rep", z_ring(2))
    )
    total = total + lax.ppermute(total, "rep", YLO_FLIP)
    own = momentum.shape
    new_rows = whole_call(
        finish_kernel,
        [yh],
        [merged, coeffs, rowmat_t, colmat_t],
        [own],
        [pltpu.VMEM((ROWS, width), F32)],
        2 * 64 * 256 * width * 6,
        ROWS * width * 8,
    )[0]
    update = whole_call(
        update_kernel,
        [yh],
        [total / 16.0, rowmat_t, colmat_t],
        [own],
        [pltpu.VMEM((ROWS, width), F32)],
        2 * 64 * 256 * width * 6,
        ROWS * width * 4,
    )[0]
    return new_rows[None], update


def add_plain(value, piece, offset, tiles):
    return value + piece[:, offset * LANES : (offset + tiles) * LANES]


def solution(mesh):
    placed = (P("rep", "shard", None, None), P("rep", None, "shard"))
    return jax.shard_map(
        local,
        mesh=mesh,
        in_specs=placed,
        out_specs=(P("rep", None, "shard"), P(None, "shard")),
        check_vma=False,
    )
```

time: 447 us -> 242 us (0.54)
  waiting for transfers between devices: 349 us -> 76.4 us
  Pallas kernels: 0 us -> 91.4 us
  starting transfers between devices: 0.04 us -> 51.1 us
  local copies, waits for them, and re-layouts: 42.3 us -> 13.1 us
  matrix products: 23.3 us -> 0 us
  between operations: 14.1 us -> 0.92 us
  other arithmetic: 17.7 us -> 6.86 us
    unnamed x3 -> x0, waiting for transfers between devices: 239 us -> none
    psum x1 -> x0, waiting for transfers between devices: 110 us -> none  [local(): summed_coeffs = lax.psum(coeffs, 'rep')]
    pallas_call x0 -> x23, Pallas kernels: none -> 91.4 us  [the longest x20 74.9 us: rows_call(): pl.pallas_call(kernel, grid_spec=pltpu.PrefetchScalarGridSpec(num_scalar_...]
    ppermute x0 -> x29, waiting for transfers between devices: none -> 76.4 us  [the longest x6 33 us: across(): return lax.ppermute(value, 'shard', Y_FLIP)]
    ppermute x0 -> x29, starting transfers between devices: none -> 51.1 us  [the longest x9 15.1 us: down(): return lax.ppermute(value, 'shard', x_ring(-1))]
    dot_general x6 -> x0, matrix products: 23.3 us -> none  [the longest x2 7.52 us: restore(): jnp.einsum('akbl,lm->akbm', coeffs, basis, precision=lax.Precision.HIGHEST)]
    unnamed x9 -> x39, local copies, waits for them, and re-layouts: 35.7 us -> 13.1 us
    convert_element_type x1 -> x0, other arithmetic: 12.7 us -> none  [local(): partials.astype(jnp.float32)]
  transfers between devices with their start and end apart: 2 -> 29, of which waited for: 2 -> 12; matrix products, arithmetic and copies ran while one was open for 2% -> 5% of each run, Pallas kernels for 0% -> 31%
where the time goes in v1:
time: 242 us; the launch traced here: 240 us
  Pallas kernels  91.4 us (38%)
  waiting for transfers between devices  76.4 us (32%)
  starting transfers between devices  51.1 us (21%)
  local copies, waits for them, and re-layouts  13.1 us (5%)
  other arithmetic  6.86 us (3%)
    pallas_call x20, Pallas kernels, rows_call(): pl.pallas_call(kernel, grid_spec=pltpu.PrefetchScalarGridSpec(num_scalar_...  74.9 us
    ppermute x6, waiting for transfers between devices, across(): return lax.ppermute(value, 'shard', Y_FLIP)  33 us
    ppermute x9, waiting for transfers between devices, up(): return lax.ppermute(value, 'shard', x_ring(1))  28.9 us
    pallas_call x3, Pallas kernels, whole_call(): pl.pallas_call(kernel, grid_spec=pltpu.PrefetchScalarGridSpec(num_scalar_...  16.5 us
    ppermute x9, starting transfers between devices, down(): return lax.ppermute(value, 'shard', x_ring(-1))  15.1 us
    ppermute x6, starting transfers between devices, across(): return lax.ppermute(value, 'shard', Y_FLIP)  14.2 us
    unnamed x39, local copies, waits for them, and re-layouts  13.1 us
    ppermute x9, starting transfers between devices, up(): return lax.ppermute(value, 'shard', x_ring(1))  8.58 us
  transfers between devices with their start and end apart: 29, of which 12 were waited for; matrix products, arithmetic and copies ran while one was open for 5% of the time, Pallas kernels for 31%

profile of v1, /device:TPU:1, one launch (start us, length us, event | category | flops | bytes accessed | tf_op | source)
XLA Modules:
  0.0 239.8 jit_solution(12875236299118857366)
XLA Ops:
  1.4 4.4 %shard_map.84 = (f32[256,768]{1,0:T(8,128)}, f32[256,768]{1,0:T(8,128)}, f32[256,1152]{1,0:T(8,128)}) custom-call(s32[4]{0:T(128)} %pad_add_fusion.3.starts, bf16[256,22016]{1,0:T(8,128)(2,1)} %bitcast.34, bf16[256,22016]{1,0:T(8,128)(2,1)} %bitcast.35, bf16[256,22016]{1,0:T(8,128)(2,1)} %bitcast.36, bf16[256,22016]{1,0:T(8,128)(2,1)} %bitcast.37), custom_call_target="tpu_custom_call" | custom-call | flops 1032192 | bytes 4128768 | tf_op jit(solution)/shard_map/pallas_call | solution.py:63
  8.5 4.6 %shard_map.78 = (f32[256,1152]{1,0:T(8,128)}, f32[256,768]{1,0:T(8,128)}, f32[256,896]{1,0:T(8,128)}) custom-call(s32[4]{0:T(128)} %pad_add_fusion.1.starts, bf16[256,22016]{1,0:T(8,128)(2,1)} %bitcast.38, bf16[256,22016]{1,0:T(8,128)(2,1)} %bitcast.39, bf16[256,22016]{1,0:T(8,128)(2,1)} %bitcast.40, bf16[256,22016]{1,0:T(8,128)(2,1)} %bitcast.41), custom_call_target="tpu_custom_call" | custom-call | flops 1081344 | bytes 4325376 | tf_op jit(solution)/shard_map/pallas_call | solution.py:63
  19.4 4.4 %shard_map.90 = (f32[256,1152]{1,0:T(8,128)}, f32[256,1152]{1,0:T(8,128)}) custom-call(s32[4]{0:T(128)} %pad_add_fusion.5.starts, bf16[256,22016]{1,0:T(8,128)(2,1)} %bitcast.42, bf16[256,22016]{1,0:T(8,128)(2,1)} %bitcast.43, bf16[256,22016]{1,0:T(8,128)(2,1)} %bitcast.44, bf16[256,22016]{1,0:T(8,128)(2,1)} %bitcast.45), custom_call_target="tpu_custom_call" | custom-call | flops 884736 | bytes 3538944 | tf_op jit(solution)/shard_map/pallas_call | solution.py:63
  30.3 12.8 %collective-permute-done.refs_0_ = f32[256,768]{1,0:T(8,128)} collective-permute-done((f32[256,768]{1,0:T(8,128)}, f32[256,768]{1,0:T(8,128)}, u32[]{:S(2)}, u32[]{:S(2)}) %collective-permute-start) | collective-permute-done | bytes 786464 | tf_op jit(solution)/shard_map/ppermute | solution.py:39
  44.7 3.4 %shard_map.79 = f32[256,768]{1,0:T(8,128)} custom-call(s32[1]{0:T(128)} %bitcast.5.starts, bf16[256,22016]{1,0:T(8,128)(2,1)} %bitcast.46, f32[256,768]{1,0:T(8,128)} %collective-permute-done.refs_0_), custom_call_target="tpu_custom_call" | custom-call | flops 491520 | bytes 1966080 | tf_op jit(solution)/shard_map/pallas_call | solution.py:63
  48.1 3.5 %shard_map.81 = f32[256,896]{1,0:T(8,128)} custom-call(s32[1]{0:T(128)} %bitcast.11.starts, bf16[256,22016]{1,0:T(8,128)(2,1)} %bitcast.47, f32[256,896]{1,0:T(8,128)} %collective-permute-done.3.refs_0_), custom_call_target="tpu_custom_call" | custom-call | flops 573440 | bytes 2293760 | tf_op jit(solution)/shard_map/pallas_call | solution.py:63
  54.4 3.4 %shard_map.94 = f32[256,512]{1,0:T(8,128)} custom-call(s32[1]{0:T(128)} %bitcast.31.starts, bf16[256,22016]{1,0:T(8,128)(2,1)} %bitcast.48, f32[256,1152]{1,0:T(8,128)} %copy-done.11), custom_call_target="tpu_custom_call" | custom-call | flops 327680 | bytes 1310720 | tf_op jit(solution)/shard_map/pallas_call | solution.py:63
  63.7 3.4 %shard_map.91 = f32[256,640]{1,0:T(8,128)} custom-call(s32[1]{0:T(128)} %bitcast.28.starts, bf16[256,22016]{1,0:T(8,128)(2,1)} %bitcast.49, f32[256,1152]{1,0:T(8,128)} %copy-done.11), custom_call_target="tpu_custom_call" | custom-call | flops 409600 | bytes 1638400 | tf_op jit(solution)/shard_map/pallas_call | solution.py:63
  68.5 3.4 %shard_map.85 = f32[256,768]{1,0:T(8,128)} custom-call(s32[1]{0:T(128)} %bitcast.14.starts, bf16[256,22016]{1,0:T(8,128)(2,1)} %bitcast.50, f32[256,768]{1,0:T(8,128)} %copy-done.15), custom_call_target="tpu_custom_call" | custom-call | flops 491520 | bytes 1966080 | tf_op jit(solution)/shard_map/pallas_call | solution.py:63
  71.9 21.0 %collective-permute-done.15.refs_0_ = f32[256,1152]{1,0:T(8,128)S(1)} collective-permute-done((f32[256,1152]{1,0:T(8,128)}, f32[256,1152]{1,0:T(8,128)S(1)}, u32[]{:S(2)}, u32[]{:S(2)}) %collective-permute-start.15) | collective-permute-done | bytes 1179680 | tf_op jit(solution)/shard_map/ppermute | solution.py:47
  93.7 3.4 %shard_map.87 = f32[256,768]{1,0:T(8,128)} custom-call(s32[1]{0:T(128)} %bitcast.20.starts, bf16[256,22016]{1,0:T(8,128)(2,1)} %bitcast.51, f32[256,768]{1,0:T(8,128)} %collective-permute-done.10.refs_0_), custom_call_target="tpu_custom_call" | custom-call | flops 491520 | bytes 1966080 | tf_op jit(solution)/shard_map/pallas_call | solution.py:63
  103.1 3.4 %shard_map.95 = f32[256,512]{1,0:T(8,128)} custom-call(s32[1]{0:T(128)} %bitcast.30.starts, bf16[256,22016]{1,0:T(8,128)(2,1)} %bitcast.53, f32[256,1152]{1,0:T(8,128)} %copy-done.13, f32[256,512]{1,0:T(8,128)} %copy-done.17), custom_call_target="tpu_custom_call" | custom-call | flops 458752 | bytes 1835008 | tf_op jit(solution)/shard_map/pallas_call | solution.py:63
  108.5 3.4 %shard_map.82 = f32[256,896]{1,0:T(8,128)} custom-call(s32[1]{0:T(128)} %bitcast.10.starts, bf16[256,22016]{1,0:T(8,128)(2,1)} %bitcast.54, f32[256,896]{1,0:T(8,128)} %collective-permute-done.4.refs_0_), custom_call_target="tpu_custom_call" | custom-call | flops 573440 | bytes 2293760 | tf_op jit(solution)/shard_map/pallas_call | solution.py:63
  112.0 3.5 %shard_map.92 = f32[256,640]{1,0:T(8,128)} custom-call(s32[1]{0:T(128)} %bitcast.27.starts, bf16[256,22016]{1,0:T(8,128)(2,1)} %bitcast.55, f32[256,1152]{1,0:T(8,128)} %copy-done.13, f32[256,640]{1,0:T(8,128)} %collective-permute-done.17.refs_1_), custom_call_target="tpu_custom_call" | custom-call | flops 573440 | bytes 2293760 | tf_op jit(solution)/shard_map/pallas_call | solution.py:63
  119.8 3.4 %shard_map.86 = f32[256,768]{1,0:T(8,128)} custom-call(s32[1]{0:T(128)} %bitcast.13.starts, bf16[256,22016]{1,0:T(8,128)(2,1)} %bitcast.56, f32[256,768]{1,0:T(8,128)} %collective-permute-done.8.refs_0_), custom_call_target="tpu_custom_call" | custom-call | flops 491520 | bytes 1966080 | tf_op jit(solution)/shard_map/pallas_call | solution.py:63
  126.0 3.4 %shard_map.88 = f32[256,768]{1,0:T(8,128)} custom-call(s32[1]{0:T(128)} %bitcast.19.starts, bf16[256,22016]{1,0:T(8,128)(2,1)} %bitcast.57, f32[256,768]{1,0:T(8,128)} %copy-done.16), custom_call_target="tpu_custom_call" | custom-call | flops 491520 | bytes 1966080 | tf_op jit(solution)/shard_map/pallas_call | solution.py:63
  131.8 3.5 %shard_map.96 = f32[256,512]{1,0:T(8,128)} custom-call(s32[1]{0:T(128)} %bitcast.29.starts, bf16[256,22016]{1,0:T(8,128)(2,1)} %bitcast.58, f32[256,1152]{1,0:T(8,128)} %copy-done.12, f32[256,512]{1,0:T(8,128)} %collective-permute-done.22.refs_1_), custom_call_target="tpu_custom_call" | custom-call | flops 458752 | bytes 1835008 | tf_op jit(solution)/shard_map/pallas_call | solution.py:63
  135.2 6.9 %collective-permute-done.18.refs_1_ = f32[256,640]{1,0:T(8,128)} collective-permute-done((f32[256,640]{1,0:T(8,128)}, f32[256,640]{1,0:T(8,128)}, u32[]{:S(2)}, u32[]{:S(2)}) %collective-permute-start.18) | collective-permute-done | bytes 655392 | tf_op jit(solution)/shard_map/ppermute | solution.py:39
  142.4 3.5 %shard_map.93 = f32[256,640]{1,0:T(8,128)} custom-call(s32[1]{0:T(128)} %bitcast.22.starts, bf16[256,22016]{1,0:T(8,128)(2,1)} %bitcast.59, f32[256,1152]{1,0:T(8,128)} %copy-done.12, f32[256,640]{1,0:T(8,128)} %collective-permute-done.18.refs_1_), custom_call_target="tpu_custom_call" | custom-call | flops 573440 | bytes 2293760 | tf_op jit(solution)/shard_map/pallas_call | solution.py:63
  147.8 4.3 %shard_map.83 = f32[256,896]{1,0:T(8,128)} custom-call(s32[2]{0:T(128)} %pad_add_fusion.2.starts, bf16[256,22016]{1,0:T(8,128)(2,1)} %bitcast.60, f32[256,768]{1,0:T(8,128)} %copy-done.2, f32[256,896]{1,0:T(8,128)} %copy-done), custom_call_target="tpu_custom_call" | custom-call | flops 802816 | bytes 3211264 | tf_op jit(solution)/shard_map/pallas_call | solution.py:63
  152.1 6.8 %collective-permute-done.9.plus.pb = f32[256,768]{1,0:T(8,128)S(1)} collective-permute-done((f32[256,768]{1,0:T(8,128)}, f32[256,768]{1,0:T(8,128)S(1)}, u32[]{:S(2)}, u32[]{:S(2)}) %collective-permute-start.9) | collective-permute-done | bytes 786464 | tf_op jit(solution)/shard_map/ppermute | solution.py:39
  163.3 4.3 %shard_map.89 = f32[256,768]{1,0:T(8,128)} custom-call(s32[2]{0:T(128)} %pad_add_fusion.4.starts, bf16[256,22016]{1,0:T(8,128)(2,1)} %bitcast.61, f32[256,768]{1,0:T(8,128)} %copy-done.4, f32[256,768]{1,0:T(8,128)} %copy-done.6), custom_call_target="tpu_custom_call" | custom-call | flops 688128 | bytes 2752512 | tf_op jit(solution)/shard_map/pallas_call | solution.py:63
  169.8 3.4 %copy.8 = f32[1,256,2752]{2,1,0:T(8,128)} copy(f32[1,256,2752]{1,2,0:T(8,128)} %param.7) | data formatting | bytes 5636096 | tf_op args[1]
  173.8 5.1 %shard_map.77.base = f32[256,2816]{1,0:T(8,128)} custom-call(s32[2]{0:T(128)} %pad_add_fusion.starts, bf16[256,22016]{1,0:T(8,128)(2,1)} %bitcast.62, f32[256,2752]{1,0:T(8,128)} %bitcast.63), custom_call_target="tpu_custom_call" | custom-call | flops 1802240 | bytes 7208960 | tf_op jit(solution)/shard_map/pallas_call | solution.py:63
  181.9 11.6 %collective-permute-done.13.cb = f32[256,768]{1,0:T(8,128)S(1)} collective-permute-done((f32[256,768]{1,0:T(8,128)}, f32[256,768]{1,0:T(8,128)S(1)}, u32[]{:S(2)}, u32[]{:S(2)}) %collective-permute-start.13) | collective-permute-done | bytes 786464 | tf_op jit(solution)/shard_map/ppermute | solution.py:47
  194.5 8.4 %shard_map.97 = (f32[256,2816]{1,0:T(8,128)}, f32[64,704]{1,0:T(8,128)S(1)}) custom-call(s32[1]{0:T(128)} %bitcast.starts, f32[256,2816]{1,0:T(8,128)} %shard_map.77.base, f32[256,768]{1,0:T(8,128)S(1)} %copy-done.3, f32[256,896]{1,0:T(8,128)S(1)} %copy-done.1, f32[256,896]{1,0:T(8,128)} %copy-done.14, f32[256,768]{1,0:T(8,128)S(1)} %copy-done.5, ...), custom_call_target="tpu_custom_call" | custom-call | flops 553648128 | bytes 11534336 | tf_op jit(solution)/shard_map/pallas_call | solution.py:309
  202.9 6.7 %collective-permute-start.24 = (f32[64,704]{1,0:T(8,128)S(1)}, f32[64,704]{1,0:T(8,128)S(1)}, u32[]{:S(2)}, u32[]{:S(2)}) collective-permute-start(f32[64,704]{1,0:T(8,128)S(1)} %get-tuple-element.21.coeffs), channel_id=1, source_target_pairs={{0,8},{8,0},{16,24},{24,16},{32,40},{40,32},{48,56},{56,48},{64,72... | collective-permute-start | bytes 540680 | tf_op jit(solution)/shard_map/ppermute | solution.py:394
  210.7 3.7 %collective-permute-start.27 = (f32[64,704]{1,0:T(8,128)S(1)}, f32[64,704]{1,0:T(8,128)S(1)}, u32[]{:S(2)}, u32[]{:S(2)}) collective-permute-start(f32[64,704]{1,0:T(8,128)S(1)} %add.272), channel_id=1, source_target_pairs={{0,32},{8,40},{16,48},{24,56},{32,0},{40,8},{48,16},{56,24},{64,96... | collective-permute-start | bytes 540680 | tf_op jit(solution)/shard_map/ppermute | solution.py:399
  215.9 3.5 %collective-permute-done.27 = f32[64,704]{1,0:T(8,128)S(1)} collective-permute-done((f32[64,704]{1,0:T(8,128)S(1)}, f32[64,704]{1,0:T(8,128)S(1)}, u32[]{:S(2)}, u32[]{:S(2)}) %collective-permute-start.27) | collective-permute-done | bytes 180256 | tf_op jit(solution)/shard_map/ppermute | solution.py:399
  219.4 4.7 %collective-permute-done.26 = f32[64,704]{1,0:T(8,128)S(1)} collective-permute-done((f32[64,704]{1,0:T(8,128)S(1)}, f32[64,704]{1,0:T(8,128)S(1)}, u32[]{:S(2)}, u32[]{:S(2)}) %collective-permute-start.26) | collective-permute-done | bytes 180256 | tf_op jit(solution)/shard_map/ppermute | solution.py:398
  227.3 4.1 %shard_map.98 = f32[256,2752]{1,0:T(8,128)S(1)} custom-call(s32[1]{0:T(128)} %bitcast.starts, f32[256,2816]{1,0:T(8,128)S(1)} %copy-done.8, f32[64,704]{1,0:T(8,128)S(1)} %get-tuple-element.21.coeffs, f32[256,64]{1,0:T(8,128)S(1)} %copy-done.9, f32[64,256]{1,0:T(8,128)S(1)} %copy-done.10), custom_call_target="tpu_custom_call" | custom-call | flops 553648128 | bytes 5767168 | tf_op jit(solution)/shard_map/pallas_call | solution.py:309
  233.6 3.9 %shard_map.99 = f32[256,2752]{1,0:T(8,128)S(1)} custom-call(s32[1]{0:T(128)} %bitcast.starts, f32[64,704]{1,0:T(8,128)S(1)} %add_multiply_fusion.total, f32[256,64]{1,0:T(8,128)S(1)} %copy-done.9, f32[64,256]{1,0:T(8,128)S(1)} %copy-done.10), custom_call_target="tpu_custom_call" | custom-call | flops 553648128 | bytes 2883584 | tf_op jit(solution)/shard_map/pallas_call | solution.py:309
  (99 shorter events, 69.8 us)
Async XLA Ops:
  5.8 20.3 %collective-permute-start.7 = (f32[256,768]{1,0:T(8,128)}, f32[256,768]{1,0:T(8,128)S(1)}, u32[]{:S(2)}, u32[]{:S(2)}) collective-permute-start(f32[256,768]{1,0:T(8,128)} %get-tuple-element.14), channel_id=1, source_target_pairs={{0,2},{1,3},{2,4},{3,5},{4,6},{5,7},{6,0},{7,1},{8,10},{9,11},{10,... | collective-permute-start | bytes 2359304 | tf_op jit(solution)/shard_map/ppermute | solution.py:39
  13.1 30.0 %collective-permute-start = (f32[256,768]{1,0:T(8,128)}, f32[256,768]{1,0:T(8,128)}, u32[]{:S(2)}, u32[]{:S(2)}) collective-permute-start(f32[256,768]{1,0:T(8,128)} %get-tuple-element.12), channel_id=1, source_target_pairs={{0,2},{1,3},{2,4},{3,5},{4,6},{5,7},{6,0},{7,1},{8,10},{9,11},{10,... | collective-permute-start | bytes 2359304 | tf_op jit(solution)/shard_map/ppermute | solution.py:39
  14.3 37.3 %collective-permute-start.16 = (f32[256,1152]{1,0:T(8,128)}, f32[256,1152]{1,0:T(8,128)S(1)}, u32[]{:S(2)}, u32[]{:S(2)}) collective-permute-start(f32[256,1152]{1,0:T(8,128)} %get-tuple-element.18), channel_id=1, source_target_pairs={{0,1},{1,0},{2,3},{3,2},{4,5},{5,4},{6,7},{7,6},{8,9},{9,8},{10,11... | collective-permute-start | bytes 3538952 | tf_op jit(solution)/shard_map/ppermute | solution.py:47
  17.2 30.9 %collective-permute-start.3 = (f32[256,896]{1,0:T(8,128)}, f32[256,896]{1,0:T(8,128)}, u32[]{:S(2)}, u32[]{:S(2)}) collective-permute-start(f32[256,896]{1,0:T(8,128)} %get-tuple-element.13), channel_id=1, source_target_pairs={{0,6},{1,7},{2,0},{3,1},{4,2},{5,3},{6,4},{7,5},{8,14},{9,15},{10,... | collective-permute-start | bytes 2752520 | tf_op jit(solution)/shard_map/ppermute | solution.py:43
  23.7 43.8 %collective-permute-start.14 = (f32[256,1152]{1,0:T(8,128)}, f32[256,1152]{1,0:T(8,128)S(1)}, u32[]{:S(2)}, u32[]{:S(2)}) collective-permute-start(f32[256,1152]{1,0:T(8,128)} %get-tuple-element.16), channel_id=1, source_target_pairs={{0,1},{1,0},{2,3},{3,2},{4,5},{5,4},{6,7},{7,6},{8,9},{9,8},{10,11... | collective-permute-start | bytes 3538952 | tf_op jit(solution)/shard_map/ppermute | solution.py:47
  27.1 65.8 %collective-permute-start.15 = (f32[256,1152]{1,0:T(8,128)}, f32[256,1152]{1,0:T(8,128)S(1)}, u32[]{:S(2)}, u32[]{:S(2)}) collective-permute-start(f32[256,1152]{1,0:T(8,128)} %get-tuple-element.17), channel_id=1, source_target_pairs={{0,1},{1,0},{2,3},{3,2},{4,5},{5,4},{6,7},{7,6},{8,9},{9,8},{10,11... | collective-permute-start | bytes 3538952 | tf_op jit(solution)/shard_map/ppermute | solution.py:47
  43.1 17.7 %collective-permute-start.10 = (f32[256,768]{1,0:T(8,128)}, f32[256,768]{1,0:T(8,128)}, u32[]{:S(2)}, u32[]{:S(2)}) collective-permute-start(f32[256,768]{1,0:T(8,128)} %get-tuple-element.15), channel_id=1, source_target_pairs={{0,6},{1,7},{2,0},{3,1},{4,2},{5,3},{6,4},{7,5},{8,14},{9,15},{10,... | collective-permute-start | bytes 2359304 | tf_op jit(solution)/shard_map/ppermute | solution.py:43
  48.1 49.0 %collective-permute-start.1 = (f32[256,768]{1,0:T(8,128)}, f32[256,768]{1,0:T(8,128)}, u32[]{:S(2)}, u32[]{:S(2)}) collective-permute-start(f32[256,768]{1,0:T(8,128)} %shard_map.79), channel_id=1, source_target_pairs={{0,2},{1,3},{2,4},{3,5},{4,6},{5,7},{6,0},{7,1},{8,10},{9,11},{10,... | collective-permute-start | bytes 2359304 | tf_op jit(solution)/shard_map/ppermute | solution.py:39
  51.6 54.9 %collective-permute-start.4 = (f32[256,896]{1,0:T(8,128)}, f32[256,896]{1,0:T(8,128)}, u32[]{:S(2)}, u32[]{:S(2)}) collective-permute-start(f32[256,896]{1,0:T(8,128)} %shard_map.81), channel_id=1, source_target_pairs={{0,6},{1,7},{2,0},{3,1},{4,2},{5,3},{6,4},{7,5},{8,14},{9,15},{10,... | collective-permute-start | bytes 2752520 | tf_op jit(solution)/shard_map/ppermute | solution.py:43
  60.8 41.5 %collective-permute-start.21 = (f32[256,512]{1,0:T(8,128)}, f32[256,512]{1,0:T(8,128)S(1)}, u32[]{:S(2)}, u32[]{:S(2)}) collective-permute-start(f32[256,512]{1,0:T(8,128)} %shard_map.94), channel_id=1, source_target_pairs={{0,6},{1,7},{2,0},{3,1},{4,2},{5,3},{6,4},{7,5},{8,14},{9,15},{10,... | collective-permute-start | bytes 1572872 | tf_op jit(solution)/shard_map/ppermute | solution.py:43
  67.5 44.4 %collective-permute-start.17 = (f32[256,640]{1,0:T(8,128)}, f32[256,640]{1,0:T(8,128)}, u32[]{:S(2)}, u32[]{:S(2)}) collective-permute-start(f32[256,640]{1,0:T(8,128)} %shard_map.91), channel_id=1, source_target_pairs={{0,2},{1,3},{2,4},{3,5},{4,6},{5,7},{6,0},{7,1},{8,10},{9,11},{10,... | collective-permute-start | bytes 1966088 | tf_op jit(solution)/shard_map/ppermute | solution.py:39
  92.8 22.6 %collective-permute-start.8 = (f32[256,768]{1,0:T(8,128)}, f32[256,768]{1,0:T(8,128)}, u32[]{:S(2)}, u32[]{:S(2)}) collective-permute-start(f32[256,768]{1,0:T(8,128)} %shard_map.85), channel_id=1, source_target_pairs={{0,2},{1,3},{2,4},{3,5},{4,6},{5,7},{6,0},{7,1},{8,10},{9,11},{10,... | collective-permute-start | bytes 2359304 | tf_op jit(solution)/shard_map/ppermute | solution.py:39
  97.1 21.3 %collective-permute-start.11 = (f32[256,768]{1,0:T(8,128)}, f32[256,768]{1,0:T(8,128)S(1)}, u32[]{:S(2)}, u32[]{:S(2)}) collective-permute-start(f32[256,768]{1,0:T(8,128)} %shard_map.87), channel_id=1, source_target_pairs={{0,6},{1,7},{2,0},{3,1},{4,2},{5,3},{6,4},{7,5},{8,14},{9,15},{10,... | collective-permute-start | bytes 2359304 | tf_op jit(solution)/shard_map/ppermute | solution.py:43
  102.3 27.1 %collective-permute-start.2 = (f32[256,768]{1,0:T(8,128)}, f32[256,768]{1,0:T(8,128)S(1)}, u32[]{:S(2)}, u32[]{:S(2)}) collective-permute-start(f32[256,768]{1,0:T(8,128)} %shard_map.80), channel_id=1, source_target_pairs={{0,2},{1,3},{2,4},{3,5},{4,6},{5,7},{6,0},{7,1},{8,10},{9,11},{10,... | collective-permute-start | bytes 2359304 | tf_op jit(solution)/shard_map/ppermute | solution.py:39
  106.5 18.8 %collective-permute-start.22 = (f32[256,512]{1,0:T(8,128)}, f32[256,512]{1,0:T(8,128)}, u32[]{:S(2)}, u32[]{:S(2)}) collective-permute-start(f32[256,512]{1,0:T(8,128)} %shard_map.95), channel_id=1, source_target_pairs={{0,6},{1,7},{2,0},{3,1},{4,2},{5,3},{6,4},{7,5},{8,14},{9,15},{10,... | collective-permute-start | bytes 1572872 | tf_op jit(solution)/shard_map/ppermute | solution.py:43
  111.9 33.9 %collective-permute-start.5 = (f32[256,896]{1,0:T(8,128)}, f32[256,896]{1,0:T(8,128)S(1)}, u32[]{:S(2)}, u32[]{:S(2)}) collective-permute-start(f32[256,896]{1,0:T(8,128)} %shard_map.82), channel_id=1, source_target_pairs={{0,6},{1,7},{2,0},{3,1},{4,2},{5,3},{6,4},{7,5},{8,14},{9,15},{10,... | collective-permute-start | bytes 2752520 | tf_op jit(solution)/shard_map/ppermute | solution.py:43
  115.5 63.5 %collective-permute-start.20 = (f32[256,1152]{1,0:T(8,128)}, f32[256,1152]{1,0:T(8,128)}, u32[]{:S(2)}, u32[]{:S(2)}) collective-permute-start(f32[256,1152]{1,0:T(8,128)} %get-tuple-element.19), channel_id=1, source_target_pairs={{0,1},{1,0},{2,3},{3,2},{4,5},{5,4},{6,7},{7,6},{8,9},{9,8},{10,11... | collective-permute-start | bytes 3538952 | tf_op jit(solution)/shard_map/ppermute | solution.py:47
  118.4 23.7 %collective-permute-start.18 = (f32[256,640]{1,0:T(8,128)}, f32[256,640]{1,0:T(8,128)}, u32[]{:S(2)}, u32[]{:S(2)}) collective-permute-start(f32[256,640]{1,0:T(8,128)} %shard_map.92), channel_id=1, source_target_pairs={{0,2},{1,3},{2,4},{3,5},{4,6},{5,7},{6,0},{7,1},{8,10},{9,11},{10,... | collective-permute-start | bytes 1966088 | tf_op jit(solution)/shard_map/ppermute | solution.py:39
  125.3 33.5 %collective-permute-start.9 = (f32[256,768]{1,0:T(8,128)}, f32[256,768]{1,0:T(8,128)S(1)}, u32[]{:S(2)}, u32[]{:S(2)}) collective-permute-start(f32[256,768]{1,0:T(8,128)} %shard_map.86), channel_id=1, source_target_pairs={{0,2},{1,3},{2,4},{3,5},{4,6},{5,7},{6,0},{7,1},{8,10},{9,11},{10,... | collective-permute-start | bytes 2359304 | tf_op jit(solution)/shard_map/ppermute | solution.py:39
  129.4 33.0 %collective-permute-start.12 = (f32[256,768]{1,0:T(8,128)}, f32[256,768]{1,0:T(8,128)S(1)}, u32[]{:S(2)}, u32[]{:S(2)}) collective-permute-start(f32[256,768]{1,0:T(8,128)} %shard_map.88), channel_id=1, source_target_pairs={{0,6},{1,7},{2,0},{3,1},{4,2},{5,3},{6,4},{7,5},{8,14},{9,15},{10,... | collective-permute-start | bytes 2359304 | tf_op jit(solution)/shard_map/ppermute | solution.py:43
  142.1 36.8 %collective-permute-start.23 = (f32[256,512]{1,0:T(8,128)}, f32[256,512]{1,0:T(8,128)}, u32[]{:S(2)}, u32[]{:S(2)}) collective-permute-start(f32[256,512]{1,0:T(8,128)} %shard_map.96), channel_id=1, source_target_pairs={{0,6},{1,7},{2,0},{3,1},{4,2},{5,3},{6,4},{7,5},{8,14},{9,15},{10,... | collective-permute-start | bytes 1572872 | tf_op jit(solution)/shard_map/ppermute | solution.py:43
  145.9 34.5 %collective-permute-start.19 = (f32[256,640]{1,0:T(8,128)}, f32[256,640]{1,0:T(8,128)}, u32[]{:S(2)}, u32[]{:S(2)}) collective-permute-start(f32[256,640]{1,0:T(8,128)} %shard_map.93), channel_id=1, source_target_pairs={{0,2},{1,3},{2,4},{3,5},{4,6},{5,7},{6,0},{7,1},{8,10},{9,11},{10,... | collective-permute-start | bytes 1966088 | tf_op jit(solution)/shard_map/ppermute | solution.py:39
  158.9 34.6 %collective-permute-start.6 = (f32[256,896]{1,0:T(8,128)}, f32[256,896]{1,0:T(8,128)S(1)}, u32[]{:S(2)}, u32[]{:S(2)}) collective-permute-start(f32[256,896]{1,0:T(8,128)} %shard_map.83), channel_id=1, source_target_pairs={{0,1},{1,0},{2,3},{3,2},{4,5},{5,4},{6,7},{7,6},{8,9},{9,8},{10,11... | collective-permute-start | bytes 2752520 | tf_op jit(solution)/shard_map/ppermute | solution.py:47
  167.6 25.9 %collective-permute-start.13 = (f32[256,768]{1,0:T(8,128)}, f32[256,768]{1,0:T(8,128)S(1)}, u32[]{:S(2)}, u32[]{:S(2)}) collective-permute-start(f32[256,768]{1,0:T(8,128)} %shard_map.89), channel_id=1, source_target_pairs={{0,1},{1,0},{2,3},{3,2},{4,5},{5,4},{6,7},{7,6},{8,9},{9,8},{10,11... | collective-permute-start | bytes 2359304 | tf_op jit(solution)/shard_map/ppermute | solution.py:47
  178.9 15.5 %copy-start.5 = (f32[256,768]{1,0:T(8,128)S(1)}, f32[256,768]{1,0:T(8,128)}, u32[]{:S(2)}) copy-start(f32[256,768]{1,0:T(8,128)} %copy-done.4) | copy-start | bytes 2359300
  178.9 15.5 %copy-start.7 = (f32[256,768]{1,0:T(8,128)S(1)}, f32[256,768]{1,0:T(8,128)}, u32[]{:S(2)}) copy-start(f32[256,768]{1,0:T(8,128)} %copy-done.6) | copy-start | bytes 2359300
  180.4 14.1 %copy-start.1 = (f32[256,896]{1,0:T(8,128)S(1)}, f32[256,896]{1,0:T(8,128)}, u32[]{:S(2)}) copy-start(f32[256,896]{1,0:T(8,128)} %copy-done) | copy-start | bytes 2752516
  202.9 7.8 %collective-permute-start.24 = (f32[64,704]{1,0:T(8,128)S(1)}, f32[64,704]{1,0:T(8,128)S(1)}, u32[]{:S(2)}, u32[]{:S(2)}) collective-permute-start(f32[64,704]{1,0:T(8,128)S(1)} %get-tuple-element.21.coeffs), channel_id=1, source_target_pairs={{0,8},{8,0},{16,24},{24,16},{32,40},{40,32},{48,56},{56,48},{64,72... | collective-permute-start | bytes 540680 | tf_op jit(solution)/shard_map/ppermute | solution.py:394
  210.7 8.7 %collective-permute-start.27 = (f32[64,704]{1,0:T(8,128)S(1)}, f32[64,704]{1,0:T(8,128)S(1)}, u32[]{:S(2)}, u32[]{:S(2)}) collective-permute-start(f32[64,704]{1,0:T(8,128)S(1)} %add.272), channel_id=1, source_target_pairs={{0,32},{8,40},{16,48},{24,56},{32,0},{40,8},{48,16},{56,24},{64,96... | collective-permute-start | bytes 540680 | tf_op jit(solution)/shard_map/ppermute | solution.py:399
  214.4 9.6 %collective-permute-start.26 = (f32[64,704]{1,0:T(8,128)S(1)}, f32[64,704]{1,0:T(8,128)S(1)}, u32[]{:S(2)}, u32[]{:S(2)}) collective-permute-start(f32[64,704]{1,0:T(8,128)S(1)} %add.272), channel_id=1, source_target_pairs={{0,48},{8,56},{16,0},{24,8},{32,16},{40,24},{48,32},{56,40},{64,11... | collective-permute-start | bytes 540680 | tf_op jit(solution)/shard_map/ppermute | solution.py:398
  214.8 9.2 %collective-permute-start.25 = (f32[64,704]{1,0:T(8,128)S(1)}, f32[64,704]{1,0:T(8,128)S(1)}, u32[]{:S(2)}, u32[]{:S(2)}) collective-permute-start(f32[64,704]{1,0:T(8,128)S(1)} %add.272), channel_id=1, source_target_pairs={{0,16},{8,24},{16,32},{24,40},{32,48},{40,56},{48,0},{56,8},{64,80... | collective-permute-start | bytes 540680 | tf_op jit(solution)/shard_map/ppermute | solution.py:397
  224.1 9.5 %collective-permute-start.28 = (f32[64,704]{1,0:T(8,128)S(1)}, f32[64,704]{1,0:T(8,128)S(1)}, u32[]{:S(2)}, u32[]{:S(2)}) collective-permute-start(f32[64,704]{1,0:T(8,128)S(1)} %add_add_fusion), channel_id=1, source_target_pairs={{0,64},{8,72},{16,80},{24,88},{32,96},{40,104},{48,112},{56,120},{... | collective-permute-start | bytes 540680 | tf_op jit(solution)/shard_map/ppermute | solution.py:401
  (15 other events, 75.0 us)

commit v2 on v0

v2 whole, which is shorter than its diff:
```python
import functools

import jax
import jax.numpy as jnp
import numpy as np
from jax import lax
from jax.experimental import pallas as pl
from jax.experimental.pallas import tpu as pltpu
from jax.sharding import PartitionSpec as P

BETA = 0.9
SHARP = 4.0
ROWS = 256
LANES = 128
SUPER = 43
NB = 8
NBP = 4
MIDDLE = 21 - NB
NA = 7
OWN_COLS = 2752
PACKED = 352

VMEM_BYTES = 60 << 20

F32 = jnp.float32
BF16 = jnp.bfloat16


def x_shift(step):
    return [(s, ((s // 2 + step) % 4) * 2 + s % 2) for s in range(8)]


def z_shift(step):
    return [(r, (r // 8) * 8 + ((r // 2 % 4 + step) % 4) * 2 + r % 2) for r in range(16)]


def y_shift(step):
    pairs = []
    for r in range(16):
        for s in range(8):
            y = ((s % 2) * 2 + r // 8 + step) % 4
            pairs.append((r * 8 + s, ((y % 2) * 8 + r % 8) * 8 + (s // 2) * 2 + y // 2))
    return pairs


Y_FLIP = [(s, s ^ 1) for s in range(8)]
CORE_FLIP = [(r, r ^ 1) for r in range(16)]
Z_PAIR = [(r, r ^ 2) for r in range(16)]
Z_SKIP = [(r, r ^ 4) for r in range(16)]
YLO_FLIP = [(r, r ^ 8) for r in range(16)]


def send(name, value, axes, pairs):
    with jax.named_scope(name):
        return lax.ppermute(value, axes, pairs)


def up(name, value):
    return send(name + "_up", value, "shard", x_shift(1))


def down(name, value):
    return send(name + "_down", value, "shard", x_shift(-1))


def across(name, value):
    return send(name + "_across", value, "shard", Y_FLIP)


def dot(a, b, dims=((1,), (0,))):
    return lax.dot_general(a, b, (dims, ((), ())), preferred_element_type=F32)


def halves(value):
    high = value.astype(BF16)
    return high, (value - high.astype(F32)).astype(BF16)


def dot3(a, b, dims=((1,), (0,))):
    return dot(a[0], b[0], dims) + (dot(a[1], b[0], dims) + dot(a[0], b[1], dims))


def cosine_table():
    freqs = np.arange(16, dtype=np.float64)[:, None]
    points = np.arange(64, dtype=np.float64)[None, :]
    norming = np.where(freqs == 0.0, np.sqrt(1.0 / 64.0), np.sqrt(2.0 / 64.0))
    return norming * np.cos(np.pi * (2.0 * points + 1.0) * freqs / 128.0)


def table_parts():
    blocks = np.kron(np.eye(4), cosine_table())
    high = blocks.astype(jnp.bfloat16)
    low = (blocks - high.astype(np.float64)).astype(jnp.bfloat16)
    back = np.concatenate([high.T, high.T, low.T, np.zeros_like(high.T)], 1)
    return jnp.asarray(np.concatenate([high, low, back], 0))


def forward_t(whole, table):
    n = whole.shape[0]
    high, low = halves(whole)
    both = dot(high, table[:128], ((1,), (1,)))
    rowwise = both[:, :64] + (both[:, 64:] + dot(low, table[:64], ((1,), (1,))))
    out = []
    for at in range(0, n, 256):
        m = min(256, n - at)
        k = m // 4
        sides = jnp.concatenate(halves(rowwise[at : at + m, :]), 1)
        parts = table[:128] if m == 256 else jnp.concatenate([table[:k, :m], table[64 : 64 + k, :m]], 0)
        four = dot(parts, sides)
        out.append(four[:k, :64] + (four[k:, :64] + four[:k, 64:]))
    return out


def backward_t(coeffs, table):
    high, low = halves(coeffs)
    twice = jnp.concatenate([table[:64], table[:64]], 0)
    columns_of = dot(jnp.concatenate([high, low], 1), twice) + dot(high, table[64:128])
    out = []
    for at in range(0, coeffs.shape[0], 64):
        k = min(64, coeffs.shape[0] - at)
        high, low = halves(columns_of[at : at + k, :])
        if k == 64:
            out.append(dot(table[128:, :192], jnp.concatenate([high, low, high], 0)))
        else:
            out.append(dot3((table[:k, : 4 * k], table[64 : 64 + k, : 4 * k]), (high, low), ((0,), (0,))))
    return out


STEP = 128


def grads_block(rows, dx, tile, by_side, tiles):
    def where(row, place):
        first = ((place[0] + dx % 4) & 3) * SUPER + tile + by_side * place[1]
        return row * rows, pl.multiple_of(first * LANES, LANES)

    return pl.BlockSpec((pl.Element(rows), pl.Element(tiles * LANES)), where)


def columns(ref, first, tiles):
    return ref[:, first * LANES : (first + tiles) * LANES]


def step_kernel(body, n_ins, n_after, place, *refs):
    outs = refs[n_ins + n_after :]
    body(place, refs[:n_ins], outs[:-1])
    outs[-1][...] = jnp.zeros((8, LANES), F32)


class Steps:
    def __init__(self, place, grads):
        self.place, self.grads, self.mark = place, grads, []

    def __call__(self, name, body, slices, ins, out_tiles, after=()):
        after = [*self.mark, *after]
        with jax.named_scope(name):
            *outs, mark = pl.pallas_call(
                functools.partial(step_kernel, body, len(slices) + len(ins), len(after)),
                grid_spec=pltpu.PrefetchScalarGridSpec(
                    num_scalar_prefetch=1,
                    grid=(ROWS // STEP,),
                    in_specs=[grads_block(STEP, *piece) for piece in slices]
                    + [pl.BlockSpec((STEP, a.shape[1]), lambda r, _: (r, 0)) for a in ins]
                    + [pl.BlockSpec(memory_space=pl.ANY) for _ in after],
                    out_specs=[
                        pl.BlockSpec((STEP, t * LANES), lambda r, _: (r, 0)) for t in out_tiles
                    ]
                    + [pl.BlockSpec((8, LANES), lambda r, _: (0, 0))],
                ),
                out_shape=[jax.ShapeDtypeStruct((ROWS, t * LANES), F32) for t in out_tiles]
                + [jax.ShapeDtypeStruct((8, LANES), F32)],
                compiler_params=pltpu.CompilerParams(vmem_limit_bytes=VMEM_BYTES),
                cost_estimate=pl.CostEstimate(flops=0, bytes_accessed=1, transcendentals=0),
            )(self.place, *[self.grads] * len(slices), *ins, *after)
        self.mark = [mark]
        return outs


def read_body(place, ins, outs):
    ins = list(ins)
    for out in outs:
        at = 0
        while at < out.shape[1]:
            ref = ins.pop(0)
            out[:, at : at + ref.shape[1]] = ref[...].astype(F32)
            at += ref.shape[1]


def later_body(place, ins, outs):
    up_grads, down_grads, plus, minus = ins
    outs[0][...] = plus[...] + up_grads[...].astype(F32)
    outs[1][...] = minus[...] + down_grads[...].astype(F32)


def later_body(place, ins, outs):
    up_grads, down_grads, plus, minus = ins
    outs[0][...] = plus[...] + up_grads[...].astype(F32)
    outs[1][...] = minus[...] + down_grads[...].astype(F32)


def outer_body(first, place, ins, outs):
    up_grads, down_grads, came = ins[:3]
    ahead = columns(came, first, NBP) + up_grads[...].astype(F32)
    behind = columns(came, first + NBP, NB - NBP) + down_grads[...].astype(F32)
    if len(ins) > 3:
        ahead, behind = ahead + ins[3][...], behind + ins[4][...]
    outs[0][...] = ahead
    outs[1][...] = behind


def mix_a_body(place, ins, outs):
    g, plus, minus = ins

    @pl.when(place[1] == 0)
    def _():
        outs[0][...] = minus[...] + g[...].astype(F32)

    @pl.when(place[1] == 1)
    def _():
        w = NA * LANES
        outs[0][:, :w] = plus[...] + g[:, :w].astype(F32)
        outs[0][:, w:] = minus[:, :LANES] + g[:, w:].astype(F32)


def mix_b_body(place, ins, outs):
    g, plus, minus = ins

    @pl.when(place[1] == 0)
    def _():
        outs[0][...] = minus[...] + g[...].astype(F32)

    @pl.when(place[1] == 1)
    def _():
        outs[0][...] = plus[...] + g[...].astype(F32)


def pack(chunks):
    whole = jnp.concatenate(chunks, 0) if len(chunks) > 1 else chunks[0]
    n = whole.shape[0] // 2
    return jnp.concatenate([whole[:n], whole[n:]], 1)


def unpack(packed):
    return jnp.concatenate([packed[:, :64], packed[:, 64:]], 0)


def merge_kernel(plans, cols, n_before, n_ins, n_after, skips, place, *refs):
    momentum, table = refs[n_before : n_before + 2]
    ins = refs[n_before + 2 : n_before + 2 + n_ins]
    out, coeffs, mark, merged = refs[-4:]
    grads = refs[n_before + 2 + n_ins]
    for side, plan in enumerate(plans):

        @pl.when(place[1] == side)
        def _():
            for t, sources in enumerate(plan):
                total = columns(grads, t, 1).astype(F32)
                for ref, k in sources:
                    total = total + columns(ins[ref], k, 1)
                merged[t * LANES : (t + 1) * LANES, :] = total.T

    skip = pl.multiple_of(place[1] * 64, 64) if skips else 0
    whole = BETA * momentum[...] + merged[pl.ds(skip, cols), :]
    out[...] = whole
    coeffs[...] = pack(forward_t(whole, table[...]))
    mark[...] = jnp.zeros((8, LANES), F32)


def merge_call(name, steps, buffers, momentum_t, table, piece, first, row, cols, plans, ins):
    def rows(_, place):
        return pl.multiple_of(first[0] + (first[1] - first[0]) * place[1], 64), 0

    whole = lambda shape: pl.BlockSpec(shape, lambda i, _: (0, 0))
    part = pl.BlockSpec((pl.Element(cols), pl.Element(ROWS)), rows)
    packed = pl.BlockSpec((pl.Element(cols // 8), pl.Element(LANES)), lambda i, _: (row, 0))
    anywhere = lambda values: [pl.BlockSpec(memory_space=pl.ANY) for _ in values]
    tiles = piece[3]
    shapes = [(OWN_COLS, ROWS), (PACKED, LANES), (8, LANES)]
    with jax.named_scope(name):
        *buffers, mark = pl.pallas_call(
            functools.partial(
                merge_kernel, plans, cols, len(buffers), len(ins), len(steps.mark),
                cols < tiles * LANES,
            ),
            grid_spec=pltpu.PrefetchScalarGridSpec(
                num_scalar_prefetch=1,
                grid=(1,),
                in_specs=anywhere(buffers)
                + [part, whole(table.shape)]
                + [whole(a.shape) for a in ins]
                + [grads_block(ROWS, *piece)]
                + anywhere(steps.mark),
                out_specs=[part, packed, whole((8, LANES))],
                scratch_shapes=[pltpu.VMEM((tiles * LANES, ROWS), F32)],
            ),
            out_shape=[jax.ShapeDtypeStruct(shape, F32) for shape in shapes],
            input_output_aliases={1 + k: k for k in range(len(buffers))},
            compiler_params=pltpu.CompilerParams(vmem_limit_bytes=VMEM_BYTES),
            cost_estimate=pl.CostEstimate(flops=0, bytes_accessed=1, transcendentals=0),
        )(steps.place, *buffers, momentum_t, table, *ins, steps.grads, *steps.mark)
    steps.mark = [mark]
    return buffers


def groups_of(coeffs, groups):
    return [(g, unpack(coeffs[row : row + cols // 8, :])) for g, (_, row, cols) in enumerate(groups)]


def new_kernel(groups, place, whole, coeffs, table, out):
    for side in range(2):

        @pl.when(place[1] == side)
        def _():
            for g, chunks in groups_of(coeffs, groups):
                to = groups[g][0][side]
                for back in backward_t(chunks, table[...]):
                    end = to + back.shape[0]
                    out[to:end, :] = whole[to:end, :] - back
                    to = end


def update_kernel(groups, place, mine, other, table, out, coeffs):
    half = PACKED // 2
    coeffs[pl.ds(pl.multiple_of(place[3] * half, 8), half), :] = mine[...]
    coeffs[pl.ds(pl.multiple_of((1 - place[3]) * half, 8), half), :] = other[...]
    for side in range(2):

        @pl.when(place[1] == side)
        def _():
            for g, chunks in groups_of(coeffs, groups):
                to = groups[g][0][side]
                for back in backward_t(chunks, table[...]):
                    out[to : to + back.shape[0], :] = jnp.tanh((SHARP / 16.0) * back)
                    to += back.shape[0]


def output_call(name, kernel, place, ins, scratch):
    whole = lambda a: pl.BlockSpec(a.shape, lambda i, _: (0, 0))
    with jax.named_scope(name):
        return pl.pallas_call(
            kernel,
            grid_spec=pltpu.PrefetchScalarGridSpec(
                num_scalar_prefetch=1,
                grid=(1,),
                in_specs=[whole(a) for a in ins],
                out_specs=pl.BlockSpec((OWN_COLS, ROWS), lambda i, _: (0, 0)),
                scratch_shapes=scratch,
            ),
            out_shape=jax.ShapeDtypeStruct((OWN_COLS, ROWS), F32),
            compiler_params=pltpu.CompilerParams(vmem_limit_bytes=VMEM_BYTES),
            cost_estimate=pl.CostEstimate(flops=0, bytes_accessed=1, transcendentals=0),
        )(place, *ins)


def total_kernel(n, *refs):
    total = refs[0][...]
    for ref in refs[1:n]:
        total = total + ref[...]
    refs[-1][...] = total


def total_call(name, values, after):
    whole = lambda a: pl.BlockSpec(a.shape, lambda: (0, 0))
    with jax.named_scope(name):
        return pl.pallas_call(
            functools.partial(total_kernel, len(values)),
            in_specs=[whole(v) for v in values] + [pl.BlockSpec(memory_space=pl.ANY) for _ in after],
            out_specs=whole(values[0]),
            out_shape=jax.ShapeDtypeStruct(values[0].shape, F32),
            cost_estimate=pl.CostEstimate(flops=0, bytes_accessed=1, transcendentals=0),
        )(*values, *after)


def local(grads, momentum):
    grads = grads[0, 0]
    momentum_t = momentum[0].T
    shard = lax.axis_index("shard")
    x, yh = shard // 2, shard % 2
    table = table_parts()
    core = lax.axis_index("rep") % 2
    place = jnp.stack([x, yh, shard, core]).astype(jnp.int32)
    steps = Steps(place, grads)
    pairs = [[2 * k, 2 * k + 1] for k in range(4)]

    tiles_up, tiles_down = (21 - NA, NB), (21, 22 + NA)
    counts_up, counts_down = (NA, MIDDLE - NA), (NA + 1, MIDDLE - NA)

    def around(step, which, pair, after=()):
        name = "ab"[which] + str(step)
        slices = [
            (-1 - step, tiles_up[which], 0, counts_up[which]),
            (1 + step, tiles_down[which], 0, counts_down[which]),
        ]
        out = [counts_up[which], counts_down[which]]
        plus, minus = steps("add_" + name, later_body, slices, pair, out, after)
        return up(name, plus), down(name, minus)

    def cross(rounds):
        name = "cross" + "".join(map(str, rounds))
        slices = []
        for n in rounds:
            slices += [
                (-1 - n, SUPER - NB, NB - SUPER, NBP),
                (1 + n, SUPER - NB + NBP, NB - SUPER, NB - NBP),
            ]
        sent = steps("read_" + name, read_body, slices, [], [len(rounds) * NB])
        return across(name, sent[0])

    def outer(k, came, pair=(), after=()):
        slices = [(-1 - k, 0, SUPER - NB, NBP), (1 + k, NBP, SUPER - NB, NB - NBP)]
        body = functools.partial(outer_body, k % 2 * NB)
        plus, minus = steps(
            f"add_outer{k}", body, slices, [came, *pair], [NBP, NB - NBP], after
        )
        return up(f"outer{k}", plus), down(f"outer{k}", minus)

    slices, out = [], []
    for which in range(2):
        slices += [
            (-1, tiles_up[which], 0, counts_up[which]),
            (1, tiles_down[which], 0, counts_down[which]),
        ]
        out += [counts_up[which], counts_down[which]]
    plus_a, minus_a, plus_b, minus_b = steps("read_first", read_body, slices, [], out)
    a = up("a0", plus_a), down("a0", minus_a)
    b = up("b0", plus_b), down("b0", minus_b)
    y01 = cross((0, 1))
    y23 = cross((2, 3))
    a = around(1, 0, a)
    b = around(1, 1, b)
    o = outer(0, y01, after=a)
    a = around(2, 0, a, after=b)
    b = around(2, 1, b, after=o)
    ca = across("a", steps("mix_a", mix_a_body, [(0, 21, -NA, NA + 1)], a, [NA + 1])[0])
    o = outer(1, y01, o, after=a)
    mixed = steps(
        "mix_b", mix_b_body, [(0, 22 + NA, NB - 22 - NA, MIDDLE - NA)], b, [MIDDLE - NA]
    )
    cb = across("b", mixed[0])
    o = outer(2, y23, o, after=b)
    near, far = NA * LANES + 64, (MIDDLE - NA) * LANES
    groups = [
        (((21 - NA) * LANES, 0), 0, near),
        ((NB * LANES, near), near // 8, far),
        ((0, (SUPER - NB) * LANES - OWN_COLS), (near + far) // 8, NB * LANES),
    ]
    wide = lambda n, *refs: [[(r, t) for r in refs] for t in range(n)]
    buffers = merge_call(
        "merge_a", steps, [], momentum_t, table, (0, 21 - NA, NA, NA + 1), *groups[0],
        (wide(NA, 0, 2) + [[(1, 0), (2, NA)]], wide(NA + 1, 1, 2)), [*a, ca],
    )
    buffers = merge_call(
        "merge_b", steps, buffers, momentum_t, table, (0, NB, 22 + NA - NB, MIDDLE - NA),
        *groups[1], (wide(MIDDLE - NA, 0, 2), wide(MIDDLE - NA, 1, 2)), [*b, cb],
    )
    plan = [[(0, NB + t), (1, t) if t < NBP else (2, t - NBP)] for t in range(NB)]
    whole, coeffs = merge_call(
        "merge_outer", steps, buffers, momentum_t, table, (0, 0, SUPER - NB, NB), *groups[2],
        (plan, plan), [y23, *o],
    )
    half = PACKED // 2
    part = lambda c: lax.dynamic_slice(coeffs, (c * half, 0), (half, LANES))
    mine = part(core) + send("sum_core", part(1 - core), "rep", CORE_FLIP)
    came = [send(f"sum_z{k}", mine, "rep", z_shift(k)) for k in (2, 1, 3)]
    new_t = output_call(
        "new_momentum", functools.partial(new_kernel, groups), place, [whole, coeffs, table], []
    )
    mine = total_call("sum_z", [mine, *came], [new_t])
    mine = mine + send("sum_y", mine, "rep", YLO_FLIP)
    other = send("gather_core", mine, "rep", CORE_FLIP)
    update_t = output_call(
        "update", functools.partial(update_kernel, groups), place, [mine, other, table],
        [pltpu.VMEM((PACKED, LANES), F32)],
    )
    return new_t.T[None], update_t.T


def solution(mesh):
    placed = (P("rep", "shard", None, None), P("rep", None, "shard"))
    return jax.shard_map(
        local,
        mesh=mesh,
        in_specs=placed,
        out_specs=(P("rep", None, "shard"), P(None, "shard")),
        check_vma=False,
    )
```

time: 447 us -> 212 us (0.47)
  waiting for transfers between devices: 349 us -> 85.3 us
  Pallas kernels: 0 us -> 66.8 us
  starting transfers between devices: 0.04 us -> 43.3 us
  local copies, waits for them, and re-layouts: 42.3 us -> 12.6 us
  matrix products: 23.3 us -> 0 us
  other arithmetic: 17.7 us -> 2.48 us
  between operations: 14.1 us -> 0.8 us
    unnamed x3 -> x0, waiting for transfers between devices: 239 us -> none
    psum x1 -> x0, waiting for transfers between devices: 110 us -> none  [local(): summed_coeffs = lax.psum(coeffs, 'rep')]
    ppermute x0 -> x28, waiting for transfers between devices: none -> 85.3 us  [send(): return lax.ppermute(value, axes, pairs)]
    pallas_call x0 -> x18, Pallas kernels: none -> 66.8 us  [the longest x12 40.9 us: __call__(): pl.pallas_call(functools.partial(step_kernel, body, len(slices) + len(ins...]
    ppermute x0 -> x28, starting transfers between devices: none -> 43.3 us  [send(): return lax.ppermute(value, axes, pairs)]
    unnamed x9 -> x42, local copies, waits for them, and re-layouts: 35.7 us -> 11.7 us
    dot_general x6 -> x0, matrix products: 23.3 us -> none  [the longest x2 7.52 us: restore(): jnp.einsum('akbl,lm->akbm', coeffs, basis, precision=lax.Precision.HIGHEST)]
    convert_element_type x1 -> x0, other arithmetic: 12.7 us -> none  [local(): partials.astype(jnp.float32)]
  transfers between devices with their start and end apart: 2 -> 28, of which waited for: 2 -> 12; matrix products, arithmetic and copies ran while one was open for 2% -> 0% of each run, Pallas kernels for 0% -> 25%
where the time goes in v2:
time: 212 us; the launch traced here: 211 us
  waiting for transfers between devices  85.3 us (40%)
  Pallas kernels  66.8 us (32%)
  starting transfers between devices  43.3 us (20%)
  local copies, waits for them, and re-layouts  12.6 us (6%)
  other arithmetic  2.48 us (1%)
    ppermute x28, waiting for transfers between devices, send(): return lax.ppermute(value, axes, pairs)  85.3 us
    ppermute x28, starting transfers between devices, send(): return lax.ppermute(value, axes, pairs)  43.3 us
    pallas_call x12, Pallas kernels, __call__(): pl.pallas_call(functools.partial(step_kernel, body, len(slices) + len(ins...  40.9 us
    pallas_call x3, Pallas kernels, merge_call(): pl.pallas_call(functools.partial(merge_kernel, plans, cols, len(buffers),...  14.3 us
    unnamed x42, local copies, waits for them, and re-layouts  11.7 us
    pallas_call x2, Pallas kernels, output_call(): pl.pallas_call(kernel, grid_spec=pltpu.PrefetchScalarGridSpec(num_scalar_...  9.84 us
  transfers between devices with their start and end apart: 28, of which 12 were waited for; matrix products, arithmetic and copies ran while one was open for 0% of the time, Pallas kernels for 25%

profile of v2, /device:TPU:1, one launch (start us, length us, event | category | flops | bytes accessed | tf_op | source)
XLA Modules:
  0.0 211.2 jit_solution(217434633904427906)
XLA Ops:
  1.3 3.8 %read_first.1 = (f32[256,896]{1,0:T(8,128)}, f32[256,1024]{1,0:T(8,128)}, f32[256,768]{1,0:T(8,128)}, f32[256,768]{1,0:T(8,128)}, f32[8,128]{1,0:T(8,128)}) custom-call(s32[4]{0:T(128)} %pad_add_fusion.place, bf16[256,22016]{1,0:T(8,128)(2,1)} %bitcast.12, bf16[256,22016]{1,0:T(8,128)(2,1)} %bitcast.13, bf16[256,22016]{1,0:T(8,128)(2,1)} %bitcast.14, ...), custom_call_target="tpu_custom_call" | custom-call | bytes 1 | tf_op jit(solution)/shard_map/read_first/pallas_call | solution.py:157
  5.1 3.3 %collective-permute-start.1 = (f32[256,1024]{1,0:T(8,128)}, f32[256,1024]{1,0:T(8,128)S(1)}, u32[]{:S(2)}, u32[]{:S(2)}) collective-permute-start(f32[256,1024]{1,0:T(8,128)} %get-tuple-element.45), channel_id=1, source_target_pairs={{0,6},{1,7},{2,0},{3,1},{4,2},{5,3},{6,4},{7,5},{8,14},{9,15},{10,... | collective-permute-start | bytes 3145736 | tf_op jit(solution)/shard_map/a0_down/ppermute | solution.py:55
  8.4 3.3 %read_cross01.1 = (f32[256,2048]{1,0:T(8,128)}, f32[8,128]{1,0:T(8,128)}) custom-call(s32[4]{0:T(128)} %pad_add_fusion.place, bf16[256,22016]{1,0:T(8,128)(2,1)} %bitcast.16, bf16[256,22016]{1,0:T(8,128)(2,1)} %bitcast.17, bf16[256,22016]{1,0:T(8,128)(2,1)} %bitcast.18, bf16[256,22016]{1,0:T(8,128)(2,1)} %bitcast.19, f32[8,128]{1,0:T(8,128)} %get-tuple-element.46.refs_4_), custom_call_target="tpu_custom_call" | custom-call | bytes 1 | tf_op jit(solution)/shard_map/read_cross01/pallas_call | solution.py:157
  11.7 2.9 %collective-permute-start.4 = (f32[256,2048]{1,0:T(8,128)}, f32[256,2048]{1,0:T(8,128)S(1)}, u32[]{:S(2)}, u32[]{:S(2)}) collective-permute-start(f32[256,2048]{1,0:T(8,128)} %get-tuple-element.51), channel_id=1, source_target_pairs={{0,1},{1,0},{2,3},{3,2},{4,5},{5,4},{6,7},{7,6},{8,9},{9,8},{10,11... | collective-permute-start | bytes 6291464 | tf_op jit(solution)/shard_map/cross01_across/ppermute | solution.py:55
  17.4 3.2 %read_cross23.1 = (f32[256,2048]{1,0:T(8,128)}, f32[8,128]{1,0:T(8,128)}) custom-call(s32[4]{0:T(128)} %pad_add_fusion.place, bf16[256,22016]{1,0:T(8,128)(2,1)} %bitcast.20, bf16[256,22016]{1,0:T(8,128)(2,1)} %bitcast.21, bf16[256,22016]{1,0:T(8,128)(2,1)} %bitcast.22, bf16[256,22016]{1,0:T(8,128)(2,1)} %bitcast.23, f32[8,128]{1,0:T(8,128)} %get-tuple-element.47.refs_4_), custom_call_target="tpu_custom_call" | custom-call | bytes 1 | tf_op jit(solution)/shard_map/read_cross23/pallas_call | solution.py:157
  20.6 16.0 %collective-permute-done.refs_2_ = f32[256,896]{1,0:T(8,128)} collective-permute-done((f32[256,896]{1,0:T(8,128)S(1)}, f32[256,896]{1,0:T(8,128)}, u32[]{:S(2)}, u32[]{:S(2)}) %collective-permute-start) | collective-permute-done | bytes 917536 | tf_op jit(solution)/shard_map/a0_up/ppermute | solution.py:55
  37.6 3.6 %add_a1.1 = (f32[256,896]{1,0:T(8,128)}, f32[256,1024]{1,0:T(8,128)}, f32[8,128]{1,0:T(8,128)}) custom-call(s32[4]{0:T(128)} %pad_add_fusion.place, bf16[256,22016]{1,0:T(8,128)(2,1)} %bitcast.24, bf16[256,22016]{1,0:T(8,128)(2,1)} %bitcast.25, f32[256,896]{1,0:T(8,128)} %collective-permute-done.refs_2_, f32[256,1024]{1,0:T(8,128)} %copy-done.9, ...), custom_call_target="tpu_custom_call" | custom-call | bytes 1 | tf_op jit(solution)/shard_map/add_a1/pallas_call | solution.py:157
  43.9 9.5 %collective-permute-done.5.refs_2_ = f32[256,768]{1,0:T(8,128)} collective-permute-done((f32[256,768]{1,0:T(8,128)}, f32[256,768]{1,0:T(8,128)}, u32[]{:S(2)}, u32[]{:S(2)}) %collective-permute-start.5) | collective-permute-done | bytes 786464 | tf_op jit(solution)/shard_map/b0_up/ppermute | solution.py:55
  53.4 3.3 %add_b1.1 = (f32[256,768]{1,0:T(8,128)}, f32[256,768]{1,0:T(8,128)}, f32[8,128]{1,0:T(8,128)}) custom-call(s32[4]{0:T(128)} %pad_add_fusion.place, bf16[256,22016]{1,0:T(8,128)(2,1)} %bitcast.27, bf16[256,22016]{1,0:T(8,128)(2,1)} %bitcast.26, f32[256,768]{1,0:T(8,128)} %collective-permute-done.5.refs_2_, f32[256,768]{1,0:T(8,128)} %collective-permute-done.6.refs_3_, ...), custom_call_target="tpu_custom_call" | custom-call | bytes 1 | tf_op jit(solution)/shard_map/add_b1/pallas_call | solution.py:157
  59.5 13.6 %collective-permute-done.2.refs_4_.refs_2_ = f32[256,896]{1,0:T(8,128)} collective-permute-done((f32[256,896]{1,0:T(8,128)}, f32[256,896]{1,0:T(8,128)}, u32[]{:S(2)}, u32[]{:S(2)}) %collective-permute-start.2) | collective-permute-done | bytes 917536 | tf_op jit(solution)/shard_map/a1_up/ppermute | solution.py:55
  74.9 3.3 %add_outer0.1 = (f32[256,512]{1,0:T(8,128)}, f32[256,512]{1,0:T(8,128)}, f32[8,128]{1,0:T(8,128)}) custom-call(s32[4]{0:T(128)} %pad_add_fusion.place, bf16[256,22016]{1,0:T(8,128)(2,1)} %bitcast.28, bf16[256,22016]{1,0:T(8,128)(2,1)} %bitcast.29, f32[256,2048]{1,0:T(8,128)} %copy-done.1, f32[8,128]{1,0:T(8,128)} %get-tuple-element.55.refs_3_, ...), custom_call_target="tpu_custom_call" | custom-call | bytes 1 | tf_op jit(solution)/shard_map/add_outer0/pallas_call | solution.py:157
  78.2 2.7 %collective-permute-start.12 = (f32[256,512]{1,0:T(8,128)}, f32[256,512]{1,0:T(8,128)S(1)}, u32[]{:S(2)}, u32[]{:S(2)}) collective-permute-start(f32[256,512]{1,0:T(8,128)} %get-tuple-element.63), channel_id=1, source_target_pairs={{0,6},{1,7},{2,0},{3,1},{4,2},{5,3},{6,4},{7,5},{8,14},{9,15},{10,... | collective-permute-start | bytes 1572872 | tf_op jit(solution)/shard_map/outer0_down/ppermute | solution.py:55
  80.8 9.1 %collective-permute-done.7.refs_5_.refs_2_ = f32[256,768]{1,0:T(8,128)} collective-permute-done((f32[256,768]{1,0:T(8,128)}, f32[256,768]{1,0:T(8,128)}, u32[]{:S(2)}, u32[]{:S(2)}) %collective-permute-start.7) | collective-permute-done | bytes 786464 | tf_op jit(solution)/shard_map/b1_up/ppermute | solution.py:55
  89.9 3.6 %add_a2.1 = (f32[256,896]{1,0:T(8,128)}, f32[256,1024]{1,0:T(8,128)}, f32[8,128]{1,0:T(8,128)}) custom-call(s32[4]{0:T(128)} %pad_add_fusion.place, bf16[256,22016]{1,0:T(8,128)(2,1)} %bitcast.30, bf16[256,22016]{1,0:T(8,128)(2,1)} %bitcast.31, f32[256,896]{1,0:T(8,128)} %collective-permute-done.2.refs_4_.refs_2_, f32[256,1024]{1,0:T(8,128)} %copy-done.5, ...), custom_call_target="tpu_custom_call" | custom-call | bytes 1 | tf_op jit(solution)/shard_map/add_a2/pallas_call | solution.py:157
  95.0 6.2 %collective-permute-done.11.refs_5_.refs_3_ = f32[256,512]{1,0:T(8,128)S(1)} collective-permute-done((f32[256,512]{1,0:T(8,128)}, f32[256,512]{1,0:T(8,128)S(1)}, u32[]{:S(2)}, u32[]{:S(2)}) %collective-permute-start.11) | collective-permute-done | bytes 524320 | tf_op jit(solution)/shard_map/outer0_up/ppermute | solution.py:55
  102.2 3.3 %add_b2.1 = (f32[256,768]{1,0:T(8,128)}, f32[256,768]{1,0:T(8,128)}, f32[8,128]{1,0:T(8,128)}) custom-call(s32[4]{0:T(128)} %pad_add_fusion.place, bf16[256,22016]{1,0:T(8,128)(2,1)} %bitcast.32, bf16[256,22016]{1,0:T(8,128)(2,1)} %bitcast.33, f32[256,768]{1,0:T(8,128)} %collective-permute-done.7.refs_5_.refs_2_, ...), custom_call_target="tpu_custom_call" | custom-call | bytes 1 | tf_op jit(solution)/shard_map/add_b2/pallas_call | solution.py:157
  108.2 12.6 %collective-permute-done.9.refs_1_.refs_6_.refs_2_ = f32[256,896]{1,0:T(8,128)S(1)} collective-permute-done((f32[256,896]{1,0:T(8,128)}, f32[256,896]{1,0:T(8,128)S(1)}, u32[]{:S(2)}, u32[]{:S(2)}) %collective-permute-start.9) | collective-permute-done | bytes 917536 | tf_op jit(solution)/shard_map/a2_up/ppermute | solution.py:55
  122.1 3.2 %mix_a.1 = (f32[256,1024]{1,0:T(8,128)}, f32[8,128]{1,0:T(8,128)}) custom-call(s32[4]{0:T(128)} %pad_add_fusion.place, bf16[256,22016]{1,0:T(8,128)(2,1)} %bitcast.34, f32[256,896]{1,0:T(8,128)} %copy-done.2, f32[256,1024]{1,0:T(8,128)} %copy-done, f32[8,128]{1,0:T(8,128)} %get-tuple-element.64.refs_3_), custom_call_target="tpu_custom_call" | custom-call | bytes 1 | tf_op jit(solution)/shard_map/mix_a/pallas_call | solution.py:157
  127.5 3.6 %add_outer1.1 = (f32[256,512]{1,0:T(8,128)}, f32[256,512]{1,0:T(8,128)}, f32[8,128]{1,0:T(8,128)}) custom-call(s32[4]{0:T(128)} %pad_add_fusion.place, bf16[256,22016]{1,0:T(8,128)(2,1)} %bitcast.35, bf16[256,22016]{1,0:T(8,128)(2,1)} %bitcast.36, f32[256,2048]{1,0:T(8,128)} %copy-done.1, f32[256,512]{1,0:T(8,128)} %copy-done.6, f32[256,512]{1,0:T(8,128)} %copy-done.7, ...), custom_call_target="tpu_custom_call" | custom-call | bytes 1 | tf_op jit(solution)/shard_map/add_outer1/pallas_call | solution.py:157
  131.9 5.7 %collective-permute-done.17.refs_1_.refs_6_.refs_4_ = f32[256,768]{1,0:T(8,128)S(1)} collective-permute-done((f32[256,768]{1,0:T(8,128)}, f32[256,768]{1,0:T(8,128)S(1)}, u32[]{:S(2)}, u32[]{:S(2)}) %collective-permute-start.17) | collective-permute-done | bytes 786464 | tf_op jit(solution)/shard_map/b2_up/ppermute | solution.py:55
  138.7 3.0 %mix_b.1 = (f32[256,768]{1,0:T(8,128)}, f32[8,128]{1,0:T(8,128)}) custom-call(s32[4]{0:T(128)} %pad_add_fusion.place, bf16[256,22016]{1,0:T(8,128)(2,1)} %bitcast.37, f32[256,768]{1,0:T(8,128)} %copy-done.3, f32[256,768]{1,0:T(8,128)} %copy-done.4, f32[8,128]{1,0:T(8,128)} %get-tuple-element.72.refs_3_), custom_call_target="tpu_custom_call" | custom-call | bytes 1 | tf_op jit(solution)/shard_map/mix_b/pallas_call | solution.py:157
  144.1 4.7 %collective-permute-done.15.refs_3_ = f32[256,512]{1,0:T(8,128)S(1)} collective-permute-done((f32[256,512]{1,0:T(8,128)}, f32[256,512]{1,0:T(8,128)S(1)}, u32[]{:S(2)}, u32[]{:S(2)}) %collective-permute-start.15) | collective-permute-done | bytes 524320 | tf_op jit(solution)/shard_map/outer1_up/ppermute | solution.py:55
  149.6 3.7 %add_outer2.1 = (f32[256,512]{1,0:T(8,128)}, f32[256,512]{1,0:T(8,128)}, f32[8,128]{1,0:T(8,128)}) custom-call(s32[4]{0:T(128)} %pad_add_fusion.place, bf16[256,22016]{1,0:T(8,128)(2,1)} %bitcast.38, bf16[256,22016]{1,0:T(8,128)(2,1)} %bitcast.39, f32[256,2048]{1,0:T(8,128)} %collective-permute-done.14.refs_2_.refs_4_, f32[256,512]{1,0:T(8,128)} %copy-done.13, ...), custom_call_target="tpu_custom_call" | custom-call | bytes 1 | tf_op jit(solution)/shard_map/add_outer2/pallas_call | solution.py:157
  157.0 4.9 %merge_a.1 = (f32[2752,256]{1,0:T(8,128)}, f32[352,128]{1,0:T(8,128)}, f32[8,128]{1,0:T(8,128)}) custom-call(s32[4]{0:T(128)} %pad_add_fusion.place, f32[2752,256]{1,0:T(8,128)} %bitcast.43, bf16[384,256]{1,0:T(8,128)(2,1)} %constant.45.clone.refs_1_.refs_3_.table, f32[256,896]{1,0:T(8,128)} %copy-done.2, f32[256,1024]{1,0:T(8,128)} %copy-done, ...), custom_call_target="tpu_custom_call" | custom-call | bytes 1 | tf_op jit(solution)/shard_map/merge_a/pallas_call | solution.py:280
  161.9 2.9 %collective-permute-done.19.refs_6_ = f32[256,768]{1,0:T(8,128)S(1)} collective-permute-done((f32[256,768]{1,0:T(8,128)}, f32[256,768]{1,0:T(8,128)S(1)}, u32[]{:S(2)}, u32[]{:S(2)}) %collective-permute-start.19) | collective-permute-done | bytes 786464 | tf_op jit(solution)/shard_map/b_across/ppermute | solution.py:55
  165.6 4.4 %merge_b.1 = (f32[2752,256]{1,0:T(8,128)}, f32[352,128]{1,0:T(8,128)}, f32[8,128]{1,0:T(8,128)}) custom-call(s32[4]{0:T(128)} %pad_add_fusion.place, f32[2752,256]{1,0:T(8,128)} %get-tuple-element.75.refs_0_, f32[352,128]{1,0:T(8,128)} %get-tuple-element.76.refs_1_, f32[2752,256]{1,0:T(8,128)} %bitcast.44, ...), custom_call_target="tpu_custom_call", output_to_operand_aliasing={{0}: (1, {}), {1}: (2, {})} | custom-call | bytes 1 | tf_op jit(solution)/shard_map/merge_b/pallas_call | solution.py:280
  171.0 5.0 %merge_outer.1 = (f32[2752,256]{1,0:T(8,128)}, f32[352,128]{1,0:T(8,128)}, f32[8,128]{1,0:T(8,128)}) custom-call(s32[4]{0:T(128)} %pad_add_fusion.place, f32[2752,256]{1,0:T(8,128)} %get-tuple-element.79.refs_0_, f32[352,128]{1,0:T(8,128)} %get-tuple-element.80.refs_1_, f32[2752,256]{1,0:T(8,128)} %bitcast.45, ...), custom_call_target="tpu_custom_call", output_to_operand_aliasing={{0}: (1, {}), {1}: (2, {})} | custom-call | bytes 1 | tf_op jit(solution)/shard_map/merge_outer/pallas_call | solution.py:280
  176.9 4.7 %collective-permute-start.22 = (f32[176,128]{1,0:T(8,128)S(1)}, f32[176,128]{1,0:T(8,128)S(1)}, u32[]{:S(2)}, u32[]{:S(2)}) collective-permute-start(f32[176,128]{1,0:T(8,128)S(1)} %constant_dynamic-slice_fusion), channel_id=1, source_target_pairs={{0,8},{8,0},{16,24},{24,16},{32,40},{40,32},{48,56},{56,48},{64,72... | collective-permute-start | bytes 270344 | tf_op jit(solution)/shard_map/sum_core/ppermute | solution.py:55
  183.5 3.7 %collective-permute-start.23 = (f32[176,128]{1,0:T(8,128)S(1)}, f32[176,128]{1,0:T(8,128)S(1)}, u32[]{:S(2)}, u32[]{:S(2)}) collective-permute-start(f32[176,128]{1,0:T(8,128)S(1)} %dynamic-slice_add_fusion.refs_0_), channel_id=1, source_target_pairs={{0,32},{8,40},{16,48},{24,56},{32,0},{40,8},{48,16},{56,24},{64,96... | collective-permute-start | bytes 270344 | tf_op jit(solution)/shard_map/sum_z2/ppermute | solution.py:55
  189.9 5.4 %new_momentum.1.refs_4_ = f32[2752,256]{1,0:T(8,128)} custom-call(s32[4]{0:T(128)} %pad_add_fusion.place, f32[2752,256]{1,0:T(8,128)} %get-tuple-element.84.whole, f32[352,128]{1,0:T(8,128)} %get-tuple-element.85.coeffs, bf16[384,256]{1,0:T(8,128)(2,1)} %constant.45.clone.refs_1_.refs_3_.table), custom_call_target="tpu_custom_call" | custom-call | bytes 1 | tf_op jit(solution)/shard_map/new_momentum/pallas_call | solution.py:340
  198.7 3.0 %collective-permute-done.26 = f32[176,128]{1,0:T(8,128)S(1)} collective-permute-done((f32[176,128]{1,0:T(8,128)}, f32[176,128]{1,0:T(8,128)S(1)}, u32[]{:S(2)}, u32[]{:S(2)}) %collective-permute-start.26) | collective-permute-done | bytes 90144 | tf_op jit(solution)/shard_map/sum_y/ppermute | solution.py:55
  206.7 4.5 %update.1 = f32[2752,256]{1,0:T(8,128)} custom-call(s32[4]{0:T(128)} %pad_add_fusion.place, f32[176,128]{1,0:T(8,128)} %copy-done.15, f32[176,128]{1,0:T(8,128)} %copy-done.19, bf16[384,256]{1,0:T(8,128)(2,1)} %constant.45.clone.refs_1_.refs_3_.table), custom_call_target="tpu_custom_call" | custom-call | bytes 1 | tf_op jit(solution)/shard_map/update/pallas_call | solution.py:340
  (88 shorter events, 44.6 us)
Async XLA Ops:
  5.1 31.5 %collective-permute-start.1 = (f32[256,1024]{1,0:T(8,128)}, f32[256,1024]{1,0:T(8,128)S(1)}, u32[]{:S(2)}, u32[]{:S(2)}) collective-permute-start(f32[256,1024]{1,0:T(8,128)} %get-tuple-element.45), channel_id=1, source_target_pairs={{0,6},{1,7},{2,0},{3,1},{4,2},{5,3},{6,4},{7,5},{8,14},{9,15},{10,... | collective-permute-start | bytes 3145736 | tf_op jit(solution)/shard_map/a0_down/ppermute | solution.py:55
  8.4 6.2 %copy-start.20 = (f32[256,896]{1,0:T(8,128)S(1)}, f32[256,896]{1,0:T(8,128)}, u32[]{:S(2)}) copy-start(f32[256,896]{1,0:T(8,128)} %get-tuple-element.44) | copy-start | bytes 2752516
  11.7 61.5 %collective-permute-start.4 = (f32[256,2048]{1,0:T(8,128)}, f32[256,2048]{1,0:T(8,128)S(1)}, u32[]{:S(2)}, u32[]{:S(2)}) collective-permute-start(f32[256,2048]{1,0:T(8,128)} %get-tuple-element.51), channel_id=1, source_target_pairs={{0,1},{1,0},{2,3},{3,2},{4,5},{5,4},{6,7},{7,6},{8,9},{9,8},{10,11... | collective-permute-start | bytes 6291464 | tf_op jit(solution)/shard_map/cross01_across/ppermute | solution.py:55
  14.7 21.9 %collective-permute-start = (f32[256,896]{1,0:T(8,128)S(1)}, f32[256,896]{1,0:T(8,128)}, u32[]{:S(2)}, u32[]{:S(2)}) collective-permute-start(f32[256,896]{1,0:T(8,128)S(1)} %copy-done.20), channel_id=1, source_target_pairs={{0,2},{1,3},{2,4},{3,5},{4,6},{5,7},{6,0},{7,1},{8,10},{9,11},{10,... | collective-permute-start | bytes 2752520 | tf_op jit(solution)/shard_map/a0_up/ppermute | solution.py:55
  14.7 38.8 %collective-permute-start.5 = (f32[256,768]{1,0:T(8,128)}, f32[256,768]{1,0:T(8,128)}, u32[]{:S(2)}, u32[]{:S(2)}) collective-permute-start(f32[256,768]{1,0:T(8,128)} %get-tuple-element.52), channel_id=1, source_target_pairs={{0,2},{1,3},{2,4},{3,5},{4,6},{5,7},{6,0},{7,1},{8,10},{9,11},{10,... | collective-permute-start | bytes 2359304 | tf_op jit(solution)/shard_map/b0_up/ppermute | solution.py:55
  14.9 38.6 %collective-permute-start.6 = (f32[256,768]{1,0:T(8,128)}, f32[256,768]{1,0:T(8,128)}, u32[]{:S(2)}, u32[]{:S(2)}) collective-permute-start(f32[256,768]{1,0:T(8,128)} %get-tuple-element.53), channel_id=1, source_target_pairs={{0,6},{1,7},{2,0},{3,1},{4,2},{5,3},{6,4},{7,5},{8,14},{9,15},{10,... | collective-permute-start | bytes 2359304 | tf_op jit(solution)/shard_map/b0_down/ppermute | solution.py:55
  41.2 31.9 %collective-permute-start.2 = (f32[256,896]{1,0:T(8,128)}, f32[256,896]{1,0:T(8,128)}, u32[]{:S(2)}, u32[]{:S(2)}) collective-permute-start(f32[256,896]{1,0:T(8,128)} %get-tuple-element.49), channel_id=1, source_target_pairs={{0,2},{1,3},{2,4},{3,5},{4,6},{5,7},{6,0},{7,1},{8,10},{9,11},{10,... | collective-permute-start | bytes 2752520 | tf_op jit(solution)/shard_map/a1_up/ppermute | solution.py:55
  41.2 32.0 %collective-permute-start.3 = (f32[256,1024]{1,0:T(8,128)}, f32[256,1024]{1,0:T(8,128)S(1)}, u32[]{:S(2)}, u32[]{:S(2)}) collective-permute-start(f32[256,1024]{1,0:T(8,128)} %get-tuple-element.50), channel_id=1, source_target_pairs={{0,6},{1,7},{2,0},{3,1},{4,2},{5,3},{6,4},{7,5},{8,14},{9,15},{10,... | collective-permute-start | bytes 3145736 | tf_op jit(solution)/shard_map/a1_down/ppermute | solution.py:55
  56.8 33.2 %collective-permute-start.7 = (f32[256,768]{1,0:T(8,128)}, f32[256,768]{1,0:T(8,128)}, u32[]{:S(2)}, u32[]{:S(2)}) collective-permute-start(f32[256,768]{1,0:T(8,128)} %get-tuple-element.57), channel_id=1, source_target_pairs={{0,2},{1,3},{2,4},{3,5},{4,6},{5,7},{6,0},{7,1},{8,10},{9,11},{10,... | collective-permute-start | bytes 2359304 | tf_op jit(solution)/shard_map/b1_up/ppermute | solution.py:55
  56.8 33.2 %collective-permute-start.8 = (f32[256,768]{1,0:T(8,128)}, f32[256,768]{1,0:T(8,128)}, u32[]{:S(2)}, u32[]{:S(2)}) collective-permute-start(f32[256,768]{1,0:T(8,128)} %get-tuple-element.58), channel_id=1, source_target_pairs={{0,6},{1,7},{2,0},{3,1},{4,2},{5,3},{6,4},{7,5},{8,14},{9,15},{10,... | collective-permute-start | bytes 2359304 | tf_op jit(solution)/shard_map/b1_down/ppermute | solution.py:55
  73.1 71.0 %collective-permute-start.14 = (f32[256,2048]{1,0:T(8,128)}, f32[256,2048]{1,0:T(8,128)}, u32[]{:S(2)}, u32[]{:S(2)}) collective-permute-start(f32[256,2048]{1,0:T(8,128)} %get-tuple-element.66), channel_id=1, source_target_pairs={{0,1},{1,0},{2,3},{3,2},{4,5},{5,4},{6,7},{7,6},{8,9},{9,8},{10,11... | collective-permute-start | bytes 6291464 | tf_op jit(solution)/shard_map/cross23_across/ppermute | solution.py:55
  73.2 1.7 copy-start.1
  78.2 23.0 %collective-permute-start.11 = (f32[256,512]{1,0:T(8,128)}, f32[256,512]{1,0:T(8,128)S(1)}, u32[]{:S(2)}, u32[]{:S(2)}) collective-permute-start(f32[256,512]{1,0:T(8,128)} %get-tuple-element.62), channel_id=1, source_target_pairs={{0,2},{1,3},{2,4},{3,5},{4,6},{5,7},{6,0},{7,1},{8,10},{9,11},{10,... | collective-permute-start | bytes 1572872 | tf_op jit(solution)/shard_map/outer0_up/ppermute | solution.py:55
  78.2 23.0 %collective-permute-start.12 = (f32[256,512]{1,0:T(8,128)}, f32[256,512]{1,0:T(8,128)S(1)}, u32[]{:S(2)}, u32[]{:S(2)}) collective-permute-start(f32[256,512]{1,0:T(8,128)} %get-tuple-element.63), channel_id=1, source_target_pairs={{0,6},{1,7},{2,0},{3,1},{4,2},{5,3},{6,4},{7,5},{8,14},{9,15},{10,... | collective-permute-start | bytes 1572872 | tf_op jit(solution)/shard_map/outer0_down/ppermute | solution.py:55
  93.5 27.3 %collective-permute-start.10 = (f32[256,1024]{1,0:T(8,128)}, f32[256,1024]{1,0:T(8,128)S(1)}, u32[]{:S(2)}, u32[]{:S(2)}) collective-permute-start(f32[256,1024]{1,0:T(8,128)} %get-tuple-element.60), channel_id=1, source_target_pairs={{0,6},{1,7},{2,0},{3,1},{4,2},{5,3},{6,4},{7,5},{8,14},{9,15},{10,... | collective-permute-start | bytes 3145736 | tf_op jit(solution)/shard_map/a2_down/ppermute | solution.py:55
  93.7 27.1 %collective-permute-start.9 = (f32[256,896]{1,0:T(8,128)}, f32[256,896]{1,0:T(8,128)S(1)}, u32[]{:S(2)}, u32[]{:S(2)}) collective-permute-start(f32[256,896]{1,0:T(8,128)} %get-tuple-element.59), channel_id=1, source_target_pairs={{0,2},{1,3},{2,4},{3,5},{4,6},{5,7},{6,0},{7,1},{8,10},{9,11},{10,... | collective-permute-start | bytes 2752520 | tf_op jit(solution)/shard_map/a2_up/ppermute | solution.py:55
  105.5 32.0 %collective-permute-start.17 = (f32[256,768]{1,0:T(8,128)}, f32[256,768]{1,0:T(8,128)S(1)}, u32[]{:S(2)}, u32[]{:S(2)}) collective-permute-start(f32[256,768]{1,0:T(8,128)} %get-tuple-element.70), channel_id=1, source_target_pairs={{0,2},{1,3},{2,4},{3,5},{4,6},{5,7},{6,0},{7,1},{8,10},{9,11},{10,... | collective-permute-start | bytes 2359304 | tf_op jit(solution)/shard_map/b2_up/ppermute | solution.py:55
  105.6 32.0 %collective-permute-start.18 = (f32[256,768]{1,0:T(8,128)}, f32[256,768]{1,0:T(8,128)S(1)}, u32[]{:S(2)}, u32[]{:S(2)}) collective-permute-start(f32[256,768]{1,0:T(8,128)} %get-tuple-element.71), channel_id=1, source_target_pairs={{0,6},{1,7},{2,0},{3,1},{4,2},{5,3},{6,4},{7,5},{8,14},{9,15},{10,... | collective-permute-start | bytes 2359304 | tf_op jit(solution)/shard_map/b2_down/ppermute | solution.py:55
  125.3 30.7 %collective-permute-start.13 = (f32[256,1024]{1,0:T(8,128)}, f32[256,1024]{1,0:T(8,128)S(1)}, u32[]{:S(2)}, u32[]{:S(2)}) collective-permute-start(f32[256,1024]{1,0:T(8,128)} %get-tuple-element.65), channel_id=1, source_target_pairs={{0,1},{1,0},{2,3},{3,2},{4,5},{5,4},{6,7},{7,6},{8,9},{9,8},{10,11... | collective-permute-start | bytes 3145736 | tf_op jit(solution)/shard_map/a_across/ppermute | solution.py:55
  131.1 17.7 %collective-permute-start.15 = (f32[256,512]{1,0:T(8,128)}, f32[256,512]{1,0:T(8,128)S(1)}, u32[]{:S(2)}, u32[]{:S(2)}) collective-permute-start(f32[256,512]{1,0:T(8,128)} %get-tuple-element.68), channel_id=1, source_target_pairs={{0,2},{1,3},{2,4},{3,5},{4,6},{5,7},{6,0},{7,1},{8,10},{9,11},{10,... | collective-permute-start | bytes 1572872 | tf_op jit(solution)/shard_map/outer1_up/ppermute | solution.py:55
  137.6 11.2 %collective-permute-start.16 = (f32[256,512]{1,0:T(8,128)}, f32[256,512]{1,0:T(8,128)}, u32[]{:S(2)}, u32[]{:S(2)}) collective-permute-start(f32[256,512]{1,0:T(8,128)} %get-tuple-element.69), channel_id=1, source_target_pairs={{0,6},{1,7},{2,0},{3,1},{4,2},{5,3},{6,4},{7,5},{8,14},{9,15},{10,... | collective-permute-start | bytes 1572872 | tf_op jit(solution)/shard_map/outer1_down/ppermute | solution.py:55
  141.7 23.0 %collective-permute-start.19 = (f32[256,768]{1,0:T(8,128)}, f32[256,768]{1,0:T(8,128)S(1)}, u32[]{:S(2)}, u32[]{:S(2)}) collective-permute-start(f32[256,768]{1,0:T(8,128)} %get-tuple-element.77), channel_id=1, source_target_pairs={{0,1},{1,0},{2,3},{3,2},{4,5},{5,4},{6,7},{7,6},{8,9},{9,8},{10,11... | collective-permute-start | bytes 2359304 | tf_op jit(solution)/shard_map/b_across/ppermute | solution.py:55
  153.3 16.7 %collective-permute-start.20 = (f32[256,512]{1,0:T(8,128)}, f32[256,512]{1,0:T(8,128)S(1)}, u32[]{:S(2)}, u32[]{:S(2)}) collective-permute-start(f32[256,512]{1,0:T(8,128)} %get-tuple-element.81), channel_id=1, source_target_pairs={{0,2},{1,3},{2,4},{3,5},{4,6},{5,7},{6,0},{7,1},{8,10},{9,11},{10,... | collective-permute-start | bytes 1572872 | tf_op jit(solution)/shard_map/outer2_up/ppermute | solution.py:55
  153.3 16.7 %collective-permute-start.21 = (f32[256,512]{1,0:T(8,128)}, f32[256,512]{1,0:T(8,128)S(1)}, u32[]{:S(2)}, u32[]{:S(2)}) collective-permute-start(f32[256,512]{1,0:T(8,128)} %get-tuple-element.82), channel_id=1, source_target_pairs={{0,6},{1,7},{2,0},{3,1},{4,2},{5,3},{6,4},{7,5},{8,14},{9,15},{10,... | collective-permute-start | bytes 1572872 | tf_op jit(solution)/shard_map/outer2_down/ppermute | solution.py:55
  176.9 5.7 %collective-permute-start.22 = (f32[176,128]{1,0:T(8,128)S(1)}, f32[176,128]{1,0:T(8,128)S(1)}, u32[]{:S(2)}, u32[]{:S(2)}) collective-permute-start(f32[176,128]{1,0:T(8,128)S(1)} %constant_dynamic-slice_fusion), channel_id=1, source_target_pairs={{0,8},{8,0},{16,24},{24,16},{32,40},{40,32},{48,56},{56,48},{64,72... | collective-permute-start | bytes 270344 | tf_op jit(solution)/shard_map/sum_core/ppermute | solution.py:55
  183.5 11.7 %copy-start.14 = (f32[176,128]{1,0:T(8,128)}, f32[176,128]{1,0:T(8,128)S(1)}, u32[]{:S(2)}) copy-start(f32[176,128]{1,0:T(8,128)S(1)} %dynamic-slice_add_fusion.refs_0_) | copy-start | bytes 270340
  183.5 11.7 %collective-permute-start.23 = (f32[176,128]{1,0:T(8,128)S(1)}, f32[176,128]{1,0:T(8,128)S(1)}, u32[]{:S(2)}, u32[]{:S(2)}) collective-permute-start(f32[176,128]{1,0:T(8,128)S(1)} %dynamic-slice_add_fusion.refs_0_), channel_id=1, source_target_pairs={{0,32},{8,40},{16,48},{24,56},{32,0},{40,8},{48,16},{56,24},{64,96... | collective-permute-start | bytes 270344 | tf_op jit(solution)/shard_map/sum_z2/ppermute | solution.py:55
  187.2 8.0 %collective-permute-start.24 = (f32[176,128]{1,0:T(8,128)S(1)}, f32[176,128]{1,0:T(8,128)S(1)}, u32[]{:S(2)}, u32[]{:S(2)}) collective-permute-start(f32[176,128]{1,0:T(8,128)S(1)} %dynamic-slice_add_fusion.refs_0_), channel_id=1, source_target_pairs={{0,16},{8,24},{16,32},{24,40},{32,48},{40,56},{48,0},{56,8},{64,80... | collective-permute-start | bytes 270344 | tf_op jit(solution)/shard_map/sum_z1/ppermute | solution.py:55
  187.9 7.3 %collective-permute-start.25 = (f32[176,128]{1,0:T(8,128)S(1)}, f32[176,128]{1,0:T(8,128)S(1)}, u32[]{:S(2)}, u32[]{:S(2)}) collective-permute-start(f32[176,128]{1,0:T(8,128)S(1)} %dynamic-slice_add_fusion.refs_0_), channel_id=1, source_target_pairs={{0,48},{8,56},{16,0},{24,8},{32,16},{40,24},{48,32},{56,40},{64,11... | collective-permute-start | bytes 270344 | tf_op jit(solution)/shard_map/sum_z3/ppermute | solution.py:55
  198.2 3.6 %collective-permute-start.26 = (f32[176,128]{1,0:T(8,128)}, f32[176,128]{1,0:T(8,128)S(1)}, u32[]{:S(2)}, u32[]{:S(2)}) collective-permute-start(f32[176,128]{1,0:T(8,128)} %sum_z.1), channel_id=1, source_target_pairs={{0,64},{8,72},{16,80},{24,88},{32,96},{40,104},{48,112},{56,120},{... | collective-permute-start | bytes 270344 | tf_op jit(solution)/shard_map/sum_y/ppermute | solution.py:55
  202.7 3.4 %copy-start.15 = (f32[176,128]{1,0:T(8,128)}, f32[176,128]{1,0:T(8,128)S(1)}, u32[]{:S(2)}) copy-start(f32[176,128]{1,0:T(8,128)S(1)} %add.25.mine) | copy-start | bytes 270340
  202.7 3.4 %collective-permute-start.27 = (f32[176,128]{1,0:T(8,128)S(1)}, f32[176,128]{1,0:T(8,128)S(1)}, u32[]{:S(2)}, u32[]{:S(2)}) collective-permute-start(f32[176,128]{1,0:T(8,128)S(1)} %add.25.mine), channel_id=1, source_target_pairs={{0,8},{8,0},{16,24},{24,16},{32,40},{40,32},{48,56},{56,48},{64,72... | collective-permute-start | bytes 270344 | tf_op jit(solution)/shard_map/gather_core/ppermute | solution.py:55
  (17 other events, 15.1 us)

commit v3 on v2

--- a/solution.py
+++ b/solution.py
@@ -13,10 +13,10 @@
 ROWS = 256
 LANES = 128
 SUPER = 43
-NB = 8
-NBP = 4
+NB = 9
+NBP = 5
 MIDDLE = 21 - NB
-NA = 7
+NA = 6
 OWN_COLS = 2752
 PACKED = 352
 
@@ -244,79 +244,103 @@
     return jnp.concatenate([packed[:, :64], packed[:, 64:]], 0)
 
 
-def merge_kernel(plans, cols, n_before, n_ins, n_after, skips, place, *refs):
-    momentum, table = refs[n_before : n_before + 2]
-    ins = refs[n_before + 2 : n_before + 2 + n_ins]
-    out, coeffs, mark, merged = refs[-4:]
-    grads = refs[n_before + 2 + n_ins]
-    for side, plan in enumerate(plans):
-
-        @pl.when(place[1] == side)
-        def _():
-            for t, sources in enumerate(plan):
-                total = columns(grads, t, 1).astype(F32)
-                for ref, k in sources:
-                    total = total + columns(ins[ref], k, 1)
-                merged[t * LANES : (t + 1) * LANES, :] = total.T
-
-    skip = pl.multiple_of(place[1] * 64, 64) if skips else 0
-    whole = BETA * momentum[...] + merged[pl.ds(skip, cols), :]
-    out[...] = whole
-    coeffs[...] = pack(forward_t(whole, table[...]))
+def merge_kernel(groups, n_before, final, place, *refs):
+    refs = list(refs[n_before:])
+    table, coeffs, mark, merged = refs.pop(0), refs[-3], refs[-2], refs[-1]
+    row = 0
+    for g, (n_ins, cols, tiles, skips, plans) in enumerate(groups):
+        momentum, grads, *ins = refs[: 2 + n_ins]
+        del refs[: 2 + n_ins]
+        out = refs[len(refs) - 3 - len(groups) + g]
+        for side, plan in enumerate(plans):
+
+            @pl.when(place[1] == side)
+            def _():
+                for t, sources in enumerate(plan):
+                    total = columns(grads, t, 1).astype(F32)
+                    for ref, k in sources:
+                        total = total + columns(ins[ref], k, 1)
+                    merged[t * LANES : (t + 1) * LANES, :] = total.T
+
+        skip = pl.multiple_of(place[1] * 64, 64) if skips else 0
+        whole = BETA * momentum[...] + merged[pl.ds(skip, cols), :]
+        chunks = forward_t(whole, table[...])
+        coeffs[row : row + cols // 8, :] = pack(chunks)
+        if final:
+            at = 0
+            for back in backward_t(jnp.concatenate(chunks, 0), table[...]):
+                end = at + back.shape[0]
+                out[at:end, :] = whole[at:end] - back
+                at = end
+        else:
+            out[...] = whole
+        row += cols // 8
     mark[...] = jnp.zeros((8, LANES), F32)
 
 
-def merge_call(name, steps, buffers, momentum_t, table, piece, first, row, cols, plans, ins):
-    def rows(_, place):
-        return pl.multiple_of(first[0] + (first[1] - first[0]) * place[1], 64), 0
-
+def merge_call(name, steps, before, momentum_t, table, row, groups, final=False):
     whole = lambda shape: pl.BlockSpec(shape, lambda i, _: (0, 0))
-    part = pl.BlockSpec((pl.Element(cols), pl.Element(ROWS)), rows)
-    packed = pl.BlockSpec((pl.Element(cols // 8), pl.Element(LANES)), lambda i, _: (row, 0))
-    anywhere = lambda values: [pl.BlockSpec(memory_space=pl.ANY) for _ in values]
-    tiles = piece[3]
-    shapes = [(OWN_COLS, ROWS), (PACKED, LANES), (8, LANES)]
+
+    def part(first, cols):
+        def rows(_, place):
+            return pl.multiple_of(first[0] + (first[1] - first[0]) * place[1], 64), 0
+
+        return pl.BlockSpec((pl.Element(cols), pl.Element(ROWS)), rows)
+
+    before = [*before, *steps.mark]
+    aliases = {1: len(groups)} if len(before) > len(steps.mark) else {}
+    anywhere = [pl.BlockSpec(memory_space=pl.ANY) for _ in before]
+    in_specs, ins, counts = [], [], []
+    for piece, first, cols, plans, values in groups:
+        in_specs += [part(first, cols), grads_block(ROWS, *piece), *[whole(v.shape) for v in values]]
+        ins += [momentum_t, steps.grads, *values]
+        counts.append((len(values), cols, piece[3], cols < piece[3] * LANES, plans))
+    rows = sum(group[2] for group in groups) // 8
+    packed = pl.BlockSpec((pl.Element(rows), pl.Element(LANES)), lambda i, _: (row, 0))
+    shapes = [(group[2], ROWS) for group in groups]
+    tiles = max(group[0][3] for group in groups)
     with jax.named_scope(name):
-        *buffers, mark = pl.pallas_call(
-            functools.partial(
-                merge_kernel, plans, cols, len(buffers), len(ins), len(steps.mark),
-                cols < tiles * LANES,
-            ),
+        *wholes, coeffs, mark = pl.pallas_call(
+            functools.partial(merge_kernel, counts, len(before), final),
             grid_spec=pltpu.PrefetchScalarGridSpec(
                 num_scalar_prefetch=1,
                 grid=(1,),
-                in_specs=anywhere(buffers)
-                + [part, whole(table.shape)]
-                + [whole(a.shape) for a in ins]
-                + [grads_block(ROWS, *piece)]
-                + anywhere(steps.mark),
-                out_specs=[part, packed, whole((8, LANES))],
+                in_specs=anywhere + [whole(table.shape)] + in_specs,
+                out_specs=[whole(shape) for shape in shapes] + [packed, whole((8, LANES))],
                 scratch_shapes=[pltpu.VMEM((tiles * LANES, ROWS), F32)],
             ),
-            out_shape=[jax.ShapeDtypeStruct(shape, F32) for shape in shapes],
-            input_output_aliases={1 + k: k for k in range(len(buffers))},
+            out_shape=[
+                jax.ShapeDtypeStruct(shape, F32)
+                for shape in [*shapes, (PACKED, LANES), (8, LANES)]
+            ],
+            input_output_aliases=aliases,
             compiler_params=pltpu.CompilerParams(vmem_limit_bytes=VMEM_BYTES),
             cost_estimate=pl.CostEstimate(flops=0, bytes_accessed=1, transcendentals=0),
-        )(steps.place, *buffers, momentum_t, table, *ins, steps.grads, *steps.mark)
+        )(steps.place, *before, table, *ins)
     steps.mark = [mark]
-    return buffers
+    return wholes, coeffs
 
 
 def groups_of(coeffs, groups):
     return [(g, unpack(coeffs[row : row + cols // 8, :])) for g, (_, row, cols) in enumerate(groups)]
 
 
-def new_kernel(groups, place, whole, coeffs, table, out):
+def new_kernel(groups, place, *refs):
+    *wholes, coeffs, table, out = refs
     for side in range(2):
 
         @pl.when(place[1] == side)
         def _():
             for g, chunks in groups_of(coeffs, groups):
-                to = groups[g][0][side]
+                to, n = groups[g][0][side], groups[g][2]
+                if g == 0:
+                    out[to : to + n, :] = wholes[0][...]
+                    continue
+                at = 0
                 for back in backward_t(chunks, table[...]):
-                    end = to + back.shape[0]
-                    out[to:end, :] = whole[to:end, :] - back
-                    to = end
+                    n = back.shape[0]
+                    out[to + at : to + at + n, :] = wholes[g][at : at + n, :] - back
+                    at += n
 
 
 def update_kernel(groups, place, mine, other, table, out, coeffs):
@@ -428,16 +452,17 @@
     y23 = cross((2, 3))
     a = around(1, 0, a)
     b = around(1, 1, b)
-    o = outer(0, y01, after=a)
-    a = around(2, 0, a, after=b)
-    b = around(2, 1, b, after=o)
+    a = around(2, 0, a)
+    o = outer(0, y01, after=b)
+    b = around(2, 1, b, after=a)
     ca = across("a", steps("mix_a", mix_a_body, [(0, 21, -NA, NA + 1)], a, [NA + 1])[0])
-    o = outer(1, y01, o, after=a)
+    o = outer(1, y01, o, after=[y23])
     mixed = steps(
         "mix_b", mix_b_body, [(0, 22 + NA, NB - 22 - NA, MIDDLE - NA)], b, [MIDDLE - NA]
     )
     cb = across("b", mixed[0])
     o = outer(2, y23, o, after=b)
+
     near, far = NA * LANES + 64, (MIDDLE - NA) * LANES
     groups = [
         (((21 - NA) * LANES, 0), 0, near),
@@ -445,25 +470,28 @@
         ((0, (SUPER - NB) * LANES - OWN_COLS), (near + far) // 8, NB * LANES),
     ]
     wide = lambda n, *refs: [[(r, t) for r in refs] for t in range(n)]
-    buffers = merge_call(
-        "merge_a", steps, [], momentum_t, table, (0, 21 - NA, NA, NA + 1), *groups[0],
-        (wide(NA, 0, 2) + [[(1, 0), (2, NA)]], wide(NA + 1, 1, 2)), [*a, ca],
+    plan = [[(0, NB + t), (1, t) if t < NBP else (2, t - NBP)] for t in range(NB)]
+    sides = (wide(NA, 0, 2) + [[(1, 0), (2, NA)]], wide(NA + 1, 1, 2))
+    (whole_a,), coeffs = merge_call(
+        "merge_a", steps, [], momentum_t, table, groups[0][1],
+        [((0, 21 - NA, NA, NA + 1), groups[0][0], near, sides, [*a, ca])],
+        final=True,
     )
-    buffers = merge_call(
-        "merge_b", steps, buffers, momentum_t, table, (0, NB, 22 + NA - NB, MIDDLE - NA),
-        *groups[1], (wide(MIDDLE - NA, 0, 2), wide(MIDDLE - NA, 1, 2)), [*b, cb],
-    )
-    plan = [[(0, NB + t), (1, t) if t < NBP else (2, t - NBP)] for t in range(NB)]
-    whole, coeffs = merge_call(
-        "merge_outer", steps, buffers, momentum_t, table, (0, 0, SUPER - NB, NB), *groups[2],
-        (plan, plan), [y23, *o],
+    sides = (wide(MIDDLE - NA, 0, 2), wide(MIDDLE - NA, 1, 2))
+    rest, coeffs = merge_call(
+        "merge_rest", steps, [coeffs], momentum_t, table, groups[1][1],
+        [
+            ((0, NB, 22 + NA - NB, MIDDLE - NA), groups[1][0], far, sides, [*b, cb]),
+            ((0, 0, SUPER - NB, NB), groups[2][0], NB * LANES, (plan, plan), [y23, *o]),
+        ],
     )
     half = PACKED // 2
     part = lambda c: lax.dynamic_slice(coeffs, (c * half, 0), (half, LANES))
     mine = part(core) + send("sum_core", part(1 - core), "rep", CORE_FLIP)
     came = [send(f"sum_z{k}", mine, "rep", z_shift(k)) for k in (2, 1, 3)]
     new_t = output_call(
-        "new_momentum", functools.partial(new_kernel, groups), place, [whole, coeffs, table], []
+        "new_momentum", functools.partial(new_kernel, groups), place,
+        [whole_a, *rest, coeffs, table], [],
     )
     mine = total_call("sum_z", [mine, *came], [new_t])
     mine = mine + send("sum_y", mine, "rep", YLO_FLIP)

time: 212 us -> 205 us (0.967)
  waiting for transfers between devices: 85.3 us -> 79.7 us
    ppermute x28, waiting for transfers between devices: 85.3 us -> 79.7 us  [send(): return lax.ppermute(value, axes, pairs)]
    pallas_call x3 -> x2, Pallas kernels: 14.3 us -> 12.6 us  [merge_call(): pl.pallas_call(functools.partial(merge_kernel, counts, len(before), final...]
    unnamed x42 -> x40, local copies, waits for them, and re-layouts: 11.7 us -> 10.1 us
  transfers between devices with their start and end apart: 28 -> 28, of which waited for: 12 -> 18; matrix products, arithmetic and copies ran while one was open for 0% -> 0% of each run, Pallas kernels for 25% -> 23%
where the time goes in v3:
time: 205 us; the launch traced here: 204 us
  waiting for transfers between devices  79.7 us (39%)
  Pallas kernels  65.2 us (32%)
  starting transfers between devices  44.8 us (22%)
  local copies, waits for them, and re-layouts  11 us (5%)
  other arithmetic  2.4 us (1%)
    ppermute x28, waiting for transfers between devices, send(): return lax.ppermute(value, axes, pairs)  79.7 us
    ppermute x28, starting transfers between devices, send(): return lax.ppermute(value, axes, pairs)  44.8 us
    pallas_call x12, Pallas kernels, __call__(): pl.pallas_call(functools.partial(step_kernel, body, len(slices) + len(ins...  41.2 us
    pallas_call x2, Pallas kernels, merge_call(): pl.pallas_call(functools.partial(merge_kernel, counts, len(before), final...  12.6 us
    unnamed x40, local copies, waits for them, and re-layouts  10.1 us
    pallas_call x2, Pallas kernels, output_call(): pl.pallas_call(kernel, grid_spec=pltpu.PrefetchScalarGridSpec(num_scalar_...  9.69 us
  transfers between devices with their start and end apart: 28, of which 18 were waited for; matrix products, arithmetic and copies ran while one was open for 0% of the time, Pallas kernels for 23%

profile of v3, /device:TPU:1, one launch (start us, length us, event | category | flops | bytes accessed | tf_op | source)
XLA Modules:
  0.0 203.9 jit_solution(6978556571492544324)
XLA Ops:
  1.2 3.7 %read_first.1 = (f32[256,768]{1,0:T(8,128)}, f32[256,896]{1,0:T(8,128)}, f32[256,768]{1,0:T(8,128)}, f32[256,768]{1,0:T(8,128)}, f32[8,128]{1,0:T(8,128)}) custom-call(s32[4]{0:T(128)} %pad_add_fusion.place, bf16[256,22016]{1,0:T(8,128)(2,1)} %bitcast.12, bf16[256,22016]{1,0:T(8,128)(2,1)} %bitcast.13, bf16[256,22016]{1,0:T(8,128)(2,1)} %bitcast.14, ...), custom_call_target="tpu_custom_call" | custom-call | bytes 1 | tf_op jit(solution)/shard_map/read_first/pallas_call | solution.py:157
  4.9 3.3 %collective-permute-start.3 = (f32[256,896]{1,0:T(8,128)}, f32[256,896]{1,0:T(8,128)S(1)}, u32[]{:S(2)}, u32[]{:S(2)}) collective-permute-start(f32[256,896]{1,0:T(8,128)} %get-tuple-element.47), channel_id=1, source_target_pairs={{0,6},{1,7},{2,0},{3,1},{4,2},{5,3},{6,4},{7,5},{8,14},{9,15},{10,... | collective-permute-start | bytes 2752520 | tf_op jit(solution)/shard_map/a0_down/ppermute | solution.py:55
  8.3 3.4 %read_cross01.1 = (f32[256,2304]{1,0:T(8,128)}, f32[8,128]{1,0:T(8,128)}) custom-call(s32[4]{0:T(128)} %pad_add_fusion.place, bf16[256,22016]{1,0:T(8,128)(2,1)} %bitcast.16, bf16[256,22016]{1,0:T(8,128)(2,1)} %bitcast.17, bf16[256,22016]{1,0:T(8,128)(2,1)} %bitcast.18, bf16[256,22016]{1,0:T(8,128)(2,1)} %bitcast.19, f32[8,128]{1,0:T(8,128)} %get-tuple-element.42.refs_4_), custom_call_target="tpu_custom_call" | custom-call | bytes 1 | tf_op jit(solution)/shard_map/read_cross01/pallas_call | solution.py:157
  11.7 2.9 %collective-permute-start.1 = (f32[256,2304]{1,0:T(8,128)}, f32[256,2304]{1,0:T(8,128)}, u32[]{:S(2)}, u32[]{:S(2)}) collective-permute-start(f32[256,2304]{1,0:T(8,128)} %get-tuple-element.45), channel_id=1, source_target_pairs={{0,1},{1,0},{2,3},{3,2},{4,5},{5,4},{6,7},{7,6},{8,9},{9,8},{10,11... | collective-permute-start | bytes 7077896 | tf_op jit(solution)/shard_map/cross01_across/ppermute | solution.py:55
  17.3 3.3 %read_cross23.1 = (f32[256,2304]{1,0:T(8,128)}, f32[8,128]{1,0:T(8,128)}) custom-call(s32[4]{0:T(128)} %pad_add_fusion.place, bf16[256,22016]{1,0:T(8,128)(2,1)} %bitcast.20, bf16[256,22016]{1,0:T(8,128)(2,1)} %bitcast.21, bf16[256,22016]{1,0:T(8,128)(2,1)} %bitcast.22, bf16[256,22016]{1,0:T(8,128)(2,1)} %bitcast.23, f32[8,128]{1,0:T(8,128)} %get-tuple-element.43.refs_4_), custom_call_target="tpu_custom_call" | custom-call | bytes 1 | tf_op jit(solution)/shard_map/read_cross23/pallas_call | solution.py:157
  20.6 7.3 %collective-permute-done.2.refs_2_ = f32[256,768]{1,0:T(8,128)S(1)} collective-permute-done((f32[256,768]{1,0:T(8,128)}, f32[256,768]{1,0:T(8,128)S(1)}, u32[]{:S(2)}, u32[]{:S(2)}) %collective-permute-start.2) | collective-permute-done | bytes 786464 | tf_op jit(solution)/shard_map/a0_up/ppermute | solution.py:55
  32.5 3.5 %add_a1.1 = (f32[256,768]{1,0:T(8,128)}, f32[256,896]{1,0:T(8,128)}, f32[8,128]{1,0:T(8,128)}) custom-call(s32[4]{0:T(128)} %pad_add_fusion.place, bf16[256,22016]{1,0:T(8,128)(2,1)} %bitcast.24, bf16[256,22016]{1,0:T(8,128)(2,1)} %bitcast.25, f32[256,768]{1,0:T(8,128)} %copy-done.6, f32[256,896]{1,0:T(8,128)} %copy-done.4, f32[8,128]{1,0:T(8,128)} %get-tuple-element.48.refs_4_), custom_call_target="tpu_custom_call" | custom-call | bytes 1 | tf_op jit(solution)/shard_map/add_a1/pallas_call | solution.py:157
  36.0 8.8 %collective-permute-done.6.refs_2_ = f32[256,768]{1,0:T(8,128)} collective-permute-done((f32[256,768]{1,0:T(8,128)}, f32[256,768]{1,0:T(8,128)}, u32[]{:S(2)}, u32[]{:S(2)}) %collective-permute-start.6) | collective-permute-done | bytes 786464 | tf_op jit(solution)/shard_map/b0_up/ppermute | solution.py:55
  44.7 3.3 %add_b1.1 = (f32[256,768]{1,0:T(8,128)}, f32[256,768]{1,0:T(8,128)}, f32[8,128]{1,0:T(8,128)}) custom-call(s32[4]{0:T(128)} %pad_add_fusion.place, bf16[256,22016]{1,0:T(8,128)(2,1)} %bitcast.27, bf16[256,22016]{1,0:T(8,128)(2,1)} %bitcast.26, f32[256,768]{1,0:T(8,128)} %collective-permute-done.6.refs_2_, f32[256,768]{1,0:T(8,128)} %collective-permute-done.7.refs_3_, ...), custom_call_target="tpu_custom_call" | custom-call | bytes 1 | tf_op jit(solution)/shard_map/add_b1/pallas_call | solution.py:157
  49.5 12.0 %collective-permute-done.4.refs_2_ = f32[256,768]{1,0:T(8,128)} collective-permute-done((f32[256,768]{1,0:T(8,128)}, f32[256,768]{1,0:T(8,128)}, u32[]{:S(2)}, u32[]{:S(2)}) %collective-permute-start.4) | collective-permute-done | bytes 786464 | tf_op jit(solution)/shard_map/a1_up/ppermute | solution.py:55
  64.5 3.5 %add_a2.1 = (f32[256,768]{1,0:T(8,128)}, f32[256,896]{1,0:T(8,128)}, f32[8,128]{1,0:T(8,128)}) custom-call(s32[4]{0:T(128)} %pad_add_fusion.place, bf16[256,22016]{1,0:T(8,128)(2,1)} %bitcast.28, bf16[256,22016]{1,0:T(8,128)(2,1)} %bitcast.29, f32[256,768]{1,0:T(8,128)} %collective-permute-done.4.refs_2_, f32[256,896]{1,0:T(8,128)} %copy-done.5, ...), custom_call_target="tpu_custom_call" | custom-call | bytes 1 | tf_op jit(solution)/shard_map/add_a2/pallas_call | solution.py:157
  69.6 8.8 %collective-permute-done.8.refs_4_.refs_2_ = f32[256,768]{1,0:T(8,128)} collective-permute-done((f32[256,768]{1,0:T(8,128)}, f32[256,768]{1,0:T(8,128)}, u32[]{:S(2)}, u32[]{:S(2)}) %collective-permute-start.8) | collective-permute-done | bytes 786464 | tf_op jit(solution)/shard_map/b1_up/ppermute | solution.py:55
  78.4 3.1 %collective-permute-done.9.refs_5_.refs_3_ = f32[256,768]{1,0:T(8,128)} collective-permute-done((f32[256,768]{1,0:T(8,128)}, f32[256,768]{1,0:T(8,128)}, u32[]{:S(2)}, u32[]{:S(2)}) %collective-permute-start.9) | collective-permute-done | bytes 786464 | tf_op jit(solution)/shard_map/b1_down/ppermute | solution.py:55
  81.5 3.5 %add_outer0.1 = (f32[256,640]{1,0:T(8,128)}, f32[256,512]{1,0:T(8,128)}, f32[8,128]{1,0:T(8,128)}) custom-call(s32[4]{0:T(128)} %pad_add_fusion.place, bf16[256,22016]{1,0:T(8,128)(2,1)} %bitcast.30, bf16[256,22016]{1,0:T(8,128)(2,1)} %bitcast.31, f32[256,2304]{1,0:T(8,128)} %collective-permute-done.1.refs_2_, f32[8,128]{1,0:T(8,128)} %get-tuple-element.55.refs_3_, ...), custom_call_target="tpu_custom_call" | custom-call | bytes 1 | tf_op jit(solution)/shard_map/add_outer0/pallas_call | solution.py:157
  87.7 9.5 %collective-permute-done.12.refs_5_.refs_1_.refs_4_ = f32[256,768]{1,0:T(8,128)} collective-permute-done((f32[256,768]{1,0:T(8,128)}, f32[256,768]{1,0:T(8,128)}, u32[]{:S(2)}, u32[]{:S(2)}) %collective-permute-start.12) | collective-permute-done | bytes 786464 | tf_op jit(solution)/shard_map/a2_up/ppermute | solution.py:55
  97.1 4.1 %collective-permute-done.13.refs_6_.refs_2_.refs_5_ = f32[256,896]{1,0:T(8,128)S(1)} collective-permute-done((f32[256,896]{1,0:T(8,128)}, f32[256,896]{1,0:T(8,128)S(1)}, u32[]{:S(2)}, u32[]{:S(2)}) %collective-permute-start.13) | collective-permute-done | bytes 917536 | tf_op jit(solution)/shard_map/a2_down/ppermute | solution.py:55
  102.1 3.4 %add_b2.1 = (f32[256,768]{1,0:T(8,128)}, f32[256,768]{1,0:T(8,128)}, f32[8,128]{1,0:T(8,128)}) custom-call(s32[4]{0:T(128)} %pad_add_fusion.place, bf16[256,22016]{1,0:T(8,128)(2,1)} %bitcast.32, bf16[256,22016]{1,0:T(8,128)(2,1)} %bitcast.33, f32[256,768]{1,0:T(8,128)} %collective-permute-done.8.refs_4_.refs_2_, ...), custom_call_target="tpu_custom_call" | custom-call | bytes 1 | tf_op jit(solution)/shard_map/add_b2/pallas_call | solution.py:157
  108.2 3.1 %mix_a.1 = (f32[256,896]{1,0:T(8,128)}, f32[8,128]{1,0:T(8,128)}) custom-call(s32[4]{0:T(128)} %pad_add_fusion.place, bf16[256,22016]{1,0:T(8,128)(2,1)} %bitcast.34, f32[256,768]{1,0:T(8,128)} %collective-permute-done.12.refs_5_.refs_1_.refs_4_, f32[256,896]{1,0:T(8,128)} %copy-done.1, f32[8,128]{1,0:T(8,128)} %get-tuple-element.63.refs_3_), custom_call_target="tpu_custom_call" | custom-call | bytes 1 | tf_op jit(solution)/shard_map/mix_a/pallas_call | solution.py:157
  111.3 4.5 %collective-permute-done.refs_6_.refs_2_.refs_10_ = f32[256,2304]{1,0:T(8,128)S(1)} collective-permute-done((f32[256,2304]{1,0:T(8,128)}, f32[256,2304]{1,0:T(8,128)S(1)}, u32[]{:S(2)}, u32[]{:S(2)}) %collective-permute-start) | collective-permute-done | bytes 2359328 | tf_op jit(solution)/shard_map/cross23_across/ppermute | solution.py:55
  117.4 3.8 %add_outer1.1 = (f32[256,640]{1,0:T(8,128)}, f32[256,512]{1,0:T(8,128)}, f32[8,128]{1,0:T(8,128)}) custom-call(s32[4]{0:T(128)} %pad_add_fusion.place, bf16[256,22016]{1,0:T(8,128)(2,1)} %bitcast.35, bf16[256,22016]{1,0:T(8,128)(2,1)} %bitcast.36, f32[256,2304]{1,0:T(8,128)} %collective-permute-done.1.refs_2_, f32[256,640]{1,0:T(8,128)} %collective-permute-done.10.refs_3_, ...), custom_call_target="tpu_custom_call" | custom-call | bytes 1 | tf_op jit(solution)/shard_map/add_outer1/pallas_call | solution.py:157
  123.8 3.0 %collective-permute-start.18 = (f32[256,896]{1,0:T(8,128)}, f32[256,896]{1,0:T(8,128)S(1)}, u32[]{:S(2)}, u32[]{:S(2)}) collective-permute-start(f32[256,896]{1,0:T(8,128)} %get-tuple-element.72), channel_id=1, source_target_pairs={{0,1},{1,0},{2,3},{3,2},{4,5},{5,4},{6,7},{7,6},{8,9},{9,8},{10,11... | collective-permute-start | bytes 2752520 | tf_op jit(solution)/shard_map/a_across/ppermute | solution.py:55
  129.3 3.0 %mix_b.1 = (f32[256,768]{1,0:T(8,128)}, f32[8,128]{1,0:T(8,128)}) custom-call(s32[4]{0:T(128)} %pad_add_fusion.place, bf16[256,22016]{1,0:T(8,128)(2,1)} %bitcast.37, f32[256,768]{1,0:T(8,128)} %copy-done.2, f32[256,768]{1,0:T(8,128)} %collective-permute-done.17.refs_2_.refs_7_.refs_6_, f32[8,128]{1,0:T(8,128)} %get-tuple-element.69.refs_3_), custom_call_target="tpu_custom_call" | custom-call | bytes 1 | tf_op jit(solution)/shard_map/mix_b/pallas_call | solution.py:157
  132.3 2.9 %collective-permute-start.19 = (f32[256,768]{1,0:T(8,128)}, f32[256,768]{1,0:T(8,128)S(1)}, u32[]{:S(2)}, u32[]{:S(2)}) collective-permute-start(f32[256,768]{1,0:T(8,128)} %get-tuple-element.76), channel_id=1, source_target_pairs={{0,1},{1,0},{2,3},{3,2},{4,5},{5,4},{6,7},{7,6},{8,9},{9,8},{10,11... | collective-permute-start | bytes 2359304 | tf_op jit(solution)/shard_map/b_across/ppermute | solution.py:55
  135.2 5.2 %collective-permute-done.15.refs_4_ = f32[256,512]{1,0:T(8,128)S(1)} collective-permute-done((f32[256,512]{1,0:T(8,128)}, f32[256,512]{1,0:T(8,128)S(1)}, u32[]{:S(2)}, u32[]{:S(2)}) %collective-permute-start.15) | collective-permute-done | bytes 524320 | tf_op jit(solution)/shard_map/outer1_down/ppermute | solution.py:55
  142.7 3.8 %add_outer2.1 = (f32[256,640]{1,0:T(8,128)}, f32[256,512]{1,0:T(8,128)}, f32[8,128]{1,0:T(8,128)}) custom-call(s32[4]{0:T(128)} %pad_add_fusion.place, bf16[256,22016]{1,0:T(8,128)(2,1)} %bitcast.38, bf16[256,22016]{1,0:T(8,128)(2,1)} %bitcast.39, f32[256,2304]{1,0:T(8,128)} %copy-done, f32[256,640]{1,0:T(8,128)} %copy-done.8, f32[256,512]{1,0:T(8,128)} %copy-done.12, ...), custom_call_target="tpu_custom_call" | custom-call | bytes 1 | tf_op jit(solution)/shard_map/add_outer2/pallas_call | solution.py:157
  150.1 5.3 %merge_a.1 = (f32[832,256]{1,0:T(8,128)}, f32[352,128]{1,0:T(8,128)}, f32[8,128]{1,0:T(8,128)}) custom-call(s32[4]{0:T(128)} %pad_add_fusion.place, f32[8,128]{1,0:T(8,128)} %get-tuple-element.71.refs_0_, bf16[384,256]{1,0:T(8,128)(2,1)} %constant.45.clone.refs_1_.refs_2_.refs_4_.table, f32[2752,256]{1,0:T(8,128)} %bitcast.43, bf16[256,22016]{1,0:T(8,128)(2,1)} %bitcast.40, ...), custom_call_target="tpu_custom_call" | custom-call | bytes 1 | tf_op jit(solution)/shard_map/merge_a/pallas_call | solution.py:303
  157.6 4.3 %collective-permute-done.19.refs_7_ = f32[256,768]{1,0:T(8,128)S(1)} collective-permute-done((f32[256,768]{1,0:T(8,128)}, f32[256,768]{1,0:T(8,128)S(1)}, u32[]{:S(2)}, u32[]{:S(2)}) %collective-permute-start.19) | collective-permute-done | bytes 786464 | tf_op jit(solution)/shard_map/b_across/ppermute | solution.py:55
  163.0 7.3 %merge_rest.1 = (f32[768,256]{1,0:T(8,128)}, f32[1152,256]{1,0:T(8,128)}, f32[352,128]{1,0:T(8,128)}, f32[8,128]{1,0:T(8,128)}) custom-call(s32[4]{0:T(128)} %pad_add_fusion.place, f32[352,128]{1,0:T(8,128)} %get-tuple-element.74.refs_0_, f32[8,128]{1,0:T(8,128)} %get-tuple-element.75.refs_1_, ...), custom_call_target="tpu_custom_call", output_to_operand_aliasing={{2}: (1, {})} | custom-call | bytes 1 | tf_op jit(solution)/shard_map/merge_rest/pallas_call | solution.py:303
  171.2 3.3 %collective-permute-start.22 = (f32[176,128]{1,0:T(8,128)S(1)}, f32[176,128]{1,0:T(8,128)S(1)}, u32[]{:S(2)}, u32[]{:S(2)}) collective-permute-start(f32[176,128]{1,0:T(8,128)S(1)} %constant_dynamic-slice_fusion), channel_id=1, source_target_pairs={{0,8},{8,0},{16,24},{24,16},{32,40},{40,32},{48,56},{56,48},{64,72... | collective-permute-start | bytes 270344 | tf_op jit(solution)/shard_map/sum_core/ppermute | solution.py:55
  176.4 3.7 %collective-permute-start.23 = (f32[176,128]{1,0:T(8,128)S(1)}, f32[176,128]{1,0:T(8,128)S(1)}, u32[]{:S(2)}, u32[]{:S(2)}) collective-permute-start(f32[176,128]{1,0:T(8,128)S(1)} %dynamic-slice_add_fusion.refs_0_), channel_id=1, source_target_pairs={{0,32},{8,40},{16,48},{24,56},{32,0},{40,8},{48,16},{56,24},{64,96... | collective-permute-start | bytes 270344 | tf_op jit(solution)/shard_map/sum_z2/ppermute | solution.py:55
  182.7 5.1 %new_momentum.1.refs_4_ = f32[2752,256]{1,0:T(8,128)} custom-call(s32[4]{0:T(128)} %pad_add_fusion.place, f32[832,256]{1,0:T(8,128)} %get-tuple-element.73.refs_0_, f32[768,256]{1,0:T(8,128)} %get-tuple-element.79.refs_1_, f32[1152,256]{1,0:T(8,128)} %get-tuple-element.80.refs_2_, f32[352,128]{1,0:T(8,128)} %get-tuple-element.81.refs_3_, ...), custom_call_target="tpu_custom_call" | custom-call | bytes 1 | tf_op jit(solution)/shard_map/new_momentum/pallas_call | solution.py:364
  199.3 4.6 %update.1 = f32[2752,256]{1,0:T(8,128)} custom-call(s32[4]{0:T(128)} %pad_add_fusion.place, f32[176,128]{1,0:T(8,128)} %copy-done.14, f32[176,128]{1,0:T(8,128)} %copy-done.18, bf16[384,256]{1,0:T(8,128)(2,1)} %constant.45.clone.refs_1_.refs_2_.refs_4_.table), custom_call_target="tpu_custom_call" | custom-call | bytes 1 | tf_op jit(solution)/shard_map/update/pallas_call | solution.py:364
  (85 shorter events, 53.0 us)
Async XLA Ops:
  4.9 26.6 %collective-permute-start.3 = (f32[256,896]{1,0:T(8,128)}, f32[256,896]{1,0:T(8,128)S(1)}, u32[]{:S(2)}, u32[]{:S(2)}) collective-permute-start(f32[256,896]{1,0:T(8,128)} %get-tuple-element.47), channel_id=1, source_target_pairs={{0,6},{1,7},{2,0},{3,1},{4,2},{5,3},{6,4},{7,5},{8,14},{9,15},{10,... | collective-permute-start | bytes 2752520 | tf_op jit(solution)/shard_map/a0_down/ppermute | solution.py:55
  8.3 19.6 %collective-permute-start.2 = (f32[256,768]{1,0:T(8,128)}, f32[256,768]{1,0:T(8,128)S(1)}, u32[]{:S(2)}, u32[]{:S(2)}) collective-permute-start(f32[256,768]{1,0:T(8,128)} %get-tuple-element.46), channel_id=1, source_target_pairs={{0,2},{1,3},{2,4},{3,5},{4,6},{5,7},{6,0},{7,1},{8,10},{9,11},{10,... | collective-permute-start | bytes 2359304 | tf_op jit(solution)/shard_map/a0_up/ppermute | solution.py:55
  8.3 6.6 %copy-start.19 = (f32[256,768]{1,0:T(8,128)S(1)}, f32[256,768]{1,0:T(8,128)}, u32[]{:S(2)}) copy-start(f32[256,768]{1,0:T(8,128)} %get-tuple-element.52) | copy-start | bytes 2359300
  11.7 69.8 %collective-permute-start.1 = (f32[256,2304]{1,0:T(8,128)}, f32[256,2304]{1,0:T(8,128)}, u32[]{:S(2)}, u32[]{:S(2)}) collective-permute-start(f32[256,2304]{1,0:T(8,128)} %get-tuple-element.45), channel_id=1, source_target_pairs={{0,1},{1,0},{2,3},{3,2},{4,5},{5,4},{6,7},{7,6},{8,9},{9,8},{10,11... | collective-permute-start | bytes 7077896 | tf_op jit(solution)/shard_map/cross01_across/ppermute | solution.py:55
  14.6 30.1 %collective-permute-start.6 = (f32[256,768]{1,0:T(8,128)}, f32[256,768]{1,0:T(8,128)}, u32[]{:S(2)}, u32[]{:S(2)}) collective-permute-start(f32[256,768]{1,0:T(8,128)} %get-tuple-element.51), channel_id=1, source_target_pairs={{0,2},{1,3},{2,4},{3,5},{4,6},{5,7},{6,0},{7,1},{8,10},{9,11},{10,... | collective-permute-start | bytes 2359304 | tf_op jit(solution)/shard_map/b0_up/ppermute | solution.py:55
  14.8 29.9 %collective-permute-start.7 = (f32[256,768]{1,0:T(8,128)S(1)}, f32[256,768]{1,0:T(8,128)}, u32[]{:S(2)}, u32[]{:S(2)}) collective-permute-start(f32[256,768]{1,0:T(8,128)S(1)} %copy-done.19), channel_id=1, source_target_pairs={{0,6},{1,7},{2,0},{3,1},{4,2},{5,3},{6,4},{7,5},{8,14},{9,15},{10,... | collective-permute-start | bytes 2359304 | tf_op jit(solution)/shard_map/b0_down/ppermute | solution.py:55
  28.8 87.0 %collective-permute-start = (f32[256,2304]{1,0:T(8,128)}, f32[256,2304]{1,0:T(8,128)S(1)}, u32[]{:S(2)}, u32[]{:S(2)}) collective-permute-start(f32[256,2304]{1,0:T(8,128)} %get-tuple-element.44), channel_id=1, source_target_pairs={{0,1},{1,0},{2,3},{3,2},{4,5},{5,4},{6,7},{7,6},{8,9},{9,8},{10,11... | collective-permute-start | bytes 7077896 | tf_op jit(solution)/shard_map/cross23_across/ppermute | solution.py:55
  36.0 25.6 %collective-permute-start.4 = (f32[256,768]{1,0:T(8,128)}, f32[256,768]{1,0:T(8,128)}, u32[]{:S(2)}, u32[]{:S(2)}) collective-permute-start(f32[256,768]{1,0:T(8,128)} %get-tuple-element.49), channel_id=1, source_target_pairs={{0,2},{1,3},{2,4},{3,5},{4,6},{5,7},{6,0},{7,1},{8,10},{9,11},{10,... | collective-permute-start | bytes 2359304 | tf_op jit(solution)/shard_map/a1_up/ppermute | solution.py:55
  44.7 18.8 %collective-permute-start.5 = (f32[256,896]{1,0:T(8,128)}, f32[256,896]{1,0:T(8,128)S(1)}, u32[]{:S(2)}, u32[]{:S(2)}) collective-permute-start(f32[256,896]{1,0:T(8,128)} %get-tuple-element.50), channel_id=1, source_target_pairs={{0,6},{1,7},{2,0},{3,1},{4,2},{5,3},{6,4},{7,5},{8,14},{9,15},{10,... | collective-permute-start | bytes 2752520 | tf_op jit(solution)/shard_map/a1_down/ppermute | solution.py:55
  48.1 30.4 %collective-permute-start.8 = (f32[256,768]{1,0:T(8,128)}, f32[256,768]{1,0:T(8,128)}, u32[]{:S(2)}, u32[]{:S(2)}) collective-permute-start(f32[256,768]{1,0:T(8,128)} %get-tuple-element.56), channel_id=1, source_target_pairs={{0,2},{1,3},{2,4},{3,5},{4,6},{5,7},{6,0},{7,1},{8,10},{9,11},{10,... | collective-permute-start | bytes 2359304 | tf_op jit(solution)/shard_map/b1_up/ppermute | solution.py:55
  61.6 19.9 %collective-permute-start.9 = (f32[256,768]{1,0:T(8,128)}, f32[256,768]{1,0:T(8,128)}, u32[]{:S(2)}, u32[]{:S(2)}) collective-permute-start(f32[256,768]{1,0:T(8,128)} %get-tuple-element.57), channel_id=1, source_target_pairs={{0,6},{1,7},{2,0},{3,1},{4,2},{5,3},{6,4},{7,5},{8,14},{9,15},{10,... | collective-permute-start | bytes 2359304 | tf_op jit(solution)/shard_map/b1_down/ppermute | solution.py:55
  68.1 33.1 %collective-permute-start.13 = (f32[256,896]{1,0:T(8,128)}, f32[256,896]{1,0:T(8,128)S(1)}, u32[]{:S(2)}, u32[]{:S(2)}) collective-permute-start(f32[256,896]{1,0:T(8,128)} %get-tuple-element.61), channel_id=1, source_target_pairs={{0,6},{1,7},{2,0},{3,1},{4,2},{5,3},{6,4},{7,5},{8,14},{9,15},{10,... | collective-permute-start | bytes 2752520 | tf_op jit(solution)/shard_map/a2_down/ppermute | solution.py:55
  78.4 18.7 %collective-permute-start.12 = (f32[256,768]{1,0:T(8,128)}, f32[256,768]{1,0:T(8,128)}, u32[]{:S(2)}, u32[]{:S(2)}) collective-permute-start(f32[256,768]{1,0:T(8,128)} %get-tuple-element.60), channel_id=1, source_target_pairs={{0,2},{1,3},{2,4},{3,5},{4,6},{5,7},{6,0},{7,1},{8,10},{9,11},{10,... | collective-permute-start | bytes 2359304 | tf_op jit(solution)/shard_map/a2_up/ppermute | solution.py:55
  85.0 30.8 %collective-permute-start.10 = (f32[256,640]{1,0:T(8,128)}, f32[256,640]{1,0:T(8,128)}, u32[]{:S(2)}, u32[]{:S(2)}) collective-permute-start(f32[256,640]{1,0:T(8,128)} %get-tuple-element.58), channel_id=1, source_target_pairs={{0,2},{1,3},{2,4},{3,5},{4,6},{5,7},{6,0},{7,1},{8,10},{9,11},{10,... | collective-permute-start | bytes 1966088 | tf_op jit(solution)/shard_map/outer0_up/ppermute | solution.py:55
  85.0 30.8 %collective-permute-start.11 = (f32[256,512]{1,0:T(8,128)}, f32[256,512]{1,0:T(8,128)S(1)}, u32[]{:S(2)}, u32[]{:S(2)}) collective-permute-start(f32[256,512]{1,0:T(8,128)} %get-tuple-element.59), channel_id=1, source_target_pairs={{0,6},{1,7},{2,0},{3,1},{4,2},{5,3},{6,4},{7,5},{8,14},{9,15},{10,... | collective-permute-start | bytes 1572872 | tf_op jit(solution)/shard_map/outer0_down/ppermute | solution.py:55
  105.5 22.4 %collective-permute-start.16 = (f32[256,768]{1,0:T(8,128)}, f32[256,768]{1,0:T(8,128)S(1)}, u32[]{:S(2)}, u32[]{:S(2)}) collective-permute-start(f32[256,768]{1,0:T(8,128)} %get-tuple-element.67), channel_id=1, source_target_pairs={{0,2},{1,3},{2,4},{3,5},{4,6},{5,7},{6,0},{7,1},{8,10},{9,11},{10,... | collective-permute-start | bytes 2359304 | tf_op jit(solution)/shard_map/b2_up/ppermute | solution.py:55
  105.5 23.8 %collective-permute-start.17 = (f32[256,768]{1,0:T(8,128)}, f32[256,768]{1,0:T(8,128)}, u32[]{:S(2)}, u32[]{:S(2)}) collective-permute-start(f32[256,768]{1,0:T(8,128)} %get-tuple-element.68), channel_id=1, source_target_pairs={{0,6},{1,7},{2,0},{3,1},{4,2},{5,3},{6,4},{7,5},{8,14},{9,15},{10,... | collective-permute-start | bytes 2359304 | tf_op jit(solution)/shard_map/b2_down/ppermute | solution.py:55
  121.1 20.8 %collective-permute-start.14 = (f32[256,640]{1,0:T(8,128)}, f32[256,640]{1,0:T(8,128)S(1)}, u32[]{:S(2)}, u32[]{:S(2)}) collective-permute-start(f32[256,640]{1,0:T(8,128)} %get-tuple-element.65), channel_id=1, source_target_pairs={{0,2},{1,3},{2,4},{3,5},{4,6},{5,7},{6,0},{7,1},{8,10},{9,11},{10,... | collective-permute-start | bytes 1966088 | tf_op jit(solution)/shard_map/outer1_up/ppermute | solution.py:55
  121.1 19.3 %collective-permute-start.15 = (f32[256,512]{1,0:T(8,128)}, f32[256,512]{1,0:T(8,128)S(1)}, u32[]{:S(2)}, u32[]{:S(2)}) collective-permute-start(f32[256,512]{1,0:T(8,128)} %get-tuple-element.66), channel_id=1, source_target_pairs={{0,6},{1,7},{2,0},{3,1},{4,2},{5,3},{6,4},{7,5},{8,14},{9,15},{10,... | collective-permute-start | bytes 1572872 | tf_op jit(solution)/shard_map/outer1_down/ppermute | solution.py:55
  123.8 25.4 %collective-permute-start.18 = (f32[256,896]{1,0:T(8,128)}, f32[256,896]{1,0:T(8,128)S(1)}, u32[]{:S(2)}, u32[]{:S(2)}) collective-permute-start(f32[256,896]{1,0:T(8,128)} %get-tuple-element.72), channel_id=1, source_target_pairs={{0,1},{1,0},{2,3},{3,2},{4,5},{5,4},{6,7},{7,6},{8,9},{9,8},{10,11... | collective-permute-start | bytes 2752520 | tf_op jit(solution)/shard_map/a_across/ppermute | solution.py:55
  132.3 29.6 %collective-permute-start.19 = (f32[256,768]{1,0:T(8,128)}, f32[256,768]{1,0:T(8,128)S(1)}, u32[]{:S(2)}, u32[]{:S(2)}) collective-permute-start(f32[256,768]{1,0:T(8,128)} %get-tuple-element.76), channel_id=1, source_target_pairs={{0,1},{1,0},{2,3},{3,2},{4,5},{5,4},{6,7},{7,6},{8,9},{9,8},{10,11... | collective-permute-start | bytes 2359304 | tf_op jit(solution)/shard_map/b_across/ppermute | solution.py:55
  146.5 15.4 %collective-permute-start.20 = (f32[256,640]{1,0:T(8,128)}, f32[256,640]{1,0:T(8,128)S(1)}, u32[]{:S(2)}, u32[]{:S(2)}) collective-permute-start(f32[256,640]{1,0:T(8,128)} %get-tuple-element.77), channel_id=1, source_target_pairs={{0,2},{1,3},{2,4},{3,5},{4,6},{5,7},{6,0},{7,1},{8,10},{9,11},{10,... | collective-permute-start | bytes 1966088 | tf_op jit(solution)/shard_map/outer2_up/ppermute | solution.py:55
  146.5 11.1 %collective-permute-start.21 = (f32[256,512]{1,0:T(8,128)}, f32[256,512]{1,0:T(8,128)S(1)}, u32[]{:S(2)}, u32[]{:S(2)}) collective-permute-start(f32[256,512]{1,0:T(8,128)} %get-tuple-element.78), channel_id=1, source_target_pairs={{0,6},{1,7},{2,0},{3,1},{4,2},{5,3},{6,4},{7,5},{8,14},{9,15},{10,... | collective-permute-start | bytes 1572872 | tf_op jit(solution)/shard_map/outer2_down/ppermute | solution.py:55
  157.6 4.3 %copy-start.10 = (f32[256,512]{1,0:T(8,128)}, f32[256,512]{1,0:T(8,128)S(1)}, u32[]{:S(2)}) copy-start(f32[256,512]{1,0:T(8,128)S(1)} %collective-permute-done.21.refs_12_) | copy-start | bytes 1572868
  171.2 4.2 %collective-permute-start.22 = (f32[176,128]{1,0:T(8,128)S(1)}, f32[176,128]{1,0:T(8,128)S(1)}, u32[]{:S(2)}, u32[]{:S(2)}) collective-permute-start(f32[176,128]{1,0:T(8,128)S(1)} %constant_dynamic-slice_fusion), channel_id=1, source_target_pairs={{0,8},{8,0},{16,24},{24,16},{32,40},{40,32},{48,56},{56,48},{64,72... | collective-permute-start | bytes 270344 | tf_op jit(solution)/shard_map/sum_core/ppermute | solution.py:55
  176.4 11.5 %copy-start.13 = (f32[176,128]{1,0:T(8,128)}, f32[176,128]{1,0:T(8,128)S(1)}, u32[]{:S(2)}) copy-start(f32[176,128]{1,0:T(8,128)S(1)} %dynamic-slice_add_fusion.refs_0_) | copy-start | bytes 270340
  176.4 11.5 %collective-permute-start.23 = (f32[176,128]{1,0:T(8,128)S(1)}, f32[176,128]{1,0:T(8,128)S(1)}, u32[]{:S(2)}, u32[]{:S(2)}) collective-permute-start(f32[176,128]{1,0:T(8,128)S(1)} %dynamic-slice_add_fusion.refs_0_), channel_id=1, source_target_pairs={{0,32},{8,40},{16,48},{24,56},{32,0},{40,8},{48,16},{56,24},{64,96... | collective-permute-start | bytes 270344 | tf_op jit(solution)/shard_map/sum_z2/ppermute | solution.py:55
  180.1 7.8 %collective-permute-start.24 = (f32[176,128]{1,0:T(8,128)S(1)}, f32[176,128]{1,0:T(8,128)S(1)}, u32[]{:S(2)}, u32[]{:S(2)}) collective-permute-start(f32[176,128]{1,0:T(8,128)S(1)} %dynamic-slice_add_fusion.refs_0_), channel_id=1, source_target_pairs={{0,16},{8,24},{16,32},{24,40},{32,48},{40,56},{48,0},{56,8},{64,80... | collective-permute-start | bytes 270344 | tf_op jit(solution)/shard_map/sum_z1/ppermute | solution.py:55
  180.8 7.1 %collective-permute-start.25 = (f32[176,128]{1,0:T(8,128)S(1)}, f32[176,128]{1,0:T(8,128)S(1)}, u32[]{:S(2)}, u32[]{:S(2)}) collective-permute-start(f32[176,128]{1,0:T(8,128)S(1)} %dynamic-slice_add_fusion.refs_0_), channel_id=1, source_target_pairs={{0,48},{8,56},{16,0},{24,8},{32,16},{40,24},{48,32},{56,40},{64,11... | collective-permute-start | bytes 270344 | tf_op jit(solution)/shard_map/sum_z3/ppermute | solution.py:55
  190.8 3.6 %collective-permute-start.26 = (f32[176,128]{1,0:T(8,128)}, f32[176,128]{1,0:T(8,128)S(1)}, u32[]{:S(2)}, u32[]{:S(2)}) collective-permute-start(f32[176,128]{1,0:T(8,128)} %sum_z.1), channel_id=1, source_target_pairs={{0,64},{8,72},{16,80},{24,88},{32,96},{40,104},{48,112},{56,120},{... | collective-permute-start | bytes 270344 | tf_op jit(solution)/shard_map/sum_y/ppermute | solution.py:55
  195.3 3.4 %copy-start.14 = (f32[176,128]{1,0:T(8,128)}, f32[176,128]{1,0:T(8,128)S(1)}, u32[]{:S(2)}) copy-start(f32[176,128]{1,0:T(8,128)S(1)} %add.25.mine) | copy-start | bytes 270340
  195.4 3.4 %collective-permute-start.27 = (f32[176,128]{1,0:T(8,128)S(1)}, f32[176,128]{1,0:T(8,128)S(1)}, u32[]{:S(2)}, u32[]{:S(2)}) collective-permute-start(f32[176,128]{1,0:T(8,128)S(1)} %add.25.mine), channel_id=1, source_target_pairs={{0,8},{8,0},{16,24},{24,16},{32,40},{40,32},{48,56},{56,48},{64,72... | collective-permute-start | bytes 270344 | tf_op jit(solution)/shard_map/gather_core/ppermute | solution.py:55
  (16 other events, 16.0 us)

commit v4 on v3

--- a/solution.py
+++ b/solution.py
@@ -244,14 +244,13 @@
     return jnp.concatenate([packed[:, :64], packed[:, 64:]], 0)
 
 
-def merge_kernel(groups, n_before, final, place, *refs):
+def merge_kernel(groups, n_before, place, *refs):
     refs = list(refs[n_before:])
-    table, coeffs, mark, merged = refs.pop(0), refs[-3], refs[-2], refs[-1]
+    table, (out, coeffs, mark, merged) = refs.pop(0), refs[-4:]
     row = 0
-    for g, (n_ins, cols, tiles, skips, plans) in enumerate(groups):
+    for n_ins, cols, tiles, skips, starts, plans in groups:
         momentum, grads, *ins = refs[: 2 + n_ins]
         del refs[: 2 + n_ins]
-        out = refs[len(refs) - 3 - len(groups) + g]
         for side, plan in enumerate(plans):
 
             @pl.when(place[1] == side)
@@ -266,19 +265,17 @@
         whole = BETA * momentum[...] + merged[pl.ds(skip, cols), :]
         chunks = forward_t(whole, table[...])
         coeffs[row : row + cols // 8, :] = pack(chunks)
-        if final:
-            at = 0
-            for back in backward_t(jnp.concatenate(chunks, 0), table[...]):
-                end = at + back.shape[0]
-                out[at:end, :] = whole[at:end] - back
-                at = end
-        else:
-            out[...] = whole
+        start = pl.multiple_of(starts[0] + (starts[1] - starts[0]) * place[1], 64)
+        at = 0
+        for back in backward_t(jnp.concatenate(chunks, 0), table[...]):
+            n = back.shape[0]
+            out[pl.ds(start + at, n), :] = whole[at : at + n] - back
+            at += n
         row += cols // 8
     mark[...] = jnp.zeros((8, LANES), F32)
 
 
-def merge_call(name, steps, before, momentum_t, table, row, groups, final=False):
+def merge_call(name, steps, before, momentum_t, table, row, groups):
     whole = lambda shape: pl.BlockSpec(shape, lambda i, _: (0, 0))
 
     def part(first, cols):
@@ -288,59 +285,42 @@
         return pl.BlockSpec((pl.Element(cols), pl.Element(ROWS)), rows)
 
     before = [*before, *steps.mark]
-    aliases = {1: len(groups)} if len(before) > len(steps.mark) else {}
+    aliases = {1: 0, 2: 1} if len(before) > len(steps.mark) else {}
     anywhere = [pl.BlockSpec(memory_space=pl.ANY) for _ in before]
+    least = tuple(min(group[1][side] for group in groups) for side in range(2))
     in_specs, ins, counts = [], [], []
     for piece, first, cols, plans, values in groups:
         in_specs += [part(first, cols), grads_block(ROWS, *piece), *[whole(v.shape) for v in values]]
         ins += [momentum_t, steps.grads, *values]
-        counts.append((len(values), cols, piece[3], cols < piece[3] * LANES, plans))
+        starts = (first[0] - least[0], first[1] - least[1])
+        counts.append((len(values), cols, piece[3], cols < piece[3] * LANES, starts, plans))
     rows = sum(group[2] for group in groups) // 8
     packed = pl.BlockSpec((pl.Element(rows), pl.Element(LANES)), lambda i, _: (row, 0))
-    shapes = [(group[2], ROWS) for group in groups]
     tiles = max(group[0][3] for group in groups)
     with jax.named_scope(name):
-        *wholes, coeffs, mark = pl.pallas_call(
-            functools.partial(merge_kernel, counts, len(before), final),
+        out, coeffs, mark = pl.pallas_call(
+            functools.partial(merge_kernel, counts, len(before)),
             grid_spec=pltpu.PrefetchScalarGridSpec(
                 num_scalar_prefetch=1,
                 grid=(1,),
                 in_specs=anywhere + [whole(table.shape)] + in_specs,
-                out_specs=[whole(shape) for shape in shapes] + [packed, whole((8, LANES))],
+                out_specs=[part(least, rows * 8), packed, whole((8, LANES))],
                 scratch_shapes=[pltpu.VMEM((tiles * LANES, ROWS), F32)],
             ),
             out_shape=[
                 jax.ShapeDtypeStruct(shape, F32)
-                for shape in [*shapes, (PACKED, LANES), (8, LANES)]
+                for shape in [(OWN_COLS, ROWS), (PACKED, LANES), (8, LANES)]
             ],
             input_output_aliases=aliases,
             compiler_params=pltpu.CompilerParams(vmem_limit_bytes=VMEM_BYTES),
             cost_estimate=pl.CostEstimate(flops=0, bytes_accessed=1, transcendentals=0),
         )(steps.place, *before, table, *ins)
     steps.mark = [mark]
-    return wholes, coeffs
+    return out, coeffs
 
 
 def groups_of(coeffs, groups):
     return [(g, unpack(coeffs[row : row + cols // 8, :])) for g, (_, row, cols) in enumerate(groups)]
-
-
-def new_kernel(groups, place, *refs):
-    *wholes, coeffs, table, out = refs
-    for side in range(2):
-
-        @pl.when(place[1] == side)
-        def _():
-            for g, chunks in groups_of(coeffs, groups):
-                to, n = groups[g][0][side], groups[g][2]
-                if g == 0:
-                    out[to : to + n, :] = wholes[0][...]
-                    continue
-                at = 0
-                for back in backward_t(chunks, table[...]):
-                    n = back.shape[0]
-                    out[to + at : to + at + n, :] = wholes[g][at : at + n, :] - back
-                    at += n
 
 
 def update_kernel(groups, place, mine, other, table, out, coeffs):
@@ -374,25 +354,6 @@
             compiler_params=pltpu.CompilerParams(vmem_limit_bytes=VMEM_BYTES),
             cost_estimate=pl.CostEstimate(flops=0, bytes_accessed=1, transcendentals=0),
         )(place, *ins)
-
-
-def total_kernel(n, *refs):
-    total = refs[0][...]
-    for ref in refs[1:n]:
-        total = total + ref[...]
-    refs[-1][...] = total
-
-
-def total_call(name, values, after):
-    whole = lambda a: pl.BlockSpec(a.shape, lambda: (0, 0))
-    with jax.named_scope(name):
-        return pl.pallas_call(
-            functools.partial(total_kernel, len(values)),
-            in_specs=[whole(v) for v in values] + [pl.BlockSpec(memory_space=pl.ANY) for _ in after],
-            out_specs=whole(values[0]),
-            out_shape=jax.ShapeDtypeStruct(values[0].shape, F32),
-            cost_estimate=pl.CostEstimate(flops=0, bytes_accessed=1, transcendentals=0),
-        )(*values, *after)
 
 
 def local(grads, momentum):
@@ -472,14 +433,13 @@
     wide = lambda n, *refs: [[(r, t) for r in refs] for t in range(n)]
     plan = [[(0, NB + t), (1, t) if t < NBP else (2, t - NBP)] for t in range(NB)]
     sides = (wide(NA, 0, 2) + [[(1, 0), (2, NA)]], wide(NA + 1, 1, 2))
-    (whole_a,), coeffs = merge_call(
+    new_t, coeffs = merge_call(
         "merge_a", steps, [], momentum_t, table, groups[0][1],
         [((0, 21 - NA, NA, NA + 1), groups[0][0], near, sides, [*a, ca])],
-        final=True,
     )
     sides = (wide(MIDDLE - NA, 0, 2), wide(MIDDLE - NA, 1, 2))
-    rest, coeffs = merge_call(
-        "merge_rest", steps, [coeffs], momentum_t, table, groups[1][1],
+    new_t, coeffs = merge_call(
+        "merge_rest", steps, [new_t, coeffs], momentum_t, table, groups[1][1],
         [
             ((0, NB, 22 + NA - NB, MIDDLE - NA), groups[1][0], far, sides, [*b, cb]),
             ((0, 0, SUPER - NB, NB), groups[2][0], NB * LANES, (plan, plan), [y23, *o]),
@@ -489,11 +449,7 @@
     part = lambda c: lax.dynamic_slice(coeffs, (c * half, 0), (half, LANES))
     mine = part(core) + send("sum_core", part(1 - core), "rep", CORE_FLIP)
     came = [send(f"sum_z{k}", mine, "rep", z_shift(k)) for k in (2, 1, 3)]
-    new_t = output_call(
-        "new_momentum", functools.partial(new_kernel, groups), place,
-        [whole_a, *rest, coeffs, table], [],
-    )
-    mine = total_call("sum_z", [mine, *came], [new_t])
+    mine = mine + came[0] + came[1] + came[2]
     mine = mine + send("sum_y", mine, "rep", YLO_FLIP)
     other = send("gather_core", mine, "rep", CORE_FLIP)
     update_t = output_call(

time: 205 us -> 202 us (0.985)
  waiting for transfers between devices: 79.7 us -> 85.3 us
  Pallas kernels: 65.2 us -> 59.9 us
    ppermute x28, waiting for transfers between devices: 79.7 us -> 85.3 us  [send(): return lax.ppermute(value, axes, pairs)]
    pallas_call x2 -> x1, Pallas kernels: 9.69 us -> 4.59 us  [output_call(): pl.pallas_call(kernel, grid_spec=pltpu.PrefetchScalarGridSpec(num_scalar_...]
    unnamed x40 -> x32, local copies, waits for them, and re-layouts: 10.1 us -> 8.95 us
    pallas_call x3 -> x2, Pallas kernels: 14.3 us -> 14.1 us  [merge_call(): pl.pallas_call(functools.partial(merge_kernel, counts, len(before)), grid...]
  transfers between devices with their start and end apart: 28 -> 28, of which waited for: 18 -> 20; matrix products, arithmetic and copies ran while one was open for 0% -> 0% of each run, Pallas kernels for 23% -> 21%
where the time goes in v4:
time: 202 us; the launch traced here: 201 us
  waiting for transfers between devices  85.3 us (42%)
  Pallas kernels  59.9 us (30%)
  starting transfers between devices  43.5 us (22%)
  local copies, waits for them, and re-layouts  9.84 us (5%)
    ppermute x28, waiting for transfers between devices, send(): return lax.ppermute(value, axes, pairs)  85.3 us
    ppermute x28, starting transfers between devices, send(): return lax.ppermute(value, axes, pairs)  43.5 us
    pallas_call x12, Pallas kernels, __call__(): pl.pallas_call(functools.partial(step_kernel, body, len(slices) + len(ins...  41.1 us
    pallas_call x2, Pallas kernels, merge_call(): pl.pallas_call(functools.partial(merge_kernel, counts, len(before)), grid...  14.1 us
    unnamed x32, local copies, waits for them, and re-layouts  8.95 us
    pallas_call x1, Pallas kernels, output_call(): pl.pallas_call(kernel, grid_spec=pltpu.PrefetchScalarGridSpec(num_scalar_...  4.59 us
  transfers between devices with their start and end apart: 28, of which 20 were waited for; matrix products, arithmetic and copies ran while one was open for 0% of the time, Pallas kernels for 21%

profile of v4, /device:TPU:1, one launch (start us, length us, event | category | flops | bytes accessed | tf_op | source)
XLA Modules:
  0.0 200.9 jit_solution(13125308783400425736)
XLA Ops:
  1.3 3.7 %read_first.1 = (f32[256,768]{1,0:T(8,128)}, f32[256,896]{1,0:T(8,128)}, f32[256,768]{1,0:T(8,128)}, f32[256,768]{1,0:T(8,128)}, f32[8,128]{1,0:T(8,128)}) custom-call(s32[4]{0:T(128)} %pad_add_fusion.place, bf16[256,22016]{1,0:T(8,128)(2,1)} %bitcast.12, bf16[256,22016]{1,0:T(8,128)(2,1)} %bitcast.13, bf16[256,22016]{1,0:T(8,128)(2,1)} %bitcast.14, ...), custom_call_target="tpu_custom_call" | custom-call | bytes 1 | tf_op jit(solution)/shard_map/read_first/pallas_call | solution.py:157
  5.0 3.3 %collective-permute-start.3 = (f32[256,896]{1,0:T(8,128)}, f32[256,896]{1,0:T(8,128)S(1)}, u32[]{:S(2)}, u32[]{:S(2)}) collective-permute-start(f32[256,896]{1,0:T(8,128)} %get-tuple-element.46), channel_id=1, source_target_pairs={{0,6},{1,7},{2,0},{3,1},{4,2},{5,3},{6,4},{7,5},{8,14},{9,15},{10,... | collective-permute-start | bytes 2752520 | tf_op jit(solution)/shard_map/a0_down/ppermute | solution.py:55
  8.3 3.4 %read_cross01.1 = (f32[256,2304]{1,0:T(8,128)}, f32[8,128]{1,0:T(8,128)}) custom-call(s32[4]{0:T(128)} %pad_add_fusion.place, bf16[256,22016]{1,0:T(8,128)(2,1)} %bitcast.16, bf16[256,22016]{1,0:T(8,128)(2,1)} %bitcast.17, bf16[256,22016]{1,0:T(8,128)(2,1)} %bitcast.18, bf16[256,22016]{1,0:T(8,128)(2,1)} %bitcast.19, f32[8,128]{1,0:T(8,128)} %get-tuple-element.41.refs_4_), custom_call_target="tpu_custom_call" | custom-call | bytes 1 | tf_op jit(solution)/shard_map/read_cross01/pallas_call | solution.py:157
  11.8 2.9 %collective-permute-start.1 = (f32[256,2304]{1,0:T(8,128)}, f32[256,2304]{1,0:T(8,128)}, u32[]{:S(2)}, u32[]{:S(2)}) collective-permute-start(f32[256,2304]{1,0:T(8,128)} %get-tuple-element.44), channel_id=1, source_target_pairs={{0,1},{1,0},{2,3},{3,2},{4,5},{5,4},{6,7},{7,6},{8,9},{9,8},{10,11... | collective-permute-start | bytes 7077896 | tf_op jit(solution)/shard_map/cross01_across/ppermute | solution.py:55
  17.4 3.3 %read_cross23.1 = (f32[256,2304]{1,0:T(8,128)}, f32[8,128]{1,0:T(8,128)}) custom-call(s32[4]{0:T(128)} %pad_add_fusion.place, bf16[256,22016]{1,0:T(8,128)(2,1)} %bitcast.20, bf16[256,22016]{1,0:T(8,128)(2,1)} %bitcast.21, bf16[256,22016]{1,0:T(8,128)(2,1)} %bitcast.22, bf16[256,22016]{1,0:T(8,128)(2,1)} %bitcast.23, f32[8,128]{1,0:T(8,128)} %get-tuple-element.42.refs_4_), custom_call_target="tpu_custom_call" | custom-call | bytes 1 | tf_op jit(solution)/shard_map/read_cross23/pallas_call | solution.py:157
  20.7 7.3 %collective-permute-done.2.refs_2_ = f32[256,768]{1,0:T(8,128)S(1)} collective-permute-done((f32[256,768]{1,0:T(8,128)}, f32[256,768]{1,0:T(8,128)S(1)}, u32[]{:S(2)}, u32[]{:S(2)}) %collective-permute-start.2) | collective-permute-done | bytes 786464 | tf_op jit(solution)/shard_map/a0_up/ppermute | solution.py:55
  32.6 3.4 %add_a1.1 = (f32[256,768]{1,0:T(8,128)}, f32[256,896]{1,0:T(8,128)}, f32[8,128]{1,0:T(8,128)}) custom-call(s32[4]{0:T(128)} %pad_add_fusion.place, bf16[256,22016]{1,0:T(8,128)(2,1)} %bitcast.24, bf16[256,22016]{1,0:T(8,128)(2,1)} %bitcast.25, f32[256,768]{1,0:T(8,128)} %copy-done.6, f32[256,896]{1,0:T(8,128)} %copy-done.4, f32[8,128]{1,0:T(8,128)} %get-tuple-element.47.refs_4_), custom_call_target="tpu_custom_call" | custom-call | bytes 1 | tf_op jit(solution)/shard_map/add_a1/pallas_call | solution.py:157
  36.1 8.7 %collective-permute-done.6.refs_2_ = f32[256,768]{1,0:T(8,128)} collective-permute-done((f32[256,768]{1,0:T(8,128)}, f32[256,768]{1,0:T(8,128)}, u32[]{:S(2)}, u32[]{:S(2)}) %collective-permute-start.6) | collective-permute-done | bytes 786464 | tf_op jit(solution)/shard_map/b0_up/ppermute | solution.py:55
  44.8 3.4 %add_b1.1 = (f32[256,768]{1,0:T(8,128)}, f32[256,768]{1,0:T(8,128)}, f32[8,128]{1,0:T(8,128)}) custom-call(s32[4]{0:T(128)} %pad_add_fusion.place, bf16[256,22016]{1,0:T(8,128)(2,1)} %bitcast.27, bf16[256,22016]{1,0:T(8,128)(2,1)} %bitcast.26, f32[256,768]{1,0:T(8,128)} %collective-permute-done.6.refs_2_, f32[256,768]{1,0:T(8,128)} %collective-permute-done.7.refs_3_, ...), custom_call_target="tpu_custom_call" | custom-call | bytes 1 | tf_op jit(solution)/shard_map/add_b1/pallas_call | solution.py:157
  49.6 12.0 %collective-permute-done.4.refs_2_ = f32[256,768]{1,0:T(8,128)} collective-permute-done((f32[256,768]{1,0:T(8,128)}, f32[256,768]{1,0:T(8,128)}, u32[]{:S(2)}, u32[]{:S(2)}) %collective-permute-start.4) | collective-permute-done | bytes 786464 | tf_op jit(solution)/shard_map/a1_up/ppermute | solution.py:55
  64.6 3.5 %add_a2.1 = (f32[256,768]{1,0:T(8,128)}, f32[256,896]{1,0:T(8,128)}, f32[8,128]{1,0:T(8,128)}) custom-call(s32[4]{0:T(128)} %pad_add_fusion.place, bf16[256,22016]{1,0:T(8,128)(2,1)} %bitcast.28, bf16[256,22016]{1,0:T(8,128)(2,1)} %bitcast.29, f32[256,768]{1,0:T(8,128)} %collective-permute-done.4.refs_2_, f32[256,896]{1,0:T(8,128)} %copy-done.5, ...), custom_call_target="tpu_custom_call" | custom-call | bytes 1 | tf_op jit(solution)/shard_map/add_a2/pallas_call | solution.py:157
  69.6 8.8 %collective-permute-done.8.refs_4_.refs_2_ = f32[256,768]{1,0:T(8,128)} collective-permute-done((f32[256,768]{1,0:T(8,128)}, f32[256,768]{1,0:T(8,128)}, u32[]{:S(2)}, u32[]{:S(2)}) %collective-permute-start.8) | collective-permute-done | bytes 786464 | tf_op jit(solution)/shard_map/b1_up/ppermute | solution.py:55
  78.5 3.1 %collective-permute-done.9.refs_5_.refs_3_ = f32[256,768]{1,0:T(8,128)} collective-permute-done((f32[256,768]{1,0:T(8,128)}, f32[256,768]{1,0:T(8,128)}, u32[]{:S(2)}, u32[]{:S(2)}) %collective-permute-start.9) | collective-permute-done | bytes 786464 | tf_op jit(solution)/shard_map/b1_down/ppermute | solution.py:55
  81.6 3.4 %add_outer0.1 = (f32[256,640]{1,0:T(8,128)}, f32[256,512]{1,0:T(8,128)}, f32[8,128]{1,0:T(8,128)}) custom-call(s32[4]{0:T(128)} %pad_add_fusion.place, bf16[256,22016]{1,0:T(8,128)(2,1)} %bitcast.30, bf16[256,22016]{1,0:T(8,128)(2,1)} %bitcast.31, f32[256,2304]{1,0:T(8,128)} %collective-permute-done.1.refs_2_, f32[8,128]{1,0:T(8,128)} %get-tuple-element.54.refs_3_, ...), custom_call_target="tpu_custom_call" | custom-call | bytes 1 | tf_op jit(solution)/shard_map/add_outer0/pallas_call | solution.py:157
  87.7 9.5 %collective-permute-done.12.refs_5_.refs_1_.refs_4_ = f32[256,768]{1,0:T(8,128)} collective-permute-done((f32[256,768]{1,0:T(8,128)}, f32[256,768]{1,0:T(8,128)}, u32[]{:S(2)}, u32[]{:S(2)}) %collective-permute-start.12) | collective-permute-done | bytes 786464 | tf_op jit(solution)/shard_map/a2_up/ppermute | solution.py:55
  97.2 4.1 %collective-permute-done.13.refs_6_.refs_2_.refs_5_ = f32[256,896]{1,0:T(8,128)S(1)} collective-permute-done((f32[256,896]{1,0:T(8,128)}, f32[256,896]{1,0:T(8,128)S(1)}, u32[]{:S(2)}, u32[]{:S(2)}) %collective-permute-start.13) | collective-permute-done | bytes 917536 | tf_op jit(solution)/shard_map/a2_down/ppermute | solution.py:55
  102.2 3.4 %add_b2.1 = (f32[256,768]{1,0:T(8,128)}, f32[256,768]{1,0:T(8,128)}, f32[8,128]{1,0:T(8,128)}) custom-call(s32[4]{0:T(128)} %pad_add_fusion.place, bf16[256,22016]{1,0:T(8,128)(2,1)} %bitcast.32, bf16[256,22016]{1,0:T(8,128)(2,1)} %bitcast.33, f32[256,768]{1,0:T(8,128)} %collective-permute-done.8.refs_4_.refs_2_, ...), custom_call_target="tpu_custom_call" | custom-call | bytes 1 | tf_op jit(solution)/shard_map/add_b2/pallas_call | solution.py:157
  108.3 3.1 %mix_a.1 = (f32[256,896]{1,0:T(8,128)}, f32[8,128]{1,0:T(8,128)}) custom-call(s32[4]{0:T(128)} %pad_add_fusion.place, bf16[256,22016]{1,0:T(8,128)(2,1)} %bitcast.34, f32[256,768]{1,0:T(8,128)} %collective-permute-done.12.refs_5_.refs_1_.refs_4_, f32[256,896]{1,0:T(8,128)} %copy-done.1, f32[8,128]{1,0:T(8,128)} %get-tuple-element.62.refs_3_), custom_call_target="tpu_custom_call" | custom-call | bytes 1 | tf_op jit(solution)/shard_map/mix_a/pallas_call | solution.py:157
  111.4 4.5 %collective-permute-done.refs_6_.refs_2_.refs_11_ = f32[256,2304]{1,0:T(8,128)S(1)} collective-permute-done((f32[256,2304]{1,0:T(8,128)}, f32[256,2304]{1,0:T(8,128)S(1)}, u32[]{:S(2)}, u32[]{:S(2)}) %collective-permute-start) | collective-permute-done | bytes 2359328 | tf_op jit(solution)/shard_map/cross23_across/ppermute | solution.py:55
  117.4 3.8 %add_outer1.1 = (f32[256,640]{1,0:T(8,128)}, f32[256,512]{1,0:T(8,128)}, f32[8,128]{1,0:T(8,128)}) custom-call(s32[4]{0:T(128)} %pad_add_fusion.place, bf16[256,22016]{1,0:T(8,128)(2,1)} %bitcast.35, bf16[256,22016]{1,0:T(8,128)(2,1)} %bitcast.36, f32[256,2304]{1,0:T(8,128)} %collective-permute-done.1.refs_2_, f32[256,640]{1,0:T(8,128)} %collective-permute-done.10.refs_3_, ...), custom_call_target="tpu_custom_call" | custom-call | bytes 1 | tf_op jit(solution)/shard_map/add_outer1/pallas_call | solution.py:157
  123.9 3.0 %collective-permute-start.18 = (f32[256,896]{1,0:T(8,128)}, f32[256,896]{1,0:T(8,128)S(1)}, u32[]{:S(2)}, u32[]{:S(2)}) collective-permute-start(f32[256,896]{1,0:T(8,128)} %get-tuple-element.71), channel_id=1, source_target_pairs={{0,1},{1,0},{2,3},{3,2},{4,5},{5,4},{6,7},{7,6},{8,9},{9,8},{10,11... | collective-permute-start | bytes 2752520 | tf_op jit(solution)/shard_map/a_across/ppermute | solution.py:55
  129.3 3.0 %mix_b.1 = (f32[256,768]{1,0:T(8,128)}, f32[8,128]{1,0:T(8,128)}) custom-call(s32[4]{0:T(128)} %pad_add_fusion.place, bf16[256,22016]{1,0:T(8,128)(2,1)} %bitcast.37, f32[256,768]{1,0:T(8,128)} %copy-done.2, f32[256,768]{1,0:T(8,128)} %collective-permute-done.17.refs_2_.refs_7_, f32[8,128]{1,0:T(8,128)} %get-tuple-element.68.refs_3_), custom_call_target="tpu_custom_call" | custom-call | bytes 1 | tf_op jit(solution)/shard_map/mix_b/pallas_call | solution.py:157
  132.3 2.9 %collective-permute-start.19 = (f32[256,768]{1,0:T(8,128)}, f32[256,768]{1,0:T(8,128)S(1)}, u32[]{:S(2)}, u32[]{:S(2)}) collective-permute-start(f32[256,768]{1,0:T(8,128)} %get-tuple-element.75), channel_id=1, source_target_pairs={{0,1},{1,0},{2,3},{3,2},{4,5},{5,4},{6,7},{7,6},{8,9},{9,8},{10,11... | collective-permute-start | bytes 2359304 | tf_op jit(solution)/shard_map/b_across/ppermute | solution.py:55
  135.2 5.2 %collective-permute-done.15.refs_4_ = f32[256,512]{1,0:T(8,128)S(1)} collective-permute-done((f32[256,512]{1,0:T(8,128)}, f32[256,512]{1,0:T(8,128)S(1)}, u32[]{:S(2)}, u32[]{:S(2)}) %collective-permute-start.15) | collective-permute-done | bytes 524320 | tf_op jit(solution)/shard_map/outer1_down/ppermute | solution.py:55
  142.8 3.8 %add_outer2.1 = (f32[256,640]{1,0:T(8,128)}, f32[256,512]{1,0:T(8,128)}, f32[8,128]{1,0:T(8,128)}) custom-call(s32[4]{0:T(128)} %pad_add_fusion.place, bf16[256,22016]{1,0:T(8,128)(2,1)} %bitcast.38, bf16[256,22016]{1,0:T(8,128)(2,1)} %bitcast.39, f32[256,2304]{1,0:T(8,128)} %copy-done, f32[256,640]{1,0:T(8,128)} %copy-done.8, f32[256,512]{1,0:T(8,128)} %copy-done.12, ...), custom_call_target="tpu_custom_call" | custom-call | bytes 1 | tf_op jit(solution)/shard_map/add_outer2/pallas_call | solution.py:157
  150.1 5.3 %merge_a.1 = (f32[2752,256]{1,0:T(8,128)}, f32[352,128]{1,0:T(8,128)}, f32[8,128]{1,0:T(8,128)}) custom-call(s32[4]{0:T(128)} %pad_add_fusion.place, f32[8,128]{1,0:T(8,128)} %get-tuple-element.70.refs_0_, bf16[384,256]{1,0:T(8,128)(2,1)} %constant.45.clone.refs_1_.refs_3_.table, f32[2752,256]{1,0:T(8,128)} %bitcast.43, bf16[256,22016]{1,0:T(8,128)(2,1)} %bitcast.40, ...), custom_call_target="tpu_custom_call" | custom-call | bytes 1 | tf_op jit(solution)/shard_map/merge_a/pallas_call | solution.py:301
  157.6 4.4 %collective-permute-done.19.refs_8_ = f32[256,768]{1,0:T(8,128)S(1)} collective-permute-done((f32[256,768]{1,0:T(8,128)}, f32[256,768]{1,0:T(8,128)S(1)}, u32[]{:S(2)}, u32[]{:S(2)}) %collective-permute-start.19) | collective-permute-done | bytes 786464 | tf_op jit(solution)/shard_map/b_across/ppermute | solution.py:55
  163.1 8.8 %merge_rest.1 = (f32[2752,256]{1,0:T(8,128)}, f32[352,128]{1,0:T(8,128)}, f32[8,128]{1,0:T(8,128)}) custom-call(s32[4]{0:T(128)} %pad_add_fusion.place, f32[2752,256]{1,0:T(8,128)} %get-tuple-element.72.refs_0_, f32[352,128]{1,0:T(8,128)} %get-tuple-element.73.refs_1_, ...), custom_call_target="tpu_custom_call", output_to_operand_aliasing={{0}: (1, {}), {1}: (2, {})} | custom-call | bytes 1 | tf_op jit(solution)/shard_map/merge_rest/pallas_call | solution.py:301
  172.8 3.3 %collective-permute-start.22 = (f32[176,128]{1,0:T(8,128)S(1)}, f32[176,128]{1,0:T(8,128)S(1)}, u32[]{:S(2)}, u32[]{:S(2)}) collective-permute-start(f32[176,128]{1,0:T(8,128)S(1)} %constant_dynamic-slice_fusion), channel_id=1, source_target_pairs={{0,8},{8,0},{16,24},{24,16},{32,40},{40,32},{48,56},{56,48},{64,72... | collective-permute-start | bytes 270344 | tf_op jit(solution)/shard_map/sum_core/ppermute | solution.py:55
  178.0 3.8 %collective-permute-start.25 = (f32[176,128]{1,0:T(8,128)S(1)}, f32[176,128]{1,0:T(8,128)S(1)}, u32[]{:S(2)}, u32[]{:S(2)}) collective-permute-start(f32[176,128]{1,0:T(8,128)S(1)} %dynamic-slice_add_fusion), channel_id=1, source_target_pairs={{0,48},{8,56},{16,0},{24,8},{32,16},{40,24},{48,32},{56,40},{64,11... | collective-permute-start | bytes 270344 | tf_op jit(solution)/shard_map/sum_z3/ppermute | solution.py:55
  183.3 5.5 %collective-permute-done.24 = f32[176,128]{1,0:T(8,128)S(1)} collective-permute-done((f32[176,128]{1,0:T(8,128)S(1)}, f32[176,128]{1,0:T(8,128)S(1)}, u32[]{:S(2)}, u32[]{:S(2)}) %collective-permute-start.24) | collective-permute-done | bytes 90144 | tf_op jit(solution)/shard_map/sum_z1/ppermute | solution.py:55
  196.3 4.6 %update.1 = f32[2752,256]{1,0:T(8,128)} custom-call(s32[4]{0:T(128)} %pad_add_fusion.place, f32[176,128]{1,0:T(8,128)} %copy-done.13, f32[176,128]{1,0:T(8,128)} %copy-done.14, bf16[384,256]{1,0:T(8,128)(2,1)} %constant.45.clone.refs_1_.refs_3_.table), custom_call_target="tpu_custom_call" | custom-call | bytes 1 | tf_op jit(solution)/shard_map/update/pallas_call | solution.py:344
  (76 shorter events, 47.9 us)
Async XLA Ops:
  5.0 26.7 %collective-permute-start.3 = (f32[256,896]{1,0:T(8,128)}, f32[256,896]{1,0:T(8,128)S(1)}, u32[]{:S(2)}, u32[]{:S(2)}) collective-permute-start(f32[256,896]{1,0:T(8,128)} %get-tuple-element.46), channel_id=1, source_target_pairs={{0,6},{1,7},{2,0},{3,1},{4,2},{5,3},{6,4},{7,5},{8,14},{9,15},{10,... | collective-permute-start | bytes 2752520 | tf_op jit(solution)/shard_map/a0_down/ppermute | solution.py:55
  8.3 19.6 %collective-permute-start.2 = (f32[256,768]{1,0:T(8,128)}, f32[256,768]{1,0:T(8,128)S(1)}, u32[]{:S(2)}, u32[]{:S(2)}) collective-permute-start(f32[256,768]{1,0:T(8,128)} %get-tuple-element.45), channel_id=1, source_target_pairs={{0,2},{1,3},{2,4},{3,5},{4,6},{5,7},{6,0},{7,1},{8,10},{9,11},{10,... | collective-permute-start | bytes 2359304 | tf_op jit(solution)/shard_map/a0_up/ppermute | solution.py:55
  8.3 6.6 %copy-start.15 = (f32[256,768]{1,0:T(8,128)S(1)}, f32[256,768]{1,0:T(8,128)}, u32[]{:S(2)}) copy-start(f32[256,768]{1,0:T(8,128)} %get-tuple-element.51) | copy-start | bytes 2359300
  11.8 69.8 %collective-permute-start.1 = (f32[256,2304]{1,0:T(8,128)}, f32[256,2304]{1,0:T(8,128)}, u32[]{:S(2)}, u32[]{:S(2)}) collective-permute-start(f32[256,2304]{1,0:T(8,128)} %get-tuple-element.44), channel_id=1, source_target_pairs={{0,1},{1,0},{2,3},{3,2},{4,5},{5,4},{6,7},{7,6},{8,9},{9,8},{10,11... | collective-permute-start | bytes 7077896 | tf_op jit(solution)/shard_map/cross01_across/ppermute | solution.py:55
  14.7 30.1 %collective-permute-start.6 = (f32[256,768]{1,0:T(8,128)}, f32[256,768]{1,0:T(8,128)}, u32[]{:S(2)}, u32[]{:S(2)}) collective-permute-start(f32[256,768]{1,0:T(8,128)} %get-tuple-element.50), channel_id=1, source_target_pairs={{0,2},{1,3},{2,4},{3,5},{4,6},{5,7},{6,0},{7,1},{8,10},{9,11},{10,... | collective-permute-start | bytes 2359304 | tf_op jit(solution)/shard_map/b0_up/ppermute | solution.py:55
  14.9 29.9 %collective-permute-start.7 = (f32[256,768]{1,0:T(8,128)S(1)}, f32[256,768]{1,0:T(8,128)}, u32[]{:S(2)}, u32[]{:S(2)}) collective-permute-start(f32[256,768]{1,0:T(8,128)S(1)} %copy-done.15), channel_id=1, source_target_pairs={{0,6},{1,7},{2,0},{3,1},{4,2},{5,3},{6,4},{7,5},{8,14},{9,15},{10,... | collective-permute-start | bytes 2359304 | tf_op jit(solution)/shard_map/b0_down/ppermute | solution.py:55
  28.9 87.0 %collective-permute-start = (f32[256,2304]{1,0:T(8,128)}, f32[256,2304]{1,0:T(8,128)S(1)}, u32[]{:S(2)}, u32[]{:S(2)}) collective-permute-start(f32[256,2304]{1,0:T(8,128)} %get-tuple-element.43), channel_id=1, source_target_pairs={{0,1},{1,0},{2,3},{3,2},{4,5},{5,4},{6,7},{7,6},{8,9},{9,8},{10,11... | collective-permute-start | bytes 7077896 | tf_op jit(solution)/shard_map/cross23_across/ppermute | solution.py:55
  36.1 25.6 %collective-permute-start.4 = (f32[256,768]{1,0:T(8,128)}, f32[256,768]{1,0:T(8,128)}, u32[]{:S(2)}, u32[]{:S(2)}) collective-permute-start(f32[256,768]{1,0:T(8,128)} %get-tuple-element.48), channel_id=1, source_target_pairs={{0,2},{1,3},{2,4},{3,5},{4,6},{5,7},{6,0},{7,1},{8,10},{9,11},{10,... | collective-permute-start | bytes 2359304 | tf_op jit(solution)/shard_map/a1_up/ppermute | solution.py:55
  44.8 18.8 %collective-permute-start.5 = (f32[256,896]{1,0:T(8,128)}, f32[256,896]{1,0:T(8,128)S(1)}, u32[]{:S(2)}, u32[]{:S(2)}) collective-permute-start(f32[256,896]{1,0:T(8,128)} %get-tuple-element.49), channel_id=1, source_target_pairs={{0,6},{1,7},{2,0},{3,1},{4,2},{5,3},{6,4},{7,5},{8,14},{9,15},{10,... | collective-permute-start | bytes 2752520 | tf_op jit(solution)/shard_map/a1_down/ppermute | solution.py:55
  48.2 30.3 %collective-permute-start.8 = (f32[256,768]{1,0:T(8,128)}, f32[256,768]{1,0:T(8,128)}, u32[]{:S(2)}, u32[]{:S(2)}) collective-permute-start(f32[256,768]{1,0:T(8,128)} %get-tuple-element.55), channel_id=1, source_target_pairs={{0,2},{1,3},{2,4},{3,5},{4,6},{5,7},{6,0},{7,1},{8,10},{9,11},{10,... | collective-permute-start | bytes 2359304 | tf_op jit(solution)/shard_map/b1_up/ppermute | solution.py:55
  61.6 19.9 %collective-permute-start.9 = (f32[256,768]{1,0:T(8,128)}, f32[256,768]{1,0:T(8,128)}, u32[]{:S(2)}, u32[]{:S(2)}) collective-permute-start(f32[256,768]{1,0:T(8,128)} %get-tuple-element.56), channel_id=1, source_target_pairs={{0,6},{1,7},{2,0},{3,1},{4,2},{5,3},{6,4},{7,5},{8,14},{9,15},{10,... | collective-permute-start | bytes 2359304 | tf_op jit(solution)/shard_map/b1_down/ppermute | solution.py:55
  68.1 33.2 %collective-permute-start.13 = (f32[256,896]{1,0:T(8,128)}, f32[256,896]{1,0:T(8,128)S(1)}, u32[]{:S(2)}, u32[]{:S(2)}) collective-permute-start(f32[256,896]{1,0:T(8,128)} %get-tuple-element.60), channel_id=1, source_target_pairs={{0,6},{1,7},{2,0},{3,1},{4,2},{5,3},{6,4},{7,5},{8,14},{9,15},{10,... | collective-permute-start | bytes 2752520 | tf_op jit(solution)/shard_map/a2_down/ppermute | solution.py:55
  78.5 18.7 %collective-permute-start.12 = (f32[256,768]{1,0:T(8,128)}, f32[256,768]{1,0:T(8,128)}, u32[]{:S(2)}, u32[]{:S(2)}) collective-permute-start(f32[256,768]{1,0:T(8,128)} %get-tuple-element.59), channel_id=1, source_target_pairs={{0,2},{1,3},{2,4},{3,5},{4,6},{5,7},{6,0},{7,1},{8,10},{9,11},{10,... | collective-permute-start | bytes 2359304 | tf_op jit(solution)/shard_map/a2_up/ppermute | solution.py:55
  85.0 30.8 %collective-permute-start.10 = (f32[256,640]{1,0:T(8,128)}, f32[256,640]{1,0:T(8,128)}, u32[]{:S(2)}, u32[]{:S(2)}) collective-permute-start(f32[256,640]{1,0:T(8,128)} %get-tuple-element.57), channel_id=1, source_target_pairs={{0,2},{1,3},{2,4},{3,5},{4,6},{5,7},{6,0},{7,1},{8,10},{9,11},{10,... | collective-permute-start | bytes 1966088 | tf_op jit(solution)/shard_map/outer0_up/ppermute | solution.py:55
  85.0 30.8 %collective-permute-start.11 = (f32[256,512]{1,0:T(8,128)}, f32[256,512]{1,0:T(8,128)S(1)}, u32[]{:S(2)}, u32[]{:S(2)}) collective-permute-start(f32[256,512]{1,0:T(8,128)} %get-tuple-element.58), channel_id=1, source_target_pairs={{0,6},{1,7},{2,0},{3,1},{4,2},{5,3},{6,4},{7,5},{8,14},{9,15},{10,... | collective-permute-start | bytes 1572872 | tf_op jit(solution)/shard_map/outer0_down/ppermute | solution.py:55
  105.6 22.3 %collective-permute-start.16 = (f32[256,768]{1,0:T(8,128)}, f32[256,768]{1,0:T(8,128)S(1)}, u32[]{:S(2)}, u32[]{:S(2)}) collective-permute-start(f32[256,768]{1,0:T(8,128)} %get-tuple-element.66), channel_id=1, source_target_pairs={{0,2},{1,3},{2,4},{3,5},{4,6},{5,7},{6,0},{7,1},{8,10},{9,11},{10,... | collective-permute-start | bytes 2359304 | tf_op jit(solution)/shard_map/b2_up/ppermute | solution.py:55
  105.6 23.7 %collective-permute-start.17 = (f32[256,768]{1,0:T(8,128)}, f32[256,768]{1,0:T(8,128)}, u32[]{:S(2)}, u32[]{:S(2)}) collective-permute-start(f32[256,768]{1,0:T(8,128)} %get-tuple-element.67), channel_id=1, source_target_pairs={{0,6},{1,7},{2,0},{3,1},{4,2},{5,3},{6,4},{7,5},{8,14},{9,15},{10,... | collective-permute-start | bytes 2359304 | tf_op jit(solution)/shard_map/b2_down/ppermute | solution.py:55
  115.8 1.6 copy-start.11
  121.2 20.7 %collective-permute-start.14 = (f32[256,640]{1,0:T(8,128)}, f32[256,640]{1,0:T(8,128)S(1)}, u32[]{:S(2)}, u32[]{:S(2)}) collective-permute-start(f32[256,640]{1,0:T(8,128)} %get-tuple-element.64), channel_id=1, source_target_pairs={{0,2},{1,3},{2,4},{3,5},{4,6},{5,7},{6,0},{7,1},{8,10},{9,11},{10,... | collective-permute-start | bytes 1966088 | tf_op jit(solution)/shard_map/outer1_up/ppermute | solution.py:55
  121.2 19.3 %collective-permute-start.15 = (f32[256,512]{1,0:T(8,128)}, f32[256,512]{1,0:T(8,128)S(1)}, u32[]{:S(2)}, u32[]{:S(2)}) collective-permute-start(f32[256,512]{1,0:T(8,128)} %get-tuple-element.65), channel_id=1, source_target_pairs={{0,6},{1,7},{2,0},{3,1},{4,2},{5,3},{6,4},{7,5},{8,14},{9,15},{10,... | collective-permute-start | bytes 1572872 | tf_op jit(solution)/shard_map/outer1_down/ppermute | solution.py:55
  123.9 25.3 %collective-permute-start.18 = (f32[256,896]{1,0:T(8,128)}, f32[256,896]{1,0:T(8,128)S(1)}, u32[]{:S(2)}, u32[]{:S(2)}) collective-permute-start(f32[256,896]{1,0:T(8,128)} %get-tuple-element.71), channel_id=1, source_target_pairs={{0,1},{1,0},{2,3},{3,2},{4,5},{5,4},{6,7},{7,6},{8,9},{9,8},{10,11... | collective-permute-start | bytes 2752520 | tf_op jit(solution)/shard_map/a_across/ppermute | solution.py:55
  132.3 29.6 %collective-permute-start.19 = (f32[256,768]{1,0:T(8,128)}, f32[256,768]{1,0:T(8,128)S(1)}, u32[]{:S(2)}, u32[]{:S(2)}) collective-permute-start(f32[256,768]{1,0:T(8,128)} %get-tuple-element.75), channel_id=1, source_target_pairs={{0,1},{1,0},{2,3},{3,2},{4,5},{5,4},{6,7},{7,6},{8,9},{9,8},{10,11... | collective-permute-start | bytes 2359304 | tf_op jit(solution)/shard_map/b_across/ppermute | solution.py:55
  146.5 15.5 %collective-permute-start.20 = (f32[256,640]{1,0:T(8,128)}, f32[256,640]{1,0:T(8,128)S(1)}, u32[]{:S(2)}, u32[]{:S(2)}) collective-permute-start(f32[256,640]{1,0:T(8,128)} %get-tuple-element.76), channel_id=1, source_target_pairs={{0,2},{1,3},{2,4},{3,5},{4,6},{5,7},{6,0},{7,1},{8,10},{9,11},{10,... | collective-permute-start | bytes 1966088 | tf_op jit(solution)/shard_map/outer2_up/ppermute | solution.py:55
  146.5 11.0 %collective-permute-start.21 = (f32[256,512]{1,0:T(8,128)}, f32[256,512]{1,0:T(8,128)S(1)}, u32[]{:S(2)}, u32[]{:S(2)}) collective-permute-start(f32[256,512]{1,0:T(8,128)} %get-tuple-element.77), channel_id=1, source_target_pairs={{0,6},{1,7},{2,0},{3,1},{4,2},{5,3},{6,4},{7,5},{8,14},{9,15},{10,... | collective-permute-start | bytes 1572872 | tf_op jit(solution)/shard_map/outer2_down/ppermute | solution.py:55
  157.6 4.4 %copy-start.10 = (f32[256,512]{1,0:T(8,128)}, f32[256,512]{1,0:T(8,128)S(1)}, u32[]{:S(2)}) copy-start(f32[256,512]{1,0:T(8,128)S(1)} %collective-permute-done.21.refs_13_) | copy-start | bytes 1572868
  172.8 4.2 %collective-permute-start.22 = (f32[176,128]{1,0:T(8,128)S(1)}, f32[176,128]{1,0:T(8,128)S(1)}, u32[]{:S(2)}, u32[]{:S(2)}) collective-permute-start(f32[176,128]{1,0:T(8,128)S(1)} %constant_dynamic-slice_fusion), channel_id=1, source_target_pairs={{0,8},{8,0},{16,24},{24,16},{32,40},{40,32},{48,56},{56,48},{64,72... | collective-permute-start | bytes 270344 | tf_op jit(solution)/shard_map/sum_core/ppermute | solution.py:55
  178.0 5.4 %collective-permute-start.25 = (f32[176,128]{1,0:T(8,128)S(1)}, f32[176,128]{1,0:T(8,128)S(1)}, u32[]{:S(2)}, u32[]{:S(2)}) collective-permute-start(f32[176,128]{1,0:T(8,128)S(1)} %dynamic-slice_add_fusion), channel_id=1, source_target_pairs={{0,48},{8,56},{16,0},{24,8},{32,16},{40,24},{48,32},{56,40},{64,11... | collective-permute-start | bytes 270344 | tf_op jit(solution)/shard_map/sum_z3/ppermute | solution.py:55
  181.8 7.1 %collective-permute-start.24 = (f32[176,128]{1,0:T(8,128)S(1)}, f32[176,128]{1,0:T(8,128)S(1)}, u32[]{:S(2)}, u32[]{:S(2)}) collective-permute-start(f32[176,128]{1,0:T(8,128)S(1)} %dynamic-slice_add_fusion), channel_id=1, source_target_pairs={{0,16},{8,24},{16,32},{24,40},{32,48},{40,56},{48,0},{56,8},{64,80... | collective-permute-start | bytes 270344 | tf_op jit(solution)/shard_map/sum_z1/ppermute | solution.py:55
  181.8 7.1 %collective-permute-start.23 = (f32[176,128]{1,0:T(8,128)S(1)}, f32[176,128]{1,0:T(8,128)S(1)}, u32[]{:S(2)}, u32[]{:S(2)}) collective-permute-start(f32[176,128]{1,0:T(8,128)S(1)} %dynamic-slice_add_fusion), channel_id=1, source_target_pairs={{0,32},{8,40},{16,48},{24,56},{32,0},{40,8},{48,16},{56,24},{64,96... | collective-permute-start | bytes 270344 | tf_op jit(solution)/shard_map/sum_z2/ppermute | solution.py:55
  188.9 3.5 %collective-permute-start.26 = (f32[176,128]{1,0:T(8,128)S(1)}, f32[176,128]{1,0:T(8,128)S(1)}, u32[]{:S(2)}, u32[]{:S(2)}) collective-permute-start(f32[176,128]{1,0:T(8,128)S(1)} %add_add_fusion), channel_id=1, source_target_pairs={{0,64},{8,72},{16,80},{24,88},{32,96},{40,104},{48,112},{56,120},{... | collective-permute-start | bytes 270344 | tf_op jit(solution)/shard_map/sum_y/ppermute | solution.py:55
  192.4 3.3 %copy-start.13 = (f32[176,128]{1,0:T(8,128)}, f32[176,128]{1,0:T(8,128)S(1)}, u32[]{:S(2)}) copy-start(f32[176,128]{1,0:T(8,128)S(1)} %add.37.mine) | copy-start | bytes 270340
  192.4 3.2 %collective-permute-start.27 = (f32[176,128]{1,0:T(8,128)S(1)}, f32[176,128]{1,0:T(8,128)S(1)}, u32[]{:S(2)}, u32[]{:S(2)}) collective-permute-start(f32[176,128]{1,0:T(8,128)S(1)} %add.37.mine), channel_id=1, source_target_pairs={{0,8},{8,0},{16,24},{24,16},{32,40},{40,32},{48,56},{56,48},{64,72... | collective-permute-start | bytes 270344 | tf_op jit(solution)/shard_map/gather_core/ppermute | solution.py:55
  (12 other events, 12.6 us)
